TPU v7x, 32 devices: a whole 2x2x4 slice. The times are simulated.
32 devices in a mesh: row: 8 (over y, x, core), col: 4 (over z).
Axes of the slice: x: 2, y: 2, z: 4, core: 2. Of those that a mesh axis runs over, the one named last changes fastest.
Arguments:
- left_panels: float32 [3, 64, 65536], P(None, 'col', 'row'), may hold values from -0.0234375 to 0.0234375
- right_panels: float32 [3, 65536, 512], P(None, 'row', 'col'), may hold values from -6 to 6
- window_tiles: float32 [3, 64, 512], P(None, 'row', 'col'), may hold values from -6 to 6
Outputs:
- updated: float32 [3, 64, 512], P(None, 'row', 'col')
All inputs are finite; a program needn't handle non-finite values.
Results may differ from a plain program's by a relative error of at most 0.00005.
Values sent between devices are 32-bit elements; how exact they have to be, the bound alone decides.
No kernel may reach another device: no remote copies, remote signals or barrier semaphores. Data moves between devices by JAX's collectives and lax.ppermute only.
A program may use at most 64 MiB of HBM per device.

v0:
```python
import jax
import jax.numpy as jnp
from jax import lax
from jax.sharding import PartitionSpec as P


def product(left_part, right_part):
    return jnp.dot(
        left_part, right_part, precision=lax.Precision.HIGHEST, preferred_element_type=jnp.float32
    )


def series_terms(left_parts, right_parts):
    square = product(left_parts[0], right_parts[0])
    first = product(left_parts[0], right_parts[1]) + product(left_parts[1], right_parts[0])
    second = (
        product(left_parts[0], right_parts[2])
        + product(left_parts[1], right_parts[1])
        + product(left_parts[2], right_parts[0])
    )
    return (square, first, second)


def on_device(left_panels, right_panels, window_tiles):
    width = right_panels.shape[2]
    partial_sums = jnp.concatenate(
        series_terms(lax.all_gather(left_panels, "col", axis=1, tiled=True), right_panels), axis=1
    )
    reduced = lax.psum_scatter(partial_sums, "row", scatter_dimension=0, tiled=True)
    height = reduced.shape[0]
    stacked = jnp.transpose(reduced.reshape(height, 3, width), (1, 0, 2))
    return 2.0 * window_tiles - stacked


def solution(mesh):
    return jax.shard_map(
        on_device,
        mesh=mesh,
        in_specs=(P(None, "col", "row"), P(None, "row", "col"), P(None, "row", "col")),
        out_specs=P(None, "row", "col"),
        check_vma=False,
    )
```

profile of v0, /device:TPU:0, one launch (start us, length us, event | category | flops | bytes accessed | tf_op | source)
XLA Modules:
  0.0 209.5 jit_solution(10879683671203739983)
XLA Ops:
  6.5 0.0 all-gather.2.cloned.1.call-start
  6.5 0.7 all-gather.2.cloned.1.call-update
  7.3 0.0 all-reduce.3.cloned.1.call-start
  7.3 119.7 %all-gather.2.cloned.1.call-done = f32[3,64,8192]{2,1,0:T(8,128)} async-done(((f32[3,16,8192]{2,1,0:T(8,128)}), f32[3,64,8192]{2,1,0:T(8,128)}) %all-gather.2.cloned.1.call-update) | async-done | bytes 6291472 | tf_op jit(solution)/shard_map/all_gather | solution.py:27
  127.0 0.0 copy-start
  127.0 5.6 %fusion = f32[64,128]{1,0:T(8,128)S(1)} fusion(f32[3,8192,128]{2,1,0:T(8,128)} %param.4, f32[3,64,8192]{2,1,0:T(8,128)} %all-gather.2.cloned.1.call-done), kind=kOutput, calls=%fused_computation | convolution fusion | flops 805306368 | bytes 6324224 | tf_op jit(solution)/shard_map/dot_general | solution.py:8
  132.6 0.0 copy-start.1
  132.7 5.6 %fusion.4 = f32[64,128]{1,0:T(8,128)S(1)} fusion(f32[3,8192,128]{2,1,0:T(8,128)} %param.4, f32[3,64,8192]{2,1,0:T(8,128)} %all-gather.2.cloned.1.call-done), kind=kOutput, calls=%fused_computation.4 | convolution fusion | flops 805306368 | bytes 6324224 | tf_op jit(solution)/shard_map/dot_general | solution.py:8
  138.3 0.0 copy-done
  138.3 4.3 %fusion.10 = f32[64,128]{1,0:T(8,128)S(1)} fusion(f32[3,8192,128]{2,1,0:T(8,128)S(1)} %copy-done, f32[3,64,8192]{2,1,0:T(8,128)} %all-gather.2.cloned.1.call-done), kind=kOutput, calls=%fused_computation.10 | convolution fusion | flops 805306368 | bytes 6324224 | tf_op jit(solution)/shard_map/dot_general | solution.py:8
  142.6 0.0 copy-done.1
  142.6 2.7 %fusion.24 = f32[64,128]{1,0:T(8,128)S(1)} fusion(f32[64,128]{1,0:T(8,128)S(1)} %fusion, f32[3,8192,128]{2,1,0:T(8,128)S(1)} %copy-done, f32[3,64,8192]{2,1,0:T(8,128)S(1)} %copy-done.1), kind=kOutput, calls=%fused_computation.23 | convolution fusion | flops 805314560 | bytes 6356992 | tf_op jit(solution)/shard_map/dot_general | solution.py:8
  145.3 0.0 copy-start.3
  145.3 0.0 copy-start.2
  145.3 2.8 %fusion.21 = f32[64,128]{1,0:T(8,128)S(1)} fusion(f32[64,128]{1,0:T(8,128)S(1)} %fusion.24, f32[3,8192,128]{2,1,0:T(8,128)S(1)} %copy-done, f32[3,64,8192]{2,1,0:T(8,128)S(1)} %copy-done.1), kind=kOutput, calls=%fused_computation.22 | convolution fusion | flops 805314560 | bytes 6356992 | tf_op jit(solution)/shard_map/dot_general | solution.py:8
  148.1 2.7 %fusion.18 = f32[64,128]{1,0:T(8,128)S(1)} fusion(f32[64,128]{1,0:T(8,128)S(1)} %fusion.4, f32[3,8192,128]{2,1,0:T(8,128)S(1)} %copy-done, f32[3,64,8192]{2,1,0:T(8,128)S(1)} %copy-done.1), kind=kOutput, calls=%fused_computation.21 | convolution fusion | flops 805314560 | bytes 6356992 | tf_op jit(solution)/shard_map/dot_general | solution.py:8
  150.8 0.6 pad_maximum_fusion
  151.4 0.0 all-reduce.3.cloned.1.call-update
  151.5 0.0 copy-done.3
  151.5 0.6 dynamic-slice
  152.7 48.6 %all-reduce.3.cloned.1.call-done = f32[64,384]{1,0:T(8,128)} async-done(((f32[64,384]{1,0:T(8,128)}), f32[64,384]{1,0:T(8,128)}) %all-reduce.3.cloned.1.call-update) | async-done | bytes 98320
  201.3 0.0 copy-done.2
  201.3 1.3 bitcast_subtract_fusion
Async XLA Ops:
  6.5 120.5 %all-gather.2.cloned.1.call-start = ((), (), s32[]{:S(2)}) async-start(), calls=%async_computation | async-start | bytes 7864320 | tf_op jit(solution)/shard_map/all_gather | solution.py:27
  7.3 194.1 %all-reduce.3.cloned.1.call-start = ((), (), s32[]{:S(2)}) async-start(), calls=%async_computation.1 | async-start | bytes 196608
  127.0 11.3 %copy-start = (f32[3,8192,128]{2,1,0:T(8,128)S(1)}, f32[3,8192,128]{2,1,0:T(8,128)}, u32[]{:S(2)}) copy-start(f32[3,8192,128]{2,1,0:T(8,128)} %param.4) | copy-start | bytes 37748740
  132.6 10.0 %copy-start.1 = (f32[3,64,8192]{2,1,0:T(8,128)S(1)}, f32[3,64,8192]{2,1,0:T(8,128)}, u32[]{:S(2)}) copy-start(f32[3,64,8192]{2,1,0:T(8,128)} %all-gather.2.cloned.1.call-done) | copy-start | bytes 18874372
  145.3 6.2 %copy-start.3 = (u32[32]{0:T(128)S(1)}, u32[32]{0:T(128)}, u32[]{:S(2)}) copy-start(u32[32]{0:T(128)} %constant.4) | copy-start | bytes 388
  145.3 56.0 %copy-start.2 = (f32[3,8,128]{2,1,0:T(8,128)S(1)}, f32[3,8,128]{2,1,0:T(8,128)}, u32[]{:S(2)}) copy-start(f32[3,8,128]{2,1,0:T(8,128)} %param.5) | copy-start | bytes 36868
Sparse Core Ops, SparseCore 0:
  8.9 118.0 all-gather.1
  151.6 49.6 all-reduce.2
where the time goes:
time: 210 us; the launch traced here: 209 us
  waiting for transfers between devices  169 us (80%)
  matrix products  23.7 us (11%)
  between operations  14.1 us (7%)
    all_gather x1, waiting for transfers between devices, on_device(): lax.all_gather(left_panels, 'col', axis=1, tiled=True)  120 us
    unnamed x3, waiting for transfers between devices  49.3 us
    dot_general x6, matrix products, product(): jnp.dot(left_part, right_part, precision=lax.Precision.HIGHEST, preferred...  23.7 us
  transfers between devices with their start and end apart: 2, of which 2 were waited for; matrix products, arithmetic and copies ran while one was open for 0% of the time, Pallas kernels for 0%

commit v1 on v0

v1 whole, which is shorter than its diff:
```python
import functools

import jax
import jax.numpy as jnp
from jax import lax
from jax.experimental import pallas as pl
from jax.experimental.pallas import tpu as pltpu
from jax.sharding import PartitionSpec as P

ORDERS = 3
VMEM_LIMIT = 48 * 1024 * 1024


def halves(values):
    high = values.astype(jnp.bfloat16)
    return high, (values - high.astype(jnp.float32)).astype(jnp.bfloat16)


def products_kernel(layout, steps, *refs):
    count = sum(sum(sources) for sources in layout)
    left_refs, right_ref, out_ref = refs[:count], refs[count], refs[count + 1]
    totals = refs[count + 2 :]
    sources_of = [len(sources) for sources in layout]
    step = pl.program_id(0)

    rows, place = [], 0
    for sources in layout:
        for arrays in sources:
            piece = left_refs[place][...]
            for extra in range(1, arrays):
                piece = piece + left_refs[place + extra][...]
            place += arrays
            rows.extend(halves(piece))
    height = rows[0].shape[0]
    stacked = jnp.concatenate(rows, axis=0)
    for order, parts in enumerate(totals):
        high, low = halves(right_ref[order])
        used = 2 * height * sum(sources_of[: ORDERS - order])
        parts[step] = jnp.dot(
            stacked[:used], jnp.concatenate([high, low], axis=1), preferred_element_type=jnp.float32
        )

    @pl.when(step == steps - 1)
    def _():
        width = right_ref.shape[2]
        sums = [jnp.sum(parts[...], axis=0) for parts in totals]
        for source in range(max(sources_of)):
            for out_order in range(ORDERS):
                value = jnp.zeros((height, width), jnp.float32)
                first_row = 0
                for left_order in range(ORDERS):
                    right_order = out_order - left_order
                    if 0 <= right_order < len(totals) and source < sources_of[left_order]:
                        top = (first_row + source) * 2 * height
                        block = sums[right_order][top : top + 2 * height]
                        block = block[:height] + block[height:]
                        value = value + (block[:, :width] + block[:, width:])
                    first_row += sources_of[left_order]
                out_ref[source, out_order] = value


def products(lefts, right, start=0, extent=None, tile=1024):
    height = next(arrays[0].shape[0] for sources in lefts for arrays in sources)
    extent = next(arrays[0].shape[1] for sources in lefts for arrays in sources) if extent is None else extent
    width = right.shape[2]
    tile = min(tile, extent)
    steps = extent // tile
    layout = [[len(arrays) for arrays in sources] for sources in lefts]
    flat = [array for sources in lefts for arrays in sources for array in arrays]
    sources_of = [len(sources) for sources in lefts]
    lowest = min(a for a in range(ORDERS) if sources_of[a])
    right_orders = min(ORDERS - lowest, right.shape[0])
    first_block = start // tile
    multiplies = sum(
        2 * height * sum(sources_of[: ORDERS - order]) * extent * 2 * width for order in range(right_orders)
    )
    return pl.pallas_call(
        functools.partial(products_kernel, layout, steps),
        grid=(steps,),
        in_specs=[pl.BlockSpec((height, tile), lambda k: (0, k))] * len(flat)
        + [pl.BlockSpec((right_orders, tile, width), lambda k: (0, k + first_block, 0))],
        out_specs=pl.BlockSpec((max(sources_of), ORDERS, height, width), lambda k: (0, 0, 0, 0)),
        out_shape=jax.ShapeDtypeStruct((max(sources_of), ORDERS, height, width), jnp.float32),
        scratch_shapes=[
            pltpu.VMEM((steps, 2 * height * sum(sources_of[: ORDERS - order]), 2 * width), jnp.float32)
            for order in range(right_orders)
        ],
        compiler_params=pltpu.CompilerParams(vmem_limit_bytes=VMEM_LIMIT),
        cost_estimate=pl.CostEstimate(
            flops=2 * multiplies,
            bytes_accessed=4 * (len(flat) * height * extent + right_orders * extent * width),
            transcendentals=0,
        ),
    )(*flat, right)


def sum_over_row(blocks, row_size):
    if row_size != 8:
        return lax.psum_scatter(blocks, "row", scatter_dimension=0, tiled=True)[0]
    me = lax.axis_index("row")
    pairs = blocks.reshape((4, 2) + blocks.shape[1:])
    core, chip = me % 2, me // 2
    keep = lax.dynamic_index_in_dim(pairs, core, 1, False)
    give = lax.dynamic_index_in_dim(pairs, 1 - core, 1, False)
    mine = keep + lax.ppermute(give, "row", [(i, i ^ 1) for i in range(8)])
    total = lax.dynamic_index_in_dim(mine, chip, 0, False)
    for offset in (1, 2, 3):
        block = lax.dynamic_index_in_dim(mine, chip ^ offset, 0, False)
        total = total + lax.ppermute(block, "row", [(i, i ^ (2 * offset)) for i in range(8)])
    return total


def line_of_four(left, right):
    place = lax.axis_index("col")
    swap = [(0, 1), (1, 0), (2, 3), (3, 2)]
    middle = [(1, 2), (2, 1)]
    outward = [(1, 0), (2, 3)]
    send = lambda array, pairs: lax.ppermute(array, "col", pairs)
    own = [left[order] for order in range(ORDERS)]
    near = [send(piece, swap) for piece in own]
    across = [send(piece, middle) for piece in own]
    across_out = [send(piece, outward) for piece in across]
    far = [send(piece, middle) for piece in near]
    far_out = [send(piece, outward) for piece in far]
    first = products([[(own[a],), (near[a],)] for a in range(ORDERS)], right)
    second = products([[(across[a], across_out[a])] for a in range(ORDERS)], right)
    third = products([[(far[a], far_out[a])] for a in range(ORDERS)], right)
    shards = jnp.stack([first[0], first[1], second[0], third[0]])
    slots = lambda *shards_at: functools.reduce(lambda rest, at: jnp.where(place == at[0], at[1], rest), enumerate(shards_at), 0)
    where_is = (slots(0, 1, 3, 3), slots(1, 0, 2, 2), slots(2, 2, 0, 1), slots(3, 3, 1, 0))
    return jnp.stack([lax.dynamic_index_in_dim(shards, slot, 0, False) for slot in where_is])


def on_device(cols, rows, left_panels, right_panels, window_tiles):
    height, width = window_tiles.shape[1:]
    if cols == 4:
        shards = line_of_four(left_panels, right_panels)
    else:
        gathered = lax.all_gather(left_panels, "col", axis=1, tiled=True)
        shards = products([[(gathered[a],)] for a in range(ORDERS)], right_panels)
    blocks = shards.reshape(-1, ORDERS, shards.shape[2] // height, height, width)
    blocks = jnp.swapaxes(blocks, 1, 2).reshape(rows, ORDERS, height, width)
    return 2.0 * window_tiles - sum_over_row(blocks, rows)


def solution(mesh):
    return jax.shard_map(
        functools.partial(on_device, mesh.shape["col"], mesh.shape["row"]),
        mesh=mesh,
        in_specs=(P(None, "col", "row"), P(None, "row", "col"), P(None, "row", "col")),
        out_specs=P(None, "row", "col"),
        check_vma=False,
    )
```

time: 210 us -> 135 us (0.64)
  waiting for transfers between devices: 169 us -> 78.5 us
  Pallas kernels: 0 us -> 25.9 us
  starting transfers between devices: 0.04 us -> 24.5 us
  matrix products: 23.7 us -> 0 us
  between operations: 14.1 us -> 0.3 us
  local copies, waits for them, and re-layouts: 0.61 us -> 4.16 us
    all_gather x1 -> x0, waiting for transfers between devices: 120 us -> none  [on_device(): lax.all_gather(left_panels, 'col', axis=1, tiled=True)]
    ppermute x0 -> x19, waiting for transfers between devices: none -> 78.5 us  [the longest x15 73.2 us: line_of_four(): send = lambda array, pairs: lax.ppermute(array, 'col', pairs)]
    unnamed x3 -> x0, waiting for transfers between devices: 49.3 us -> none
    pallas_call x0 -> x3, Pallas kernels: none -> 25.9 us  [products(): pl.pallas_call(functools.partial(products_kernel, layout, steps), grid=(s...]
    ppermute x0 -> x19, starting transfers between devices: none -> 24.5 us  [the longest x15 20.9 us: line_of_four(): send = lambda array, pairs: lax.ppermute(array, 'col', pairs)]
    dot_general x6 -> x0, matrix products: 23.7 us -> none  [product(): jnp.dot(left_part, right_part, precision=lax.Precision.HIGHEST, preferred...]
  transfers between devices with their start and end apart: 2 -> 19, of which waited for: 2 -> 12; matrix products, arithmetic and copies ran while one was open for 0% -> 0% of each run, Pallas kernels for 0% -> 13%
where the time goes in v1:
time: 135 us; the launch traced here: 134 us
  waiting for transfers between devices  78.5 us (58%)
  Pallas kernels  25.9 us (19%)
  starting transfers between devices  24.5 us (18%)
  local copies, waits for them, and re-layouts  4.16 us (3%)
    ppermute x15, waiting for transfers between devices, line_of_four(): send = lambda array, pairs: lax.ppermute(array, 'col', pairs)  73.2 us
    pallas_call x3, Pallas kernels, products(): pl.pallas_call(functools.partial(products_kernel, layout, steps), grid=(s...  25.9 us
    ppermute x15, starting transfers between devices, line_of_four(): send = lambda array, pairs: lax.ppermute(array, 'col', pairs)  20.9 us
    ppermute x3, waiting for transfers between devices, sum_over_row(): lax.ppermute(block, 'row', [(i, i ^ 2 * offset) for i in range(8)])  4.11 us
    ppermute x3, starting transfers between devices, sum_over_row(): lax.ppermute(block, 'row', [(i, i ^ 2 * offset) for i in range(8)])  3.55 us
  transfers between devices with their start and end apart: 19, of which 12 were waited for; matrix products, arithmetic and copies ran while one was open for 0% of the time, Pallas kernels for 13%

profile of v1, /device:TPU:0, one launch (start us, length us, event | category | flops | bytes accessed | tf_op | source)
XLA Modules:
  0.0 134.0 jit_solution(10210732623470827168)
XLA Ops:
  0.0 1.5 %slice_bitcast_fusion = (f32[16,8192]{1,0:T(8,128)S(1)}, f32[16,8192]{1,0:T(8,128)S(1)}, f32[16,8192]{1,0:T(8,128)S(1)}) fusion(f32[3,16,8192]{2,1,0:T(8,128)} %param.3), kind=kLoop, calls=%fused_computation | loop fusion | bytes 3145728 | tf_op jit(solution)/shard_map/squeeze | solution.py:119
  1.5 3.1 %collective-permute-start = (f32[16,8192]{1,0:T(8,128)S(1)}, f32[16,8192]{1,0:T(8,128)S(1)}, u32[]{:S(2)}, u32[]{:S(2)}) collective-permute-start(f32[16,8192]{1,0:T(8,128)S(1)} %get-tuple-element.6.refs_0_), channel_id=1, source_target_pairs={{0,1},{1,0},{2,3},{3,2},{4,5},{5,4},{6,7},{7,6},{8,9},{9,8},{10,11... | collective-permute-start | bytes 1572872 | tf_op jit(solution)/shard_map/ppermute | solution.py:118
  4.6 0.1 collective-permute-start.1
  4.6 1.9 %collective-permute-start.2 = (f32[16,8192]{1,0:T(8,128)S(1)}, f32[16,8192]{1,0:T(8,128)S(1)}, u32[]{:S(2)}, u32[]{:S(2)}) collective-permute-start(f32[16,8192]{1,0:T(8,128)S(1)} %get-tuple-element.5.refs_4_), channel_id=1, source_target_pairs={{0,1},{1,0},{2,3},{3,2},{4,5},{5,4},{6,7},{7,6},{8,9},{9,8},{10,11... | collective-permute-start | bytes 1572872 | tf_op jit(solution)/shard_map/ppermute | solution.py:118
  6.6 0.7 collective-permute-start.3
  7.3 1.5 %collective-permute-start.5 = (f32[16,8192]{1,0:T(8,128)S(1)}, f32[16,8192]{1,0:T(8,128)}, u32[]{:S(2)}, u32[]{:S(2)}) collective-permute-start(f32[16,8192]{1,0:T(8,128)S(1)} %get-tuple-element.7.refs_2_), channel_id=1, source_target_pairs={{1,2},{2,1},{5,6},{6,5},{9,10},{10,9},{13,14},{14,13},{17,18},{18,... | collective-permute-start | bytes 1572872 | tf_op jit(solution)/shard_map/ppermute | solution.py:118
  8.7 8.6 %collective-permute-done.refs_1_ = f32[16,8192]{1,0:T(8,128)S(1)} collective-permute-done((f32[16,8192]{1,0:T(8,128)S(1)}, f32[16,8192]{1,0:T(8,128)S(1)}, u32[]{:S(2)}, u32[]{:S(2)}) %collective-permute-start) | collective-permute-done | bytes 524320 | tf_op jit(solution)/shard_map/ppermute | solution.py:118
  17.3 1.5 %collective-permute-start.7 = (f32[16,8192]{1,0:T(8,128)S(1)}, f32[16,8192]{1,0:T(8,128)}, u32[]{:S(2)}, u32[]{:S(2)}) collective-permute-start(f32[16,8192]{1,0:T(8,128)S(1)} %get-tuple-element.5.refs_4_), channel_id=1, source_target_pairs={{1,2},{2,1},{5,6},{6,5},{9,10},{10,9},{13,14},{14,13},{17,18},{18,... | collective-permute-start | bytes 1572872 | tf_op jit(solution)/shard_map/ppermute | solution.py:118
  18.8 9.8 %collective-permute-done.1.refs_3_ = f32[16,8192]{1,0:T(8,128)S(1)} collective-permute-done((f32[16,8192]{1,0:T(8,128)S(1)}, f32[16,8192]{1,0:T(8,128)S(1)}, u32[]{:S(2)}, u32[]{:S(2)}) %collective-permute-start.1) | collective-permute-done | bytes 524320 | tf_op jit(solution)/shard_map/ppermute | solution.py:118
  28.5 1.5 %collective-permute-start.9 = (f32[16,8192]{1,0:T(8,128)S(1)}, f32[16,8192]{1,0:T(8,128)}, u32[]{:S(2)}, u32[]{:S(2)}) collective-permute-start(f32[16,8192]{1,0:T(8,128)S(1)} %collective-permute-done.refs_1_), channel_id=1, source_target_pairs={{1,2},{2,1},{5,6},{6,5},{9,10},{10,9},{13,14},{14,13},{17,18},{18,... | collective-permute-start | bytes 1572872 | tf_op jit(solution)/shard_map/ppermute | solution.py:118
  30.0 8.9 %collective-permute-done.2.refs_5_ = f32[16,8192]{1,0:T(8,128)S(1)} collective-permute-done((f32[16,8192]{1,0:T(8,128)S(1)}, f32[16,8192]{1,0:T(8,128)S(1)}, u32[]{:S(2)}, u32[]{:S(2)}) %collective-permute-start.2) | collective-permute-done | bytes 524320 | tf_op jit(solution)/shard_map/ppermute | solution.py:118
  38.9 1.5 %collective-permute-start.11 = (f32[16,8192]{1,0:T(8,128)S(1)}, f32[16,8192]{1,0:T(8,128)}, u32[]{:S(2)}, u32[]{:S(2)}) collective-permute-start(f32[16,8192]{1,0:T(8,128)S(1)} %collective-permute-done.1.refs_3_), channel_id=1, source_target_pairs={{1,2},{2,1},{5,6},{6,5},{9,10},{10,9},{13,14},{14,13},{17,18},{18,... | collective-permute-start | bytes 1572872 | tf_op jit(solution)/shard_map/ppermute | solution.py:118
  40.4 0.0 collective-permute-done.3.refs_0_
  40.4 1.5 %collective-permute-start.13 = (f32[16,8192]{1,0:T(8,128)S(1)}, f32[16,8192]{1,0:T(8,128)}, u32[]{:S(2)}, u32[]{:S(2)}) collective-permute-start(f32[16,8192]{1,0:T(8,128)S(1)} %collective-permute-done.2.refs_5_), channel_id=1, source_target_pairs={{1,2},{2,1},{5,6},{6,5},{9,10},{10,9},{13,14},{14,13},{17,18},{18,... | collective-permute-start | bytes 1572872 | tf_op jit(solution)/shard_map/ppermute | solution.py:118
  41.9 0.8 copy-done
  42.7 0.0 collective-permute-done.5.refs_2_
  42.7 1.3 collective-permute-start.4
  44.0 0.0 collective-permute-done.7.refs_4_
  44.0 1.3 collective-permute-start.6
  45.3 0.0 collective-permute-done.9.refs_0_
  45.3 1.3 collective-permute-start.8
  46.6 0.0 collective-permute-done.11.refs_2_
  46.6 1.3 collective-permute-start.10
  47.9 0.0 collective-permute-done.13.refs_4_
  47.9 1.3 collective-permute-start.12
  49.2 12.2 %collective-permute-done.4.refs_1_ = f32[16,8192]{1,0:T(8,128)S(1)} collective-permute-done((f32[16,8192]{1,0:T(8,128)S(1)}, f32[16,8192]{1,0:T(8,128)S(1)}, u32[]{:S(2)}, u32[]{:S(2)}) %collective-permute-start.4) | collective-permute-done | bytes 524320 | tf_op jit(solution)/shard_map/ppermute | solution.py:118
  61.5 0.8 copy-done.2
  62.3 1.3 collective-permute-start.14
  63.6 1.0 copy-done.1
  64.7 8.5 %shard_map.37 = f32[2,3,16,128]{3,2,1,0:T(8,128)S(1)} custom-call(f32[16,8192]{1,0:T(8,128)S(1)} %get-tuple-element.6.refs_0_, f32[16,8192]{1,0:T(8,128)S(1)} %collective-permute-done.refs_1_, f32[16,8192]{1,0:T(8,128)S(1)} %get-tuple-element.7.refs_2_, f32[16,8192]{1,0:T(8,128)S(1)} %collective-permute-done.1.refs_3_, ...), custom_call_target="tpu_custom_call" | custom-call | flops 1610612736 | bytes 15728640 | tf_op jit(solution)/shard_map/pallas_call | solution.py:77
  73.2 0.0 collective-permute-done.6.refs_3_
  73.2 10.9 %collective-permute-done.8.refs_5_ = f32[16,8192]{1,0:T(8,128)} collective-permute-done((f32[16,8192]{1,0:T(8,128)}, f32[16,8192]{1,0:T(8,128)}, u32[]{:S(2)}, u32[]{:S(2)}) %collective-permute-start.8) | collective-permute-done | bytes 524320 | tf_op jit(solution)/shard_map/ppermute | solution.py:118
  84.0 0.0 copy-done.3
  84.0 8.6 %shard_map.38 = f32[1,3,16,128]{3,2,1,0:T(8,128)S(1)} custom-call(f32[16,8192]{1,0:T(8,128)S(1)} %collective-permute-done.3.refs_0_, f32[16,8192]{1,0:T(8,128)S(1)} %copy-done.3, f32[16,8192]{1,0:T(8,128)} %collective-permute-done.5.refs_2_, f32[16,8192]{1,0:T(8,128)} %collective-permute-done.6.refs_3_, f32[16,8192]{1,0:T(8,128)} %collective-permute-done.7.refs_4_, ...), custom_call_target="tpu_custom_call" | custom-call | flops 805306368 | bytes 15728640 | tf_op jit(solution)/shard_map/pallas_call | solution.py:77
  92.7 0.0 copy-start.4
  92.7 2.6 %collective-permute-done.10.refs_1_ = f32[16,8192]{1,0:T(8,128)} collective-permute-done((f32[16,8192]{1,0:T(8,128)}, f32[16,8192]{1,0:T(8,128)}, u32[]{:S(2)}, u32[]{:S(2)}) %collective-permute-start.10) | collective-permute-done | bytes 524320 | tf_op jit(solution)/shard_map/ppermute | solution.py:118
  95.3 11.2 %collective-permute-done.12.refs_3_ = f32[16,8192]{1,0:T(8,128)} collective-permute-done((f32[16,8192]{1,0:T(8,128)}, f32[16,8192]{1,0:T(8,128)}, u32[]{:S(2)}, u32[]{:S(2)}) %collective-permute-start.12) | collective-permute-done | bytes 524320 | tf_op jit(solution)/shard_map/ppermute | solution.py:118
  106.5 9.0 %collective-permute-done.14.refs_5_ = f32[16,8192]{1,0:T(8,128)} collective-permute-done((f32[16,8192]{1,0:T(8,128)}, f32[16,8192]{1,0:T(8,128)}, u32[]{:S(2)}, u32[]{:S(2)}) %collective-permute-start.14) | collective-permute-done | bytes 524320 | tf_op jit(solution)/shard_map/ppermute | solution.py:118
  115.5 8.8 %shard_map.39 = f32[1,3,16,128]{3,2,1,0:T(8,128)S(1)} custom-call(f32[16,8192]{1,0:T(8,128)} %collective-permute-done.9.refs_0_, f32[16,8192]{1,0:T(8,128)} %collective-permute-done.10.refs_1_, f32[16,8192]{1,0:T(8,128)} %collective-permute-done.11.refs_2_, f32[16,8192]{1,0:T(8,128)} %collective-permute-done.12.refs_3_, ...), custom_call_target="tpu_custom_call" | custom-call | flops 805306368 | bytes 15728640 | tf_op jit(solution)/shard_map/pallas_call | solution.py:77
  124.4 0.1 collective-permute-start.15
  124.5 1.2 collective-permute-done.15
  125.7 1.6 %collective-permute-start.16 = (f32[3,8,128]{2,1,0:T(8,128)S(1)}, f32[3,8,128]{2,1,0:T(8,128)S(1)}, u32[]{:S(2)}, u32[]{:S(2)}) collective-permute-start(f32[3,8,128]{2,1,0:T(8,128)S(1)} %get-tuple-element.12), channel_id=1, source_target_pairs={{0,8},{4,12},{8,0},{12,4},{16,24},{20,28},{24,16},{28,20},{1,9},{5... | collective-permute-start | bytes 36872 | tf_op jit(solution)/shard_map/ppermute | solution.py:109
  127.3 1.5 %collective-permute-start.17 = (f32[3,8,128]{2,1,0:T(8,128)S(1)}, f32[3,8,128]{2,1,0:T(8,128)S(1)}, u32[]{:S(2)}, u32[]{:S(2)}) collective-permute-start(f32[3,8,128]{2,1,0:T(8,128)S(1)} %get-tuple-element.14), channel_id=1, source_target_pairs={{0,16},{4,20},{8,24},{12,28},{16,0},{20,4},{24,8},{28,12},{1,17},{... | collective-permute-start | bytes 36872 | tf_op jit(solution)/shard_map/ppermute | solution.py:109
  128.8 0.5 collective-permute-start.18
  129.3 0.2 collective-permute-done.16
  129.5 1.5 %collective-permute-done.17 = f32[3,8,128]{2,1,0:T(8,128)S(1)} collective-permute-done((f32[3,8,128]{2,1,0:T(8,128)S(1)}, f32[3,8,128]{2,1,0:T(8,128)S(1)}, u32[]{:S(2)}, u32[]{:S(2)}) %collective-permute-start.17) | collective-permute-done | bytes 12320 | tf_op jit(solution)/shard_map/ppermute | solution.py:109
  131.0 2.4 %collective-permute-done.18 = f32[3,8,128]{2,1,0:T(8,128)S(1)} collective-permute-done((f32[3,8,128]{2,1,0:T(8,128)S(1)}, f32[3,8,128]{2,1,0:T(8,128)S(1)}, u32[]{:S(2)}, u32[]{:S(2)}) %collective-permute-start.18) | collective-permute-done | bytes 12320 | tf_op jit(solution)/shard_map/ppermute | solution.py:109
  133.4 0.6 fusion.2
  (11 shorter events, 0.1 us)
Async XLA Ops:
  1.5 15.8 %collective-permute-start = (f32[16,8192]{1,0:T(8,128)S(1)}, f32[16,8192]{1,0:T(8,128)S(1)}, u32[]{:S(2)}, u32[]{:S(2)}) collective-permute-start(f32[16,8192]{1,0:T(8,128)S(1)} %get-tuple-element.6.refs_0_), channel_id=1, source_target_pairs={{0,1},{1,0},{2,3},{3,2},{4,5},{5,4},{6,7},{7,6},{8,9},{9,8},{10,11... | collective-permute-start | bytes 1572872 | tf_op jit(solution)/shard_map/ppermute | solution.py:118
  4.6 24.0 %collective-permute-start.1 = (f32[16,8192]{1,0:T(8,128)S(1)}, f32[16,8192]{1,0:T(8,128)S(1)}, u32[]{:S(2)}, u32[]{:S(2)}) collective-permute-start(f32[16,8192]{1,0:T(8,128)S(1)} %get-tuple-element.7.refs_2_), channel_id=1, source_target_pairs={{0,1},{1,0},{2,3},{3,2},{4,5},{5,4},{6,7},{7,6},{8,9},{9,8},{10,11... | collective-permute-start | bytes 1572872 | tf_op jit(solution)/shard_map/ppermute | solution.py:118
  4.6 34.3 %collective-permute-start.2 = (f32[16,8192]{1,0:T(8,128)S(1)}, f32[16,8192]{1,0:T(8,128)S(1)}, u32[]{:S(2)}, u32[]{:S(2)}) collective-permute-start(f32[16,8192]{1,0:T(8,128)S(1)} %get-tuple-element.5.refs_4_), channel_id=1, source_target_pairs={{0,1},{1,0},{2,3},{3,2},{4,5},{5,4},{6,7},{7,6},{8,9},{9,8},{10,11... | collective-permute-start | bytes 1572872 | tf_op jit(solution)/shard_map/ppermute | solution.py:118
  6.6 33.8 %collective-permute-start.3 = (f32[16,8192]{1,0:T(8,128)S(1)}, f32[16,8192]{1,0:T(8,128)S(1)}, u32[]{:S(2)}, u32[]{:S(2)}) collective-permute-start(f32[16,8192]{1,0:T(8,128)S(1)} %get-tuple-element.6.refs_0_), channel_id=1, source_target_pairs={{1,2},{2,1},{5,6},{6,5},{9,10},{10,9},{13,14},{14,13},{17,18},{18,... | collective-permute-start | bytes 1572872 | tf_op jit(solution)/shard_map/ppermute | solution.py:118
  7.3 35.4 %collective-permute-start.5 = (f32[16,8192]{1,0:T(8,128)S(1)}, f32[16,8192]{1,0:T(8,128)}, u32[]{:S(2)}, u32[]{:S(2)}) collective-permute-start(f32[16,8192]{1,0:T(8,128)S(1)} %get-tuple-element.7.refs_2_), channel_id=1, source_target_pairs={{1,2},{2,1},{5,6},{6,5},{9,10},{10,9},{13,14},{14,13},{17,18},{18,... | collective-permute-start | bytes 1572872 | tf_op jit(solution)/shard_map/ppermute | solution.py:118
  17.3 26.7 %collective-permute-start.7 = (f32[16,8192]{1,0:T(8,128)S(1)}, f32[16,8192]{1,0:T(8,128)}, u32[]{:S(2)}, u32[]{:S(2)}) collective-permute-start(f32[16,8192]{1,0:T(8,128)S(1)} %get-tuple-element.5.refs_4_), channel_id=1, source_target_pairs={{1,2},{2,1},{5,6},{6,5},{9,10},{10,9},{13,14},{14,13},{17,18},{18,... | collective-permute-start | bytes 1572872 | tf_op jit(solution)/shard_map/ppermute | solution.py:118
  28.5 16.8 %collective-permute-start.9 = (f32[16,8192]{1,0:T(8,128)S(1)}, f32[16,8192]{1,0:T(8,128)}, u32[]{:S(2)}, u32[]{:S(2)}) collective-permute-start(f32[16,8192]{1,0:T(8,128)S(1)} %collective-permute-done.refs_1_), channel_id=1, source_target_pairs={{1,2},{2,1},{5,6},{6,5},{9,10},{10,9},{13,14},{14,13},{17,18},{18,... | collective-permute-start | bytes 1572872 | tf_op jit(solution)/shard_map/ppermute | solution.py:118
  38.9 7.7 %collective-permute-start.11 = (f32[16,8192]{1,0:T(8,128)S(1)}, f32[16,8192]{1,0:T(8,128)}, u32[]{:S(2)}, u32[]{:S(2)}) collective-permute-start(f32[16,8192]{1,0:T(8,128)S(1)} %collective-permute-done.1.refs_3_), channel_id=1, source_target_pairs={{1,2},{2,1},{5,6},{6,5},{9,10},{10,9},{13,14},{14,13},{17,18},{18,... | collective-permute-start | bytes 1572872 | tf_op jit(solution)/shard_map/ppermute | solution.py:118
  40.4 7.5 %collective-permute-start.13 = (f32[16,8192]{1,0:T(8,128)S(1)}, f32[16,8192]{1,0:T(8,128)}, u32[]{:S(2)}, u32[]{:S(2)}) collective-permute-start(f32[16,8192]{1,0:T(8,128)S(1)} %collective-permute-done.2.refs_5_), channel_id=1, source_target_pairs={{1,2},{2,1},{5,6},{6,5},{9,10},{10,9},{13,14},{14,13},{17,18},{18,... | collective-permute-start | bytes 1572872 | tf_op jit(solution)/shard_map/ppermute | solution.py:118
  41.9 0.8 copy-start
  42.7 18.8 %collective-permute-start.4 = (f32[16,8192]{1,0:T(8,128)S(1)}, f32[16,8192]{1,0:T(8,128)S(1)}, u32[]{:S(2)}, u32[]{:S(2)}) collective-permute-start(f32[16,8192]{1,0:T(8,128)S(1)} %collective-permute-done.3.refs_0_), channel_id=1, source_target_pairs={{1,0},{2,3},{5,4},{6,7},{9,8},{10,11},{13,12},{14,15},{17,16},{18,... | collective-permute-start | bytes 1572872 | tf_op jit(solution)/shard_map/ppermute | solution.py:118
  44.0 29.2 %collective-permute-start.6 = (f32[16,8192]{1,0:T(8,128)}, f32[16,8192]{1,0:T(8,128)}, u32[]{:S(2)}, u32[]{:S(2)}) collective-permute-start(f32[16,8192]{1,0:T(8,128)} %collective-permute-done.5.refs_2_), channel_id=1, source_target_pairs={{1,0},{2,3},{5,4},{6,7},{9,8},{10,11},{13,12},{14,15},{17,16},{18,... | collective-permute-start | bytes 1572872 | tf_op jit(solution)/shard_map/ppermute | solution.py:118
  45.3 38.7 %collective-permute-start.8 = (f32[16,8192]{1,0:T(8,128)}, f32[16,8192]{1,0:T(8,128)}, u32[]{:S(2)}, u32[]{:S(2)}) collective-permute-start(f32[16,8192]{1,0:T(8,128)} %collective-permute-done.7.refs_4_), channel_id=1, source_target_pairs={{1,0},{2,3},{5,4},{6,7},{9,8},{10,11},{13,12},{14,15},{17,16},{18,... | collective-permute-start | bytes 1572872 | tf_op jit(solution)/shard_map/ppermute | solution.py:118
  46.6 48.7 %collective-permute-start.10 = (f32[16,8192]{1,0:T(8,128)}, f32[16,8192]{1,0:T(8,128)}, u32[]{:S(2)}, u32[]{:S(2)}) collective-permute-start(f32[16,8192]{1,0:T(8,128)} %collective-permute-done.9.refs_0_), channel_id=1, source_target_pairs={{1,0},{2,3},{5,4},{6,7},{9,8},{10,11},{13,12},{14,15},{17,16},{18,... | collective-permute-start | bytes 1572872 | tf_op jit(solution)/shard_map/ppermute | solution.py:118
  47.9 58.6 %collective-permute-start.12 = (f32[16,8192]{1,0:T(8,128)}, f32[16,8192]{1,0:T(8,128)}, u32[]{:S(2)}, u32[]{:S(2)}) collective-permute-start(f32[16,8192]{1,0:T(8,128)} %collective-permute-done.11.refs_2_), channel_id=1, source_target_pairs={{1,0},{2,3},{5,4},{6,7},{9,8},{10,11},{13,12},{14,15},{17,16},{18,... | collective-permute-start | bytes 1572872 | tf_op jit(solution)/shard_map/ppermute | solution.py:118
  61.5 0.8 copy-start.2
  62.3 53.2 %collective-permute-start.14 = (f32[16,8192]{1,0:T(8,128)}, f32[16,8192]{1,0:T(8,128)}, u32[]{:S(2)}, u32[]{:S(2)}) collective-permute-start(f32[16,8192]{1,0:T(8,128)} %collective-permute-done.13.refs_4_), channel_id=1, source_target_pairs={{1,0},{2,3},{5,4},{6,7},{9,8},{10,11},{13,12},{14,15},{17,16},{18,... | collective-permute-start | bytes 1572872 | tf_op jit(solution)/shard_map/ppermute | solution.py:118
  63.6 1.0 copy-start.1
  64.7 19.4 %copy-start.3 = (f32[16,8192]{1,0:T(8,128)S(1)}, f32[16,8192]{1,0:T(8,128)}, u32[]{:S(2)}) copy-start(f32[16,8192]{1,0:T(8,128)} %copy-done.2) | copy-start | bytes 1572868
  92.7 40.7 %copy-start.4 = (f32[3,8,128]{2,1,0:T(8,128)S(1)}, f32[3,8,128]{2,1,0:T(8,128)}, u32[]{:S(2)}) copy-start(f32[3,8,128]{2,1,0:T(8,128)} %param.5) | copy-start | bytes 36868
  124.4 1.3 collective-permute-start.15
  125.7 3.8 %collective-permute-start.16 = (f32[3,8,128]{2,1,0:T(8,128)S(1)}, f32[3,8,128]{2,1,0:T(8,128)S(1)}, u32[]{:S(2)}, u32[]{:S(2)}) collective-permute-start(f32[3,8,128]{2,1,0:T(8,128)S(1)} %get-tuple-element.12), channel_id=1, source_target_pairs={{0,8},{4,12},{8,0},{12,4},{16,24},{20,28},{24,16},{28,20},{1,9},{5... | collective-permute-start | bytes 36872 | tf_op jit(solution)/shard_map/ppermute | solution.py:109
  127.3 3.7 %collective-permute-start.17 = (f32[3,8,128]{2,1,0:T(8,128)S(1)}, f32[3,8,128]{2,1,0:T(8,128)S(1)}, u32[]{:S(2)}, u32[]{:S(2)}) collective-permute-start(f32[3,8,128]{2,1,0:T(8,128)S(1)} %get-tuple-element.14), channel_id=1, source_target_pairs={{0,16},{4,20},{8,24},{12,28},{16,0},{20,4},{24,8},{28,12},{1,17},{... | collective-permute-start | bytes 36872 | tf_op jit(solution)/shard_map/ppermute | solution.py:109
  128.8 4.6 %collective-permute-start.18 = (f32[3,8,128]{2,1,0:T(8,128)S(1)}, f32[3,8,128]{2,1,0:T(8,128)S(1)}, u32[]{:S(2)}, u32[]{:S(2)}) collective-permute-start(f32[3,8,128]{2,1,0:T(8,128)S(1)} %get-tuple-element.13), channel_id=1, source_target_pairs={{0,24},{4,28},{8,16},{12,20},{16,8},{20,12},{24,0},{28,4},{1,25},{... | collective-permute-start | bytes 36872 | tf_op jit(solution)/shard_map/ppermute | solution.py:109

commit v2 on v1

v2 whole, which is shorter than its diff:
```python
import functools

import jax
import jax.numpy as jnp
from jax import lax
from jax.experimental import pallas as pl
from jax.experimental.pallas import tpu as pltpu
from jax.sharding import PartitionSpec as P

ORDERS = 3
LANES, SUBLANES = 128, 8
TILE = 1024
VMEM_LIMIT = 12 * 1024 * 1024


def halves(values):
    high = values.astype(jnp.bfloat16)
    return high, (values - high.astype(jnp.float32)).astype(jnp.bfloat16)


def blocked(left):
    height, extent = left.shape
    return left.reshape(height // SUBLANES, SUBLANES, extent // LANES, LANES).transpose(0, 2, 1, 3)


def unblocked(blocks):
    return jnp.concatenate(
        [jnp.concatenate([blocks[a, c] for c in range(blocks.shape[1])], axis=1) for a in range(blocks.shape[0])], axis=0
    )


def products_kernel(layout, steps, side_ref, *refs):
    count = sum(len(terms) for sources in layout for terms in sources)
    left_refs, right_ref, out_ref = refs[:count], refs[count], refs[count + 1]
    totals = refs[count + 2 :]
    sources_of = [len(sources) for sources in layout]
    step = pl.program_id(0)

    rows, place = [], 0
    for sources in layout:
        for terms in sources:
            piece = None
            for first, tiles, side in terms:
                term = unblocked(left_refs[place][...])
                counts = None
                if tiles < steps:
                    counts = (step >= first) & (step < first + tiles)
                if side is not None:
                    here = side_ref[0] == side
                    counts = here if counts is None else counts & here
                if counts is not None:
                    term = jnp.where(counts, term, 0.0)
                piece = term if piece is None else piece + term
                place += 1
            rows.extend(halves(piece))
    height = rows[0].shape[0]
    stacked = jnp.concatenate(rows, axis=0)
    for order, parts in enumerate(totals):
        high, low = halves(right_ref[order])
        used = 2 * height * sum(sources_of[: ORDERS - order])
        parts[step] = jnp.dot(
            stacked[:used], jnp.concatenate([high, low], axis=1), preferred_element_type=jnp.float32
        )

    @pl.when(step == steps - 1)
    def _():
        width = right_ref.shape[2]
        sums = [jnp.sum(parts[...], axis=0) for parts in totals]
        for source in range(max(sources_of)):
            for out_order in range(ORDERS):
                value = jnp.zeros((height, width), jnp.float32)
                first_row = 0
                for left_order in range(ORDERS):
                    right_order = out_order - left_order
                    if 0 <= right_order < len(totals) and source < sources_of[left_order]:
                        top = (first_row + source) * 2 * height
                        block = sums[right_order][top : top + 2 * height]
                        block = block[:height] + block[height:]
                        value = value + (block[:, :width] + block[:, width:])
                    first_row += sources_of[left_order]
                out_ref[source, out_order] = value


def products(lefts, right, extent, side):
    flat = [term for sources in lefts for terms in sources for term in terms]
    high_blocks = flat[0][1].shape[0]
    height = high_blocks * SUBLANES
    width = right.shape[2]
    tile = min(TILE, extent)
    steps = extent // tile
    tiles_of = lambda array: array.shape[1] * LANES // tile
    layout = [
        [[(first // tile, tiles_of(array), on) for first, array, on in terms] for terms in sources] for sources in lefts
    ]
    sources_of = [len(sources) for sources in lefts]
    right_orders = min(ORDERS - min(a for a in range(ORDERS) if sources_of[a]), right.shape[0])
    rows_of = [2 * height * sum(sources_of[: ORDERS - order]) for order in range(right_orders)]

    def left_spec(first, array, on):
        first, last = first // tile, tiles_of(array) - 1
        return pl.BlockSpec(
            (high_blocks, tile // LANES, SUBLANES, LANES), lambda k: (0, jnp.clip(k - first, 0, last), 0, 0)
        )

    return pl.pallas_call(
        functools.partial(products_kernel, layout, steps),
        grid=(steps,),
        in_specs=[pl.BlockSpec(memory_space=pltpu.SMEM)]
        + [left_spec(*term) for term in flat]
        + [pl.BlockSpec((right_orders, tile, width), lambda k: (0, k, 0))],
        out_specs=pl.BlockSpec((max(sources_of), ORDERS, height, width), lambda k: (0, 0, 0, 0)),
        out_shape=jax.ShapeDtypeStruct((max(sources_of), ORDERS, height, width), jnp.float32),
        scratch_shapes=[pltpu.VMEM((steps, rows, 2 * width), jnp.float32) for rows in rows_of],
        compiler_params=pltpu.CompilerParams(vmem_limit_bytes=VMEM_LIMIT),
        cost_estimate=pl.CostEstimate(
            flops=4 * sum(rows_of) * extent * width,
            bytes_accessed=4 * (sum(term[1].size for term in flat) + right_orders * extent * width),
            transcendentals=0,
        ),
    )(side, *[term[1] for term in flat], right)


def sum_over_row(blocks, row_size):
    if row_size != 8:
        return lax.psum_scatter(blocks, "row", scatter_dimension=0, tiled=True)[0]
    me = lax.axis_index("row")
    pairs = blocks.reshape((4, 2) + blocks.shape[1:])
    core, chip = me % 2, me // 2
    keep = lax.dynamic_index_in_dim(pairs, core, 1, False)
    give = lax.dynamic_index_in_dim(pairs, 1 - core, 1, False)
    mine = keep + lax.ppermute(give, "row", [(i, i ^ 1) for i in range(8)])
    total = lax.dynamic_index_in_dim(mine, chip, 0, False)
    for offset in (1, 2, 3):
        block = lax.dynamic_index_in_dim(mine, chip ^ offset, 0, False)
        total = total + lax.ppermute(block, "row", [(i, i ^ (2 * offset)) for i in range(8)])
    return total


def after(array, *earlier):
    return lax.optimization_barrier((array, *earlier))[0]


END, INNER = 1, 0


def line_of_four(left, right):
    place = lax.axis_index("col")
    at_end = (place == 0) | (place == 3)
    side = at_end.astype(jnp.int32).reshape(1)
    pairs = lambda array, *earlier: lax.ppermute(after(array, *earlier), "col", [(0, 1), (1, 0), (2, 3), (3, 2)])
    middle = lambda array, *earlier: lax.ppermute(after(array, *earlier), "col", [(1, 2), (2, 1)])
    outward = lambda array: lax.ppermute(array, "col", [(1, 0), (2, 3)])
    extent = left.shape[2]
    half = extent // 2
    own0, own1, own2, own3 = blocked(left[0]), blocked(left[1]), blocked(left[2, :, :half]), blocked(left[2, :, half:])
    depth = own0.size // right.shape[2]
    chunk = lambda i: right[0, half + i * depth : half + (i + 1) * depth].reshape(own0.shape)
    chunks = half // depth

    near0 = pairs(own0)
    across0 = middle(own0)
    near1 = pairs(own1)
    across1 = middle(own1)
    near2 = pairs(own2, near0)
    across2 = middle(own2, across0)
    out0 = pairs(jnp.where(at_end, chunk(0), across0), near1)
    across3 = middle(own3, across1)
    out1 = pairs(jnp.where(at_end, chunk(1), across1), near2)
    far0 = middle(near0, across2)
    out2 = pairs(jnp.where(at_end, own3, across2), out0)
    far1 = middle(near1, across3)
    far2 = middle(near2, far0)
    far_out0 = pairs(jnp.where(at_end, chunk(2), far0), out1)
    far3 = middle(out2, far1)
    far_out1 = pairs(jnp.where(at_end, chunk(3), far1), out2)
    far_out2 = pairs(far2, far_out0)

    full = lambda array: (0, array, None)
    at_ends = lambda array: (0, array, END)
    first = products(
        [
            [[full(own0)], [full(near0)]],
            [[full(own1)], [full(near1)]],
            [[full(own2), (half, own3, None)], [full(near2)]],
        ],
        right,
        extent,
        side,
    )
    second = products(
        [
            [[full(across0), at_ends(out0)]],
            [[full(across1), at_ends(out1)]],
            [[full(across2), at_ends(out2), (half, across3, None)]],
        ],
        right,
        extent,
        side,
    )
    third = products(
        [[[full(far0), at_ends(far_out0)]], [], [[(half, far3, None)], [(half, out2, INNER)]]], right, extent, side
    )
    rest = lambda array, i: array[:, i * depth // LANES : (i + 1) * depth // LANES]
    for_end = [
        products(
            [[], [], [[full(rest(piece, i))] for piece in (own3, across3, far3)]],
            panel.reshape(1, depth, right.shape[2]),
            depth,
            side,
        )[:, 2]
        for i, panel in enumerate((out0, out1, far_out0, far_out1))
    ]
    from_neighbour = outward(functools.reduce(jnp.add, for_end))
    fourth = products([[], [[full(far1), at_ends(far_out1)]], []], right, extent, side)
    fifth = products([[], [], [[full(far2), at_ends(far_out2)]]], right, half, side)

    shards = jnp.stack([first[0], first[1], second[0], third[0] + fourth[0] + fifth[0]])
    shards = shards.at[1, 2].add(third[1, 2])
    shards = shards.at[1:, 2].add(from_neighbour)
    slots = lambda *at: functools.reduce(lambda rest, i: jnp.where(place == i, at[i], rest), range(3), at[3])
    where_is = (slots(0, 1, 3, 3), slots(1, 0, 2, 2), slots(2, 2, 0, 1), slots(3, 3, 1, 0))
    return jnp.stack([lax.dynamic_index_in_dim(shards, slot, 0, False) for slot in where_is])


def on_device(cols, rows, left_panels, right_panels, window_tiles):
    height, width = window_tiles.shape[1:]
    if cols == 4:
        shards = line_of_four(left_panels, right_panels)
    else:
        gathered = lax.all_gather(left_panels, "col", axis=1, tiled=True)
        lefts = [[[(0, blocked(gathered[a]), None)]] for a in range(ORDERS)]
        shards = products(lefts, right_panels, right_panels.shape[1], jnp.zeros((1,), jnp.int32))
    blocks = shards.reshape(-1, ORDERS, shards.shape[2] // height, height, width)
    blocks = jnp.swapaxes(blocks, 1, 2).reshape(rows, ORDERS, height, width)
    return 2.0 * window_tiles - sum_over_row(blocks, rows)


def solution(mesh):
    return jax.shard_map(
        functools.partial(on_device, mesh.shape["col"], mesh.shape["row"]),
        mesh=mesh,
        in_specs=(P(None, "col", "row"), P(None, "row", "col"), P(None, "row", "col")),
        out_specs=P(None, "row", "col"),
        check_vma=False,
    )
```

time: 135 us -> 113 us (0.84)
  waiting for transfers between devices: 78.5 us -> 28.3 us
  starting transfers between devices: 24.5 us -> 45.1 us
  local copies, waits for them, and re-layouts: 4.16 us -> 12 us
  Pallas kernels: 25.9 us -> 21.7 us
  other arithmetic: 0.64 us -> 4.69 us
    ppermute x15 -> x18, waiting for transfers between devices: 73.2 us -> 23.9 us  [the longest x9 23.9 us: line_of_four(): lax.ppermute(after(array, *earlier), 'col', [(0, 1), (1, 0), (2, 3), (3,...]
    ppermute x15 -> x18, starting transfers between devices: 20.9 us -> 41.4 us  [the longest x9 33.9 us: line_of_four(): lax.ppermute(after(array, *earlier), 'col', [(0, 1), (1, 0), (2, 3), (3,...]
    slice x0 -> x4, local copies, waits for them, and re-layouts: none -> 4.28 us  [the longest x1 2.62 us: line_of_four(): right[0, half + i * depth:half + (i + 1) * depth].reshape(own0.shape)]
    pallas_call x3 -> x9, Pallas kernels: 25.9 us -> 21.7 us  [products(): pl.pallas_call(functools.partial(products_kernel, layout, steps), grid=(s...]
    select_n x0 -> x5, other arithmetic: none -> 4.02 us  [the longest x1 1.22 us: line_of_four(): far_out0 = pairs(jnp.where(at_end, chunk(2), far0), out1)]
    unnamed x10 -> x33, local copies, waits for them, and re-layouts: 2.65 us -> 5.34 us
    transpose x0 -> x2, local copies, waits for them, and re-layouts: none -> 2.34 us  [blocked(): left.reshape(height // SUBLANES, SUBLANES, extent // LANES, LANES)]
    squeeze x2 -> x0, local copies, waits for them, and re-layouts: 1.47 us -> none  [the longest x1 1.46 us: line_of_four(): own = [left[order] for order in range(ORDERS)]]
  transfers between devices with their start and end apart: 19 -> 22, of which waited for: 12 -> 8; matrix products, arithmetic and copies ran while one was open for 0% -> 8% of each run, Pallas kernels for 13% -> 19%
where the time goes in v2:
time: 113 us; the launch traced here: 112 us
  starting transfers between devices  45.1 us (40%)
  waiting for transfers between devices  28.3 us (25%)
  Pallas kernels  21.7 us (19%)
  local copies, waits for them, and re-layouts  12 us (11%)
  other arithmetic  4.69 us (4%)
    ppermute x9, starting transfers between devices, line_of_four(): lax.ppermute(after(array, *earlier), 'col', [(0, 1), (1, 0), (2, 3), (3,...  33.9 us
    ppermute x9, waiting for transfers between devices, line_of_four(): lax.ppermute(after(array, *earlier), 'col', [(0, 1), (1, 0), (2, 3), (3,...  23.9 us
    pallas_call x9, Pallas kernels, products(): pl.pallas_call(functools.partial(products_kernel, layout, steps), grid=(s...  21.7 us
    ppermute x8, starting transfers between devices, line_of_four(): lax.ppermute(after(array, *earlier), 'col', [(1, 2), (2, 1)])  6.27 us
    unnamed x33, local copies, waits for them, and re-layouts  5.34 us
    ppermute x3, starting transfers between devices, sum_over_row(): lax.ppermute(block, 'row', [(i, i ^ 2 * offset) for i in range(8)])  3.55 us
    ppermute x3, waiting for transfers between devices, sum_over_row(): lax.ppermute(block, 'row', [(i, i ^ 2 * offset) for i in range(8)])  3.19 us
    slice x1, local copies, waits for them, and re-layouts, line_of_four(): right[0, half + i * depth:half + (i + 1) * depth].reshape(own0.shape)  2.62 us
  transfers between devices with their start and end apart: 22, of which 8 were waited for; matrix products, arithmetic and copies ran while one was open for 8% of the time, Pallas kernels for 19%

profile of v2, /device:TPU:0, one launch (start us, length us, event | category | flops | bytes accessed | tf_op | source)
XLA Modules:
  0.0 112.3 jit_solution(14739812720042255216)
XLA Ops:
  0.0 1.3 %slice_bitcast_fusion = (f32[2,64,8,128]{3,2,1,0:T(8,128)S(1)}, f32[2,64,8,128]{3,2,1,0:T(8,128)S(1)}) fusion(f32[3,16,8192]{2,1,0:T(8,128)} %param.7), kind=kLoop, calls=%fused_computation | loop fusion | bytes 2097152 | tf_op jit(solution)/shard_map/transpose | solution.py:23
  1.3 0.7 collective-permute-start.3
  2.0 5.9 %collective-permute-start = (f32[2,64,8,128]{3,2,1,0:T(8,128)S(1)}, f32[2,64,8,128]{3,2,1,0:T(8,128)}, u32[]{:S(2)}, u32[]{:S(2)}) collective-permute-start(f32[2,64,8,128]{3,2,1,0:T(8,128)S(1)} %get-tuple-element.62.refs_0_), channel_id=1, source_target_pairs={{0,1},{1,0},{2,3},{3,2},{4,5},{5,4},{6,7},{7,6},{8,9},{9,8},{10,11... | collective-permute-start | bytes 1572872 | tf_op jit(solution)/shard_map/ppermute | solution.py:150
  7.9 0.7 collective-permute-start.5
  8.6 1.8 %collective-permute-start.1 = (f32[2,64,8,128]{3,2,1,0:T(8,128)S(1)}, f32[2,64,8,128]{3,2,1,0:T(8,128)}, u32[]{:S(2)}, u32[]{:S(2)}) collective-permute-start(f32[2,64,8,128]{3,2,1,0:T(8,128)S(1)} %get-tuple-element.61.refs_2_), channel_id=1, source_target_pairs={{0,1},{1,0},{2,3},{3,2},{4,5},{5,4},{6,7},{7,6},{8,9},{9,8},{10,11... | collective-permute-start | bytes 1572872 | tf_op jit(solution)/shard_map/ppermute | solution.py:150
  10.3 2.6 %fusion.10 = (f32[1,1024,128]{2,1,0:T(8,128)}, f32[1,1024,128]{2,1,0:T(8,128)}, f32[1,1024,128]{2,1,0:T(8,128)S(1)}, f32[1,1024,128]{2,1,0:T(8,128)S(1)}) fusion(f32[3,8192,128]{2,1,0:T(8,128)} %refs_2_.3), kind=kLoop, calls=%fused_computation.39 | loop fusion | bytes 4194304 | tf_op jit(solution)/shard_map/slice | solution.py:157
  13.0 1.1 slice_bitcast_fusion.2
  14.0 0.7 collective-permute-start.7
  14.7 6.0 %collective-permute-done.refs_1_ = f32[2,64,8,128]{3,2,1,0:T(8,128)} collective-permute-done((f32[2,64,8,128]{3,2,1,0:T(8,128)S(1)}, f32[2,64,8,128]{3,2,1,0:T(8,128)}, u32[]{:S(2)}, u32[]{:S(2)}) %collective-permute-start) | collective-permute-done | bytes 524320 | tf_op jit(solution)/shard_map/ppermute | solution.py:150
  20.8 3.8 %collective-permute-start.2 = (f32[2,32,8,128]{3,2,1,0:T(8,128)S(1)}, f32[2,32,8,128]{3,2,1,0:T(8,128)S(1)}, u32[]{:S(2)}, u32[]{:S(2)}) collective-permute-start(f32[2,32,8,128]{3,2,1,0:T(8,128)S(1)} %get-tuple-element.42.refs_4_), channel_id=1, source_target_pairs={{0,1},{1,0},{2,3},{3,2},{4,5},{5,4},{6,7},{7,6},{8,9},{9,8},{10,11... | collective-permute-start | bytes 786440 | tf_op jit(solution)/shard_map/ppermute | solution.py:150
  24.6 1.4 %collective-permute-start.9 = (f32[2,32,8,128]{3,2,1,0:T(8,128)S(1)}, f32[2,32,8,128]{3,2,1,0:T(8,128)}, u32[]{:S(2)}, u32[]{:S(2)}) collective-permute-start(f32[2,32,8,128]{3,2,1,0:T(8,128)S(1)} %get-tuple-element.47.refs_5_), channel_id=1, source_target_pairs={{1,2},{2,1},{5,6},{6,5},{9,10},{10,9},{13,14},{14,13},{17,18},{18,... | collective-permute-start | bytes 786440 | tf_op jit(solution)/shard_map/ppermute | solution.py:151
  26.0 0.8 broadcast_select_fusion.3
  26.8 5.2 %collective-permute-done.1.refs_3_ = f32[2,64,8,128]{3,2,1,0:T(8,128)} collective-permute-done((f32[2,64,8,128]{3,2,1,0:T(8,128)S(1)}, f32[2,64,8,128]{3,2,1,0:T(8,128)}, u32[]{:S(2)}, u32[]{:S(2)}) %collective-permute-start.1) | collective-permute-done | bytes 524320 | tf_op jit(solution)/shard_map/ppermute | solution.py:150
  32.0 4.6 %collective-permute-start.4 = (f32[2,64,8,128]{3,2,1,0:T(8,128)}, f32[2,64,8,128]{3,2,1,0:T(8,128)S(1)}, u32[]{:S(2)}, u32[]{:S(2)}) collective-permute-start(f32[2,64,8,128]{3,2,1,0:T(8,128)} %broadcast_select_fusion.3), channel_id=1, source_target_pairs={{0,1},{1,0},{2,3},{3,2},{4,5},{5,4},{6,7},{7,6},{8,9},{9,8},{10,11... | collective-permute-start | bytes 1572872 | tf_op jit(solution)/shard_map/ppermute | solution.py:150
  36.6 0.7 collective-permute-start.10
  37.3 0.9 broadcast_select_fusion.2
  38.2 0.7 collective-permute-start.12
  38.9 0.7 copy-done.10
  39.6 8.2 %collective-permute-start.6 = (f32[2,64,8,128]{3,2,1,0:T(8,128)}, f32[2,64,8,128]{3,2,1,0:T(8,128)S(1)}, u32[]{:S(2)}, u32[]{:S(2)}) collective-permute-start(f32[2,64,8,128]{3,2,1,0:T(8,128)} %broadcast_select_fusion.2), channel_id=1, source_target_pairs={{0,1},{1,0},{2,3},{3,2},{4,5},{5,4},{6,7},{7,6},{8,9},{9,8},{10,11... | collective-permute-start | bytes 1572872 | tf_op jit(solution)/shard_map/ppermute | solution.py:150
  47.8 0.7 fusion.13
  48.5 1.0 broadcast_select_fusion.4
  49.6 0.9 collective-permute-start.8
  50.5 1.2 %broadcast_select_fusion.1 = f32[2,64,8,128]{3,2,1,0:T(8,128)S(1)} fusion(f32[2,64,8,128]{3,2,1,0:T(8,128)} %bitcast.77, f32[2,64,8,128]{3,2,1,0:T(8,128)S(1)} %collective-permute-done.10.refs_0_, pred[]{:T(512)S(6)} %or.3), kind=kLoop, calls=%fused_computation.5 | loop fusion | flops 131072 | bytes 1572865 | tf_op jit(solution)/shard_map/jit(_where)/select_n | solution.py:173
  51.7 9.1 %collective-permute-done.6.refs_3_ = f32[2,64,8,128]{3,2,1,0:T(8,128)S(1)} collective-permute-done((f32[2,64,8,128]{3,2,1,0:T(8,128)}, f32[2,64,8,128]{3,2,1,0:T(8,128)S(1)}, u32[]{:S(2)}, u32[]{:S(2)}) %collective-permute-start.6) | collective-permute-done | bytes 524320 | tf_op jit(solution)/shard_map/ppermute | solution.py:150
  60.9 2.0 %collective-permute-start.11 = (f32[2,64,8,128]{3,2,1,0:T(8,128)S(1)}, f32[2,64,8,128]{3,2,1,0:T(8,128)S(1)}, u32[]{:S(2)}, u32[]{:S(2)}) collective-permute-start(f32[2,64,8,128]{3,2,1,0:T(8,128)S(1)} %broadcast_select_fusion.1), channel_id=1, source_target_pairs={{0,1},{1,0},{2,3},{3,2},{4,5},{5,4},{6,7},{7,6},{8,9},{9,8},{10,11... | collective-permute-start | bytes 1572872 | tf_op jit(solution)/shard_map/ppermute | solution.py:150
  63.0 3.5 %collective-permute-done.8.refs_5_.refs_3_ = f32[2,32,8,128]{3,2,1,0:T(8,128)S(1)} collective-permute-done((f32[2,32,8,128]{3,2,1,0:T(8,128)S(1)}, f32[2,32,8,128]{3,2,1,0:T(8,128)S(1)}, u32[]{:S(2)}, u32[]{:S(2)}) %collective-permute-start.8) | collective-permute-done | bytes 262176 | tf_op jit(solution)/shard_map/ppermute | solution.py:150
  66.5 0.7 collective-permute-start.13
  67.2 3.8 %collective-permute-start.14 = (f32[2,64,8,128]{3,2,1,0:T(8,128)S(1)}, f32[2,64,8,128]{3,2,1,0:T(8,128)S(1)}, u32[]{:S(2)}, u32[]{:S(2)}) collective-permute-start(f32[2,64,8,128]{3,2,1,0:T(8,128)S(1)} %broadcast_select_fusion), channel_id=1, source_target_pairs={{0,1},{1,0},{2,3},{3,2},{4,5},{5,4},{6,7},{7,6},{8,9},{9,8},{10,11... | collective-permute-start | bytes 1572872 | tf_op jit(solution)/shard_map/ppermute | solution.py:150
  70.9 1.0 fusion.12
  71.9 4.6 %copy-done = f32[3,8192,128]{2,1,0:T(8,128)S(1)} copy-done((f32[3,8192,128]{2,1,0:T(8,128)S(1)}, f32[3,8192,128]{2,1,0:T(8,128)}, u32[]{:S(2)}) %copy-start) | copy-done | bytes 12582936
  76.5 7.3 %shard_map.37 = f32[2,3,16,128]{3,2,1,0:T(8,128)S(1)} custom-call(s32[1]{0:T(128)} %bitcast.side_ref, f32[2,64,8,128]{3,2,1,0:T(8,128)S(1)} %copy-done.5, f32[2,64,8,128]{3,2,1,0:T(8,128)} %collective-permute-done.refs_1_, f32[2,64,8,128]{3,2,1,0:T(8,128)S(1)} %copy-done.3, f32[2,64,8,128]{3,2,1,0:T(8,128)} %collective-permute-done.1.refs_3_, ...), custom_call_target="tpu_custom_call" | custom-call | flops 1610612736 | bytes 15466496 | tf_op jit(solution)/shard_map/pallas_call | solution.py:105
  83.9 0.8 collective-permute-start.15
  84.7 5.5 %shard_map.38 = f32[1,3,16,128]{3,2,1,0:T(8,128)S(1)} custom-call(s32[1]{0:T(128)} %bitcast.side_ref, f32[2,64,8,128]{3,2,1,0:T(8,128)S(1)} %collective-permute-done.3.refs_0_, f32[2,64,8,128]{3,2,1,0:T(8,128)S(1)} %collective-permute-done.4.refs_1_, f32[2,64,8,128]{3,2,1,0:T(8,128)S(1)} %collective-permute-done.5.refs_2_, ...), custom_call_target="tpu_custom_call" | custom-call | flops 805306368 | bytes 15466496 | tf_op jit(solution)/shard_map/pallas_call | solution.py:105
  90.2 0.2 shard_map.43
  90.4 0.2 shard_map.42
  90.7 2.9 %collective-permute-start.16 = (f32[2,32,8,128]{3,2,1,0:T(8,128)S(1)}, f32[2,32,8,128]{3,2,1,0:T(8,128)S(1)}, u32[]{:S(2)}, u32[]{:S(2)}) collective-permute-start(f32[2,32,8,128]{3,2,1,0:T(8,128)S(1)} %collective-permute-done.15.refs_0_), channel_id=1, source_target_pairs={{0,1},{1,0},{2,3},{3,2},{4,5},{5,4},{6,7},{7,6},{8,9},{9,8},{10,11... | collective-permute-start | bytes 786440 | tf_op jit(solution)/shard_map/ppermute | solution.py:150
  93.8 0.2 shard_map.45
  94.1 1.3 %collective-permute-start.17 = (f32[3,16,128]{2,1,0:T(8,128)S(1)}, f32[3,16,128]{2,1,0:T(8,128)S(1)}, u32[]{:S(2)}, u32[]{:S(2)}) collective-permute-start(f32[3,16,128]{2,1,0:T(8,128)S(1)} %fusion.1), channel_id=1, source_target_pairs={{1,0},{2,3},{5,4},{6,7},{9,8},{10,11},{13,12},{14,15},{17,16},{18,... | collective-permute-start | bytes 73736 | tf_op jit(solution)/shard_map/ppermute | solution.py:152
  95.4 3.0 %shard_map.40 = f32[1,3,16,128]{3,2,1,0:T(8,128)S(1)} custom-call(s32[1]{0:T(128)} %bitcast.side_ref, f32[2,64,8,128]{3,2,1,0:T(8,128)S(1)} %collective-permute-done.12.refs_0_, f32[2,64,8,128]{3,2,1,0:T(8,128)S(1)} %collective-permute-done.14.refs_1_, f32[3,8192,128]{2,1,0:T(8,128)S(1)} %copy-done.1), custom_call_target="tpu_custom_call" | custom-call | flops 268435456 | bytes 9437184 | tf_op jit(solution)/shard_map/pallas_call | solution.py:105
  98.4 4.2 %shard_map.39 = f32[2,3,16,128]{3,2,1,0:T(8,128)S(1)} custom-call(s32[1]{0:T(128)} %bitcast.side_ref, f32[2,64,8,128]{3,2,1,0:T(8,128)S(1)} %collective-permute-done.10.refs_0_, f32[2,64,8,128]{3,2,1,0:T(8,128)S(1)} %collective-permute-done.11.refs_1_, f32[2,32,8,128]{3,2,1,0:T(8,128)S(1)} %collective-permute-done.13.refs_2_, ...), custom_call_target="tpu_custom_call" | custom-call | flops 671088640 | bytes 14155776 | tf_op jit(solution)/shard_map/pallas_call | solution.py:105
  102.5 0.9 shard_map.41
  103.7 1.2 %collective-permute-done.18 = f32[4,3,8,128]{3,2,1,0:T(8,128)S(1)} collective-permute-done((f32[4,3,8,128]{3,2,1,0:T(8,128)S(1)}, f32[4,3,8,128]{3,2,1,0:T(8,128)S(1)}, u32[]{:S(2)}, u32[]{:S(2)}) %collective-permute-start.18) | collective-permute-done | bytes 49184 | tf_op jit(solution)/shard_map/ppermute | solution.py:131
  104.9 1.6 %collective-permute-start.19 = (f32[3,8,128]{2,1,0:T(8,128)S(1)}, f32[3,8,128]{2,1,0:T(8,128)S(1)}, u32[]{:S(2)}, u32[]{:S(2)}) collective-permute-start(f32[3,8,128]{2,1,0:T(8,128)S(1)} %get-tuple-element.81), channel_id=1, source_target_pairs={{0,8},{4,12},{8,0},{12,4},{16,24},{20,28},{24,16},{28,20},{1,9},{5... | collective-permute-start | bytes 36872 | tf_op jit(solution)/shard_map/ppermute | solution.py:135
  106.5 1.5 %collective-permute-start.21 = (f32[3,8,128]{2,1,0:T(8,128)S(1)}, f32[3,8,128]{2,1,0:T(8,128)S(1)}, u32[]{:S(2)}, u32[]{:S(2)}) collective-permute-start(f32[3,8,128]{2,1,0:T(8,128)S(1)} %get-tuple-element.82), channel_id=1, source_target_pairs={{0,24},{4,28},{8,16},{12,20},{16,8},{20,12},{24,0},{28,4},{1,25},{... | collective-permute-start | bytes 36872 | tf_op jit(solution)/shard_map/ppermute | solution.py:135
  108.0 0.5 collective-permute-start.20
  108.7 2.4 %collective-permute-done.21 = f32[3,8,128]{2,1,0:T(8,128)S(1)} collective-permute-done((f32[3,8,128]{2,1,0:T(8,128)S(1)}, f32[3,8,128]{2,1,0:T(8,128)S(1)}, u32[]{:S(2)}, u32[]{:S(2)}) %collective-permute-start.21) | collective-permute-done | bytes 12320 | tf_op jit(solution)/shard_map/ppermute | solution.py:135
  111.1 0.6 collective-permute-done.20
  111.7 0.6 fusion.7
  (60 shorter events, 0.8 us)
Async XLA Ops:
  1.3 11.7 %copy-start.2 = (f32[2,64,8,128]{3,2,1,0:T(8,128)}, f32[2,64,8,128]{3,2,1,0:T(8,128)S(1)}, u32[]{:S(2)}) copy-start(f32[2,64,8,128]{3,2,1,0:T(8,128)S(1)} %get-tuple-element.61.refs_2_) | copy-start | bytes 1572868
  1.3 11.7 %copy-start.4 = (f32[2,64,8,128]{3,2,1,0:T(8,128)}, f32[2,64,8,128]{3,2,1,0:T(8,128)S(1)}, u32[]{:S(2)}) copy-start(f32[2,64,8,128]{3,2,1,0:T(8,128)S(1)} %get-tuple-element.62.refs_0_) | copy-start | bytes 1572868
  1.3 12.7 %collective-permute-start.3 = (f32[2,64,8,128]{3,2,1,0:T(8,128)S(1)}, f32[2,64,8,128]{3,2,1,0:T(8,128)S(1)}, u32[]{:S(2)}, u32[]{:S(2)}) collective-permute-start(f32[2,64,8,128]{3,2,1,0:T(8,128)S(1)} %get-tuple-element.62.refs_0_), channel_id=1, source_target_pairs={{1,2},{2,1},{5,6},{6,5},{9,10},{10,9},{13,14},{14,13},{17,18},{18,... | collective-permute-start | bytes 1572872 | tf_op jit(solution)/shard_map/ppermute | solution.py:151
  2.0 18.8 %collective-permute-start = (f32[2,64,8,128]{3,2,1,0:T(8,128)S(1)}, f32[2,64,8,128]{3,2,1,0:T(8,128)}, u32[]{:S(2)}, u32[]{:S(2)}) collective-permute-start(f32[2,64,8,128]{3,2,1,0:T(8,128)S(1)} %get-tuple-element.62.refs_0_), channel_id=1, source_target_pairs={{0,1},{1,0},{2,3},{3,2},{4,5},{5,4},{6,7},{7,6},{8,9},{9,8},{10,11... | collective-permute-start | bytes 1572872 | tf_op jit(solution)/shard_map/ppermute | solution.py:150
  7.9 16.7 %collective-permute-start.5 = (f32[2,64,8,128]{3,2,1,0:T(8,128)S(1)}, f32[2,64,8,128]{3,2,1,0:T(8,128)S(1)}, u32[]{:S(2)}, u32[]{:S(2)}) collective-permute-start(f32[2,64,8,128]{3,2,1,0:T(8,128)S(1)} %get-tuple-element.61.refs_2_), channel_id=1, source_target_pairs={{1,2},{2,1},{5,6},{6,5},{9,10},{10,9},{13,14},{14,13},{17,18},{18,... | collective-permute-start | bytes 1572872 | tf_op jit(solution)/shard_map/ppermute | solution.py:151
  8.6 23.4 %collective-permute-start.1 = (f32[2,64,8,128]{3,2,1,0:T(8,128)S(1)}, f32[2,64,8,128]{3,2,1,0:T(8,128)}, u32[]{:S(2)}, u32[]{:S(2)}) collective-permute-start(f32[2,64,8,128]{3,2,1,0:T(8,128)S(1)} %get-tuple-element.61.refs_2_), channel_id=1, source_target_pairs={{0,1},{1,0},{2,3},{3,2},{4,5},{5,4},{6,7},{7,6},{8,9},{9,8},{10,11... | collective-permute-start | bytes 1572872 | tf_op jit(solution)/shard_map/ppermute | solution.py:150
  14.0 24.1 %copy-start.8 = (f32[2,32,8,128]{3,2,1,0:T(8,128)}, f32[2,32,8,128]{3,2,1,0:T(8,128)S(1)}, u32[]{:S(2)}) copy-start(f32[2,32,8,128]{3,2,1,0:T(8,128)S(1)} %get-tuple-element.42.refs_4_) | copy-start | bytes 786436
  14.0 22.5 %collective-permute-start.7 = (f32[2,32,8,128]{3,2,1,0:T(8,128)S(1)}, f32[2,32,8,128]{3,2,1,0:T(8,128)S(1)}, u32[]{:S(2)}, u32[]{:S(2)}) collective-permute-start(f32[2,32,8,128]{3,2,1,0:T(8,128)S(1)} %get-tuple-element.42.refs_4_), channel_id=1, source_target_pairs={{1,2},{2,1},{5,6},{6,5},{9,10},{10,9},{13,14},{14,13},{17,18},{18,... | collective-permute-start | bytes 786440 | tf_op jit(solution)/shard_map/ppermute | solution.py:151
  20.8 18.1 %collective-permute-start.2 = (f32[2,32,8,128]{3,2,1,0:T(8,128)S(1)}, f32[2,32,8,128]{3,2,1,0:T(8,128)S(1)}, u32[]{:S(2)}, u32[]{:S(2)}) collective-permute-start(f32[2,32,8,128]{3,2,1,0:T(8,128)S(1)} %get-tuple-element.42.refs_4_), channel_id=1, source_target_pairs={{0,1},{1,0},{2,3},{3,2},{4,5},{5,4},{6,7},{7,6},{8,9},{9,8},{10,11... | collective-permute-start | bytes 786440 | tf_op jit(solution)/shard_map/ppermute | solution.py:150
  24.6 13.6 %collective-permute-start.9 = (f32[2,32,8,128]{3,2,1,0:T(8,128)S(1)}, f32[2,32,8,128]{3,2,1,0:T(8,128)}, u32[]{:S(2)}, u32[]{:S(2)}) collective-permute-start(f32[2,32,8,128]{3,2,1,0:T(8,128)S(1)} %get-tuple-element.47.refs_5_), channel_id=1, source_target_pairs={{1,2},{2,1},{5,6},{6,5},{9,10},{10,9},{13,14},{14,13},{17,18},{18,... | collective-permute-start | bytes 786440 | tf_op jit(solution)/shard_map/ppermute | solution.py:151
  32.0 17.5 %collective-permute-start.4 = (f32[2,64,8,128]{3,2,1,0:T(8,128)}, f32[2,64,8,128]{3,2,1,0:T(8,128)S(1)}, u32[]{:S(2)}, u32[]{:S(2)}) collective-permute-start(f32[2,64,8,128]{3,2,1,0:T(8,128)} %broadcast_select_fusion.3), channel_id=1, source_target_pairs={{0,1},{1,0},{2,3},{3,2},{4,5},{5,4},{6,7},{7,6},{8,9},{9,8},{10,11... | collective-permute-start | bytes 1572872 | tf_op jit(solution)/shard_map/ppermute | solution.py:150
  36.6 2.3 %copy-start.6 = (f32[2,32,8,128]{3,2,1,0:T(8,128)}, f32[2,32,8,128]{3,2,1,0:T(8,128)S(1)}, u32[]{:S(2)}) copy-start(f32[2,32,8,128]{3,2,1,0:T(8,128)S(1)} %collective-permute-done.7.refs_4_) | copy-start | bytes 786436
  36.6 13.9 %collective-permute-start.10 = (f32[2,64,8,128]{3,2,1,0:T(8,128)}, f32[2,64,8,128]{3,2,1,0:T(8,128)S(1)}, u32[]{:S(2)}, u32[]{:S(2)}) collective-permute-start(f32[2,64,8,128]{3,2,1,0:T(8,128)} %collective-permute-done.refs_1_), channel_id=1, source_target_pairs={{1,2},{2,1},{5,6},{6,5},{9,10},{10,9},{13,14},{14,13},{17,18},{18,... | collective-permute-start | bytes 1572872 | tf_op jit(solution)/shard_map/ppermute | solution.py:151
  38.2 24.7 %collective-permute-start.12 = (f32[2,64,8,128]{3,2,1,0:T(8,128)}, f32[2,64,8,128]{3,2,1,0:T(8,128)S(1)}, u32[]{:S(2)}, u32[]{:S(2)}) collective-permute-start(f32[2,64,8,128]{3,2,1,0:T(8,128)} %collective-permute-done.1.refs_3_), channel_id=1, source_target_pairs={{1,2},{2,1},{5,6},{6,5},{9,10},{10,9},{13,14},{14,13},{17,18},{18,... | collective-permute-start | bytes 1572872 | tf_op jit(solution)/shard_map/ppermute | solution.py:151
  38.9 0.7 copy-start.10
  39.6 21.3 %collective-permute-start.6 = (f32[2,64,8,128]{3,2,1,0:T(8,128)}, f32[2,64,8,128]{3,2,1,0:T(8,128)S(1)}, u32[]{:S(2)}, u32[]{:S(2)}) collective-permute-start(f32[2,64,8,128]{3,2,1,0:T(8,128)} %broadcast_select_fusion.2), channel_id=1, source_target_pairs={{0,1},{1,0},{2,3},{3,2},{4,5},{5,4},{6,7},{7,6},{8,9},{9,8},{10,11... | collective-permute-start | bytes 1572872 | tf_op jit(solution)/shard_map/ppermute | solution.py:150
  48.5 14.4 %copy-start.14 = (f32[1,1024,128]{2,1,0:T(8,128)S(1)}, f32[1,1024,128]{2,1,0:T(8,128)}, u32[]{:S(2)}) copy-start(f32[1,1024,128]{2,1,0:T(8,128)} %get-tuple-element.55) | copy-start | bytes 1572868
  49.6 16.9 %collective-permute-start.8 = (f32[2,32,8,128]{3,2,1,0:T(8,128)S(1)}, f32[2,32,8,128]{3,2,1,0:T(8,128)S(1)}, u32[]{:S(2)}, u32[]{:S(2)}) collective-permute-start(f32[2,32,8,128]{3,2,1,0:T(8,128)S(1)} %broadcast_select_fusion.4), channel_id=1, source_target_pairs={{0,1},{1,0},{2,3},{3,2},{4,5},{5,4},{6,7},{7,6},{8,9},{9,8},{10,11... | collective-permute-start | bytes 786440 | tf_op jit(solution)/shard_map/ppermute | solution.py:150
  50.5 21.4 %copy-start.3 = (f32[2,64,8,128]{3,2,1,0:T(8,128)S(1)}, f32[2,64,8,128]{3,2,1,0:T(8,128)}, u32[]{:S(2)}) copy-start(f32[2,64,8,128]{3,2,1,0:T(8,128)} %copy-done.2) | copy-start | bytes 1572868
  50.5 21.4 %copy-start.5 = (f32[2,64,8,128]{3,2,1,0:T(8,128)S(1)}, f32[2,64,8,128]{3,2,1,0:T(8,128)}, u32[]{:S(2)}) copy-start(f32[2,64,8,128]{3,2,1,0:T(8,128)} %copy-done.4) | copy-start | bytes 1572868
  50.5 21.4 %copy-start.9 = (f32[2,32,8,128]{3,2,1,0:T(8,128)S(1)}, f32[2,32,8,128]{3,2,1,0:T(8,128)}, u32[]{:S(2)}) copy-start(f32[2,32,8,128]{3,2,1,0:T(8,128)} %copy-done.8) | copy-start | bytes 786436
  50.5 21.4 %copy-start.11 = (f32[2,32,8,128]{3,2,1,0:T(8,128)S(1)}, f32[2,32,8,128]{3,2,1,0:T(8,128)}, u32[]{:S(2)}) copy-start(f32[2,32,8,128]{3,2,1,0:T(8,128)} %copy-done.10) | copy-start | bytes 786436
  60.9 29.8 %collective-permute-start.11 = (f32[2,64,8,128]{3,2,1,0:T(8,128)S(1)}, f32[2,64,8,128]{3,2,1,0:T(8,128)S(1)}, u32[]{:S(2)}, u32[]{:S(2)}) collective-permute-start(f32[2,64,8,128]{3,2,1,0:T(8,128)S(1)} %broadcast_select_fusion.1), channel_id=1, source_target_pairs={{0,1},{1,0},{2,3},{3,2},{4,5},{5,4},{6,7},{7,6},{8,9},{9,8},{10,11... | collective-permute-start | bytes 1572872 | tf_op jit(solution)/shard_map/ppermute | solution.py:150
  66.5 23.7 %collective-permute-start.13 = (f32[2,32,8,128]{3,2,1,0:T(8,128)S(1)}, f32[2,32,8,128]{3,2,1,0:T(8,128)S(1)}, u32[]{:S(2)}, u32[]{:S(2)}) collective-permute-start(f32[2,32,8,128]{3,2,1,0:T(8,128)S(1)} %collective-permute-done.8.refs_5_.refs_3_), channel_id=1, source_target_pairs={{1,2},{2,1},{5,6},{6,5},{9,10},{10,9},{13,14},{14,13},{17,18},{18,... | collective-permute-start | bytes 786440 | tf_op jit(solution)/shard_map/ppermute | solution.py:151
  67.2 26.6 %collective-permute-start.14 = (f32[2,64,8,128]{3,2,1,0:T(8,128)S(1)}, f32[2,64,8,128]{3,2,1,0:T(8,128)S(1)}, u32[]{:S(2)}, u32[]{:S(2)}) collective-permute-start(f32[2,64,8,128]{3,2,1,0:T(8,128)S(1)} %broadcast_select_fusion), channel_id=1, source_target_pairs={{0,1},{1,0},{2,3},{3,2},{4,5},{5,4},{6,7},{7,6},{8,9},{9,8},{10,11... | collective-permute-start | bytes 1572872 | tf_op jit(solution)/shard_map/ppermute | solution.py:150
  71.9 4.6 %copy-start = (f32[3,8192,128]{2,1,0:T(8,128)S(1)}, f32[3,8192,128]{2,1,0:T(8,128)}, u32[]{:S(2)}) copy-start(f32[3,8192,128]{2,1,0:T(8,128)} %refs_2_.3) | copy-start | bytes 37748740
  76.5 8.2 %copy-start.1 = (f32[3,8192,128]{2,1,0:T(8,128)S(1)}, f32[3,8192,128]{2,1,0:T(8,128)}, u32[]{:S(2)}) copy-start(f32[3,8192,128]{2,1,0:T(8,128)} %refs_2_.3) | copy-start | bytes 37748740
  76.5 8.2 %copy-start.7 = (f32[2,32,8,128]{3,2,1,0:T(8,128)S(1)}, f32[2,32,8,128]{3,2,1,0:T(8,128)}, u32[]{:S(2)}) copy-start(f32[2,32,8,128]{3,2,1,0:T(8,128)} %copy-done.6) | copy-start | bytes 786436
  83.8 6.4 %copy-start.13 = (f32[2,8,8,128]{3,2,1,0:T(8,128)S(1)}, f32[2,8,8,128]{3,2,1,0:T(8,128)}, u32[]{:S(2)}) copy-start(f32[2,8,8,128]{3,2,1,0:T(8,128)} %get-tuple-element.73.refs_0_) | copy-start | bytes 196612
  83.8 6.6 %copy-start.12 = (f32[2,8,8,128]{3,2,1,0:T(8,128)S(1)}, f32[2,8,8,128]{3,2,1,0:T(8,128)}, u32[]{:S(2)}) copy-start(f32[2,8,8,128]{3,2,1,0:T(8,128)} %get-tuple-element.71.refs_0_) | copy-start | bytes 196612
  83.9 6.8 %collective-permute-start.15 = (f32[2,32,8,128]{3,2,1,0:T(8,128)S(1)}, f32[2,32,8,128]{3,2,1,0:T(8,128)S(1)}, u32[]{:S(2)}, u32[]{:S(2)}) collective-permute-start(f32[2,32,8,128]{3,2,1,0:T(8,128)S(1)} %copy-done.11), channel_id=1, source_target_pairs={{1,2},{2,1},{5,6},{6,5},{9,10},{10,9},{13,14},{14,13},{17,18},{18,... | collective-permute-start | bytes 786440 | tf_op jit(solution)/shard_map/ppermute | solution.py:151
  90.7 11.8 %collective-permute-start.16 = (f32[2,32,8,128]{3,2,1,0:T(8,128)S(1)}, f32[2,32,8,128]{3,2,1,0:T(8,128)S(1)}, u32[]{:S(2)}, u32[]{:S(2)}) collective-permute-start(f32[2,32,8,128]{3,2,1,0:T(8,128)S(1)} %collective-permute-done.15.refs_0_), channel_id=1, source_target_pairs={{0,1},{1,0},{2,3},{3,2},{4,5},{5,4},{6,7},{7,6},{8,9},{9,8},{10,11... | collective-permute-start | bytes 786440 | tf_op jit(solution)/shard_map/ppermute | solution.py:150
  94.1 9.4 %collective-permute-start.17 = (f32[3,16,128]{2,1,0:T(8,128)S(1)}, f32[3,16,128]{2,1,0:T(8,128)S(1)}, u32[]{:S(2)}, u32[]{:S(2)}) collective-permute-start(f32[3,16,128]{2,1,0:T(8,128)S(1)} %fusion.1), channel_id=1, source_target_pairs={{1,0},{2,3},{5,4},{6,7},{9,8},{10,11},{13,12},{14,15},{17,16},{18,... | collective-permute-start | bytes 73736 | tf_op jit(solution)/shard_map/ppermute | solution.py:152
  102.5 9.2 %copy-start.15 = (f32[3,8,128]{2,1,0:T(8,128)S(1)}, f32[3,8,128]{2,1,0:T(8,128)}, u32[]{:S(2)}) copy-start(f32[3,8,128]{2,1,0:T(8,128)} %param.9) | copy-start | bytes 36868
  103.6 1.3 %collective-permute-start.18 = (f32[4,3,8,128]{3,2,1,0:T(8,128)S(1)}, f32[4,3,8,128]{3,2,1,0:T(8,128)S(1)}, u32[]{:S(2)}, u32[]{:S(2)}) collective-permute-start(f32[4,3,8,128]{3,2,1,0:T(8,128)S(1)} %bitcast.80), channel_id=1, source_target_pairs={{0,4},{4,0},{8,12},{12,8},{16,20},{20,16},{24,28},{28,24},{1,5},{5... | collective-permute-start | bytes 147464 | tf_op jit(solution)/shard_map/ppermute | solution.py:131
  104.9 3.8 %collective-permute-start.19 = (f32[3,8,128]{2,1,0:T(8,128)S(1)}, f32[3,8,128]{2,1,0:T(8,128)S(1)}, u32[]{:S(2)}, u32[]{:S(2)}) collective-permute-start(f32[3,8,128]{2,1,0:T(8,128)S(1)} %get-tuple-element.81), channel_id=1, source_target_pairs={{0,8},{4,12},{8,0},{12,4},{16,24},{20,28},{24,16},{28,20},{1,9},{5... | collective-permute-start | bytes 36872 | tf_op jit(solution)/shard_map/ppermute | solution.py:135
  106.5 4.6 %collective-permute-start.21 = (f32[3,8,128]{2,1,0:T(8,128)S(1)}, f32[3,8,128]{2,1,0:T(8,128)S(1)}, u32[]{:S(2)}, u32[]{:S(2)}) collective-permute-start(f32[3,8,128]{2,1,0:T(8,128)S(1)} %get-tuple-element.82), channel_id=1, source_target_pairs={{0,24},{4,28},{8,16},{12,20},{16,8},{20,12},{24,0},{28,4},{1,25},{... | collective-permute-start | bytes 36872 | tf_op jit(solution)/shard_map/ppermute | solution.py:135
  108.0 3.7 %collective-permute-start.20 = (f32[3,8,128]{2,1,0:T(8,128)S(1)}, f32[3,8,128]{2,1,0:T(8,128)S(1)}, u32[]{:S(2)}, u32[]{:S(2)}) collective-permute-start(f32[3,8,128]{2,1,0:T(8,128)S(1)} %get-tuple-element.83), channel_id=1, source_target_pairs={{0,16},{4,20},{8,24},{12,28},{16,0},{20,4},{24,8},{28,12},{1,17},{... | collective-permute-start | bytes 36872 | tf_op jit(solution)/shard_map/ppermute | solution.py:135

commit v3 on v0

v3 whole, which is shorter than its diff:
```python
import functools

import jax
import jax.numpy as jnp
from jax import lax
from jax.experimental import pallas as pl
from jax.experimental.pallas import tpu as pltpu
from jax.sharding import PartitionSpec as P

ORDERS = 3
LANES, SUBLANES = 128, 8
TILE = 1024
VMEM_LIMIT = 48 * 1024 * 1024


def halves(values):
    high = values.astype(jnp.bfloat16)
    return high, (values - high.astype(jnp.float32)).astype(jnp.bfloat16)


def blocked(left):
    height, extent = left.shape
    return left.reshape(height // SUBLANES, SUBLANES, extent // LANES, LANES).transpose(0, 2, 1, 3)


def unblocked(blocks):
    return jnp.concatenate(
        [jnp.concatenate([blocks[a, c] for c in range(blocks.shape[1])], axis=1) for a in range(blocks.shape[0])], axis=0
    )


def products_kernel(layout, steps, orders, keep, side_ref, *refs):
    count = sum(len(terms) for sources in layout for terms in sources)
    left_refs, right_ref, out_ref = refs[:count], refs[count], refs[count + 1]
    kept_ref = refs[count + 2] if keep else None
    scratch = refs[count + 2 + bool(keep) :]
    totals, held = scratch[:orders], scratch[orders:]
    sources_of = [len(sources) for sources in layout]
    tile = right_ref.shape[1] // steps if not held else held[0].shape[1] // steps
    columns = tile // LANES

    def arrival(step):
        rows = pl.ds(step * tile, tile)
        return pltpu.make_async_copy(right_ref.at[:orders, rows], held[0].at[:, rows], held[1].at[step])

    def kept():
        return pltpu.make_async_copy(right_ref.at[:1, :keep], kept_ref, held[1].at[steps])

    if held:
        for step in range(steps):
            arrival(step).start()
        if keep:
            kept().start()
    panels = held[0] if held else right_ref

    @pl.loop(0, steps)
    def _(step):
        if held:
            arrival(step).wait()
        rows, place = [], 0
        for sources in layout:
            for terms in sources:
                piece = None
                for first, tiles, skip, side in terms:
                    at = skip + (jnp.clip(step - first, 0, tiles - 1) if tiles < steps else step)
                    term = unblocked(left_refs[place][:, pl.ds(at * columns, columns)])
                    counts = None
                    if tiles < steps:
                        counts = (step >= first) & (step < first + tiles)
                    if side is not None:
                        here = side_ref[0] == side
                        counts = here if counts is None else counts & here
                    if counts is not None:
                        term = jnp.where(counts, term, 0.0)
                    piece = term if piece is None else piece + term
                    place += 1
                rows.extend(halves(piece))
        stacked = jnp.concatenate(rows, axis=0)
        height = rows[0].shape[0]
        for order, parts in enumerate(totals):
            panel = jnp.concatenate(halves(panels[order, pl.ds(step * tile, tile), :]), axis=1)
            used = 2 * height * sum(sources_of[: ORDERS - order])
            parts[step] = jnp.dot(stacked[:used], panel, preferred_element_type=jnp.float32)

    if keep:
        kept().wait()
    height, width = out_ref.shape[2:]
    sums = [jnp.sum(parts[...], axis=0) for parts in totals]
    for source in range(max(sources_of)):
        for out_order in range(ORDERS):
            value = jnp.zeros((height, width), jnp.float32)
            first_row = 0
            for left_order in range(ORDERS):
                right_order = out_order - left_order
                if 0 <= right_order < len(totals) and source < sources_of[left_order]:
                    top = (first_row + source) * 2 * height
                    block = sums[right_order][top : top + 2 * height]
                    block = block[:height] + block[height:]
                    value = value + (block[:, :width] + block[:, width:])
                first_row += sources_of[left_order]
            out_ref[source, out_order] = value


def products(lefts, right, extent, side, resident=False, keep=0):
    flat = [term for sources in lefts for terms in sources for term in terms]
    height = flat[0][1].shape[0] * SUBLANES
    width = right.shape[2]
    tile = min(TILE, extent)
    steps = extent // tile
    tiles_of = lambda array, part: (extent if part is not None else array.shape[1] * LANES) // tile
    layout = [
        [
            [(first // tile, tiles_of(array, part), (part or 0) * steps, on) for first, array, on, part in terms]
            for terms in sources
        ]
        for sources in lefts
    ]
    sources_of = [len(sources) for sources in lefts]
    orders = min(ORDERS - min(a for a in range(ORDERS) if sources_of[a]), right.shape[0])
    rows_of = [2 * height * sum(sources_of[: ORDERS - order]) for order in range(orders)]
    in_vmem = pl.BlockSpec(memory_space=pltpu.VMEM)
    held = [] if resident else [
        pltpu.VMEM((orders, extent, width), jnp.float32),
        pltpu.SemaphoreType.DMA((steps + bool(keep),)),
    ]
    out = jax.ShapeDtypeStruct((max(sources_of), ORDERS, height, width), jnp.float32)
    kept = jax.ShapeDtypeStruct((1, keep, width), jnp.float32)
    return pl.pallas_call(
        functools.partial(products_kernel, layout, steps, orders, keep),
        in_specs=[pl.BlockSpec(memory_space=pltpu.SMEM)]
        + [in_vmem] * len(flat)
        + [in_vmem if resident else pl.BlockSpec(memory_space=pltpu.HBM)],
        out_specs=(in_vmem, in_vmem) if keep else in_vmem,
        out_shape=(out, kept) if keep else out,
        scratch_shapes=[pltpu.VMEM((steps, rows, 2 * width), jnp.float32) for rows in rows_of] + held,
        compiler_params=pltpu.CompilerParams(vmem_limit_bytes=VMEM_LIMIT),
        cost_estimate=pl.CostEstimate(
            flops=4 * sum(rows_of) * extent * width,
            bytes_accessed=4 * (sum(term[1].size for term in flat) + orders * extent * width),
            transcendentals=0,
        ),
    )(side, *[term[1] for term in flat], right)


def sum_over_row(blocks, row_size):
    if row_size != 8:
        return lax.psum_scatter(blocks, "row", scatter_dimension=0, tiled=True)[0]
    me = lax.axis_index("row")
    pairs = blocks.reshape((4, 2) + blocks.shape[1:])
    core, chip = me % 2, me // 2
    keep = lax.dynamic_index_in_dim(pairs, core, 1, False)
    give = lax.dynamic_index_in_dim(pairs, 1 - core, 1, False)
    mine = keep + lax.ppermute(give, "row", [(i, i ^ 1) for i in range(8)])
    total = lax.dynamic_index_in_dim(mine, chip, 0, False)
    for offset in (1, 2, 3):
        block = lax.dynamic_index_in_dim(mine, chip ^ offset, 0, False)
        total = total + lax.ppermute(block, "row", [(i, i ^ (2 * offset)) for i in range(8)])
    return total


def after(array, *earlier):
    return lax.optimization_barrier((array, *earlier))[0]


END, INNER = 1, 0


def line_of_four(left, right):
    place = lax.axis_index("col")
    at_end = (place == 0) | (place == 3)
    side = at_end.astype(jnp.int32).reshape(1)
    pairs = lambda array, *earlier: lax.ppermute(after(array, *earlier), "col", [(0, 1), (1, 0), (2, 3), (3, 2)])
    middle = lambda array, *earlier: lax.ppermute(after(array, *earlier), "col", [(1, 2), (2, 1)])
    outward = lambda array: lax.ppermute(array, "col", [(1, 0), (2, 3)])
    extent = left.shape[2]
    half = extent // 2
    own0, own1 = blocked(left[0]), blocked(left[1])
    left2 = after(left, own0, own1)[2]
    own2, own3 = blocked(left2[:, :half]), blocked(left2[:, half:])
    width = right.shape[2]
    depth = own0.size // width
    chunk = lambda i: right[0, half + i * depth : half + (i + 1) * depth].reshape(own0.shape)
    full = lambda array: (0, array, None, None)
    at_ends = lambda array: (0, array, END, None)
    upper = lambda array, on: (half, array, on, None)

    near0 = pairs(own0)
    across0 = middle(own0)
    near1 = pairs(own1)
    across1 = middle(own1)
    near2 = pairs(own2, near0, across0)
    across2 = middle(own2, near0, across0)
    out0 = pairs(jnp.where(at_end, chunk(0), across0), near1, across1)
    across3 = middle(own3, near1, across1)
    out1 = pairs(jnp.where(at_end, chunk(1), across1), near2, across2)
    far0 = middle(near0, near2, across2)
    first = products(
        [[[full(own0)], [full(near0)]], [[full(own1)], [full(near1)]], [[full(own2), upper(own3, None)], [full(near2)]]],
        right,
        extent,
        side,
    )
    out2 = pairs(jnp.where(at_end, own3, across2), out0, across3)
    far1 = middle(near1, out0, across3)
    far2 = middle(near2, out1, far0, first)
    far_out0 = pairs(jnp.where(at_end, chunk(2), far0), out1, far0, first)
    far3 = middle(out2, far1)
    far_out1 = pairs(jnp.where(at_end, chunk(3), far1), out2, far1)
    second = products(
        [
            [[full(across0), at_ends(out0)]],
            [[full(across1), at_ends(out1)]],
            [
                [full(across2), at_ends(out2), upper(across3, None)],
                [upper(far3, None)],
                [upper(out2, INNER)],
            ],
        ],
        right,
        extent,
        side,
    )
    for_end = lambda panel, i: products(
        [[], [], [[(0, piece, None, i)] for piece in (own3, across3, far3)]],
        panel.reshape(1, depth, width),
        depth,
        side,
        resident=True,
    )[:, 2]
    to_ends = for_end(out0, 0) + for_end(out1, 1)
    third = products([[[full(far0), at_ends(far_out0)]], [], []], right, extent, side)
    to_ends = to_ends + for_end(far_out0, 2)
    far_out2 = pairs(far2, far_out0, far2, second, third, to_ends)
    from_neighbour = outward(to_ends + for_end(far_out1, 3))
    fourth, panel = products([[], [[full(far1), at_ends(far_out1)]], []], right, extent, side, keep=half)
    fifth = products([[], [], [[full(far2), at_ends(far_out2)]]], panel, half, side, resident=True)

    shards = jnp.stack([first[0], first[1], second[0], third[0] + fourth[0] + fifth[0]])
    shards = shards.at[1, 2].add(second[2, 2]).at[3, 2].add(second[1, 2])
    shards = shards.at[1:, 2].add(from_neighbour)
    slots = lambda *at: functools.reduce(lambda rest, i: jnp.where(place == i, at[i], rest), range(3), at[3])
    where_is = (slots(0, 1, 3, 3), slots(1, 0, 2, 2), slots(2, 2, 0, 1), slots(3, 3, 1, 0))
    return jnp.stack([lax.dynamic_index_in_dim(shards, slot, 0, False) for slot in where_is])


def on_device(cols, rows, left_panels, right_panels, window_tiles):
    height, width = window_tiles.shape[1:]
    if cols == 4:
        shards = line_of_four(left_panels, right_panels)
    else:
        gathered = lax.all_gather(left_panels, "col", axis=1, tiled=True)
        lefts = [[[(0, blocked(gathered[a]), None, None)]] for a in range(ORDERS)]
        shards = products(lefts, right_panels, right_panels.shape[1], jnp.zeros((1,), jnp.int32))
    blocks = shards.reshape(-1, ORDERS, shards.shape[2] // height, height, width)
    blocks = jnp.swapaxes(blocks, 1, 2).reshape(rows, ORDERS, height, width)
    return 2.0 * window_tiles - sum_over_row(blocks, rows)


def solution(mesh):
    return jax.shard_map(
        functools.partial(on_device, mesh.shape["col"], mesh.shape["row"]),
        mesh=mesh,
        in_specs=(P(None, "col", "row"), P(None, "row", "col"), P(None, "row", "col")),
        out_specs=P(None, "row", "col"),
        check_vma=False,
    )
```

time: 210 us -> 107 us (0.51)
  waiting for transfers between devices: 169 us -> 34.4 us
  starting transfers between devices: 0.04 us -> 35.4 us
  matrix products: 23.7 us -> 0 us
  Pallas kernels: 0 us -> 23.6 us
  between operations: 14.1 us -> 0.41 us
  local copies, waits for them, and re-layouts: 0.61 us -> 9.16 us
    all_gather x1 -> x0, waiting for transfers between devices: 120 us -> none  [on_device(): lax.all_gather(left_panels, 'col', axis=1, tiled=True)]
    unnamed x3 -> x0, waiting for transfers between devices: 49.3 us -> none
    ppermute x0 -> x22, starting transfers between devices: none -> 35.4 us  [the longest x9 24.3 us: line_of_four(): lax.ppermute(after(array, *earlier), 'col', [(0, 1), (1, 0), (2, 3), (3,...]
    ppermute x0 -> x22, waiting for transfers between devices: none -> 34.4 us  [the longest x9 30 us: line_of_four(): lax.ppermute(after(array, *earlier), 'col', [(0, 1), (1, 0), (2, 3), (3,...]
    dot_general x6 -> x0, matrix products: 23.7 us -> none  [product(): jnp.dot(left_part, right_part, precision=lax.Precision.HIGHEST, preferred...]
    pallas_call x0 -> x9, Pallas kernels: none -> 23.6 us  [products(): pl.pallas_call(functools.partial(products_kernel, layout, steps, orders,...]
    select_n x0 -> x5, other arithmetic: none -> 3.14 us  [the longest x1 1.9 us: line_of_four(): out0 = pairs(jnp.where(at_end, chunk(0), across0), near1, across1)]
    slice x0 -> x1, local copies, waits for them, and re-layouts: none -> 2.88 us  [line_of_four(): right[0, half + i * depth:half + (i + 1) * depth].reshape(own0.shape)]
  transfers between devices with their start and end apart: 2 -> 22, of which waited for: 2 -> 11; matrix products, arithmetic and copies ran while one was open for 0% -> 8% of each run, Pallas kernels for 0% -> 22%
where the time goes in v3:
time: 107 us
  starting transfers between devices  35.4 us (33%)
  waiting for transfers between devices  34.4 us (32%)
  Pallas kernels  23.6 us (22%)
  local copies, waits for them, and re-layouts  9.16 us (9%)
  other arithmetic  3.81 us (4%)
    ppermute x9, waiting for transfers between devices, line_of_four(): lax.ppermute(after(array, *earlier), 'col', [(0, 1), (1, 0), (2, 3), (3,...  30 us
    ppermute x9, starting transfers between devices, line_of_four(): lax.ppermute(after(array, *earlier), 'col', [(0, 1), (1, 0), (2, 3), (3,...  24.3 us
    pallas_call x9, Pallas kernels, products(): pl.pallas_call(functools.partial(products_kernel, layout, steps, orders,...  23.6 us
    ppermute x8, starting transfers between devices, line_of_four(): lax.ppermute(after(array, *earlier), 'col', [(1, 2), (2, 1)])  6.11 us
    ppermute x3, starting transfers between devices, sum_over_row(): lax.ppermute(block, 'row', [(i, i ^ 2 * offset) for i in range(8)])  3.55 us
    ppermute x3, waiting for transfers between devices, sum_over_row(): lax.ppermute(block, 'row', [(i, i ^ 2 * offset) for i in range(8)])  3.19 us
    slice x1, local copies, waits for them, and re-layouts, line_of_four(): right[0, half + i * depth:half + (i + 1) * depth].reshape(own0.shape)  2.88 us
    transpose x2, local copies, waits for them, and re-layouts, blocked(): left.reshape(height // SUBLANES, SUBLANES, extent // LANES, LANES)  2.33 us
  transfers between devices with their start and end apart: 22, of which 11 were waited for; matrix products, arithmetic and copies ran while one was open for 8% of the time, Pallas kernels for 22%

profile of v3, /device:TPU:0, one launch (start us, length us, event | category | flops | bytes accessed | tf_op | source)
XLA Modules:
  0.0 106.7 jit_solution(1667310645876102922)
XLA Ops:
  0.0 1.3 %slice_bitcast_fusion.1 = (f32[2,64,8,128]{3,2,1,0:T(8,128)S(1)}, f32[2,64,8,128]{3,2,1,0:T(8,128)S(1)}) fusion(f32[3,16,8192]{2,1,0:T(8,128)} %param.9), kind=kLoop, calls=%fused_computation.1 | loop fusion | bytes 2097152 | tf_op jit(solution)/shard_map/transpose | solution.py:23
  1.3 0.7 collective-permute-start.2
  2.0 5.9 %collective-permute-start = (f32[2,64,8,128]{3,2,1,0:T(8,128)S(1)}, f32[2,64,8,128]{3,2,1,0:T(8,128)S(1)}, u32[]{:S(2)}, u32[]{:S(2)}) collective-permute-start(f32[2,64,8,128]{3,2,1,0:T(8,128)S(1)} %get-tuple-element.78.refs_0_), channel_id=1, source_target_pairs={{0,1},{1,0},{2,3},{3,2},{4,5},{5,4},{6,7},{7,6},{8,9},{9,8},{10,11... | collective-permute-start | bytes 1572872 | tf_op jit(solution)/shard_map/ppermute | solution.py:172
  7.9 0.7 collective-permute-start.4
  8.5 1.8 %collective-permute-start.1 = (f32[2,64,8,128]{3,2,1,0:T(8,128)S(1)}, f32[2,64,8,128]{3,2,1,0:T(8,128)}, u32[]{:S(2)}, u32[]{:S(2)}) collective-permute-start(f32[2,64,8,128]{3,2,1,0:T(8,128)S(1)} %get-tuple-element.77.refs_2_), channel_id=1, source_target_pairs={{0,1},{1,0},{2,3},{3,2},{4,5},{5,4},{6,7},{7,6},{8,9},{9,8},{10,11... | collective-permute-start | bytes 1572872 | tf_op jit(solution)/shard_map/ppermute | solution.py:172
  10.3 1.9 %slice_bitcast_fusion = f32[16,8192]{1,0:T(8,128)} fusion(f32[3,16,8192]{2,1,0:T(8,128)} %param.9), kind=kLoop, calls=%fused_computation | loop fusion | bytes 1048576 | tf_op jit(solution)/shard_map/squeeze | solution.py:178
  12.2 2.9 %fusion.14 = (f32[1,1024,128]{2,1,0:T(8,128)}, f32[1,1024,128]{2,1,0:T(8,128)}, f32[1,1024,128]{2,1,0:T(8,128)}, f32[1,1024,128]{2,1,0:T(8,128)}) fusion(f32[3,8192,128]{2,1,0:T(8,128)} %refs_2_.3), kind=kLoop, calls=%fused_computation.47 | loop fusion | bytes 4194304 | tf_op jit(solution)/shard_map/slice | solution.py:182
  15.1 1.1 slice_bitcast_fusion.3
  16.1 4.5 %collective-permute-done.refs_1_ = f32[2,64,8,128]{3,2,1,0:T(8,128)S(1)} collective-permute-done((f32[2,64,8,128]{3,2,1,0:T(8,128)S(1)}, f32[2,64,8,128]{3,2,1,0:T(8,128)S(1)}, u32[]{:S(2)}, u32[]{:S(2)}) %collective-permute-start) | collective-permute-done | bytes 524320 | tf_op jit(solution)/shard_map/ppermute | solution.py:172
  20.6 0.7 collective-permute-start.6
  21.3 3.8 %collective-permute-start.3 = (f32[2,32,8,128]{3,2,1,0:T(8,128)S(1)}, f32[2,32,8,128]{3,2,1,0:T(8,128)}, u32[]{:S(2)}, u32[]{:S(2)}) collective-permute-start(f32[2,32,8,128]{3,2,1,0:T(8,128)S(1)} %get-tuple-element.57.refs_4_), channel_id=1, source_target_pairs={{0,1},{1,0},{2,3},{3,2},{4,5},{5,4},{6,7},{7,6},{8,9},{9,8},{10,11... | collective-permute-start | bytes 786440 | tf_op jit(solution)/shard_map/ppermute | solution.py:172
  25.1 1.9 %broadcast_select_fusion.3 = f32[2,64,8,128]{3,2,1,0:T(8,128)} fusion(f32[2,64,8,128]{3,2,1,0:T(8,128)} %bitcast.109, f32[2,64,8,128]{3,2,1,0:T(8,128)S(1)} %collective-permute-done.2.refs_0_, pred[]{:T(512)S(6)} %or.3), kind=kLoop, calls=%fused_computation.8 | loop fusion | flops 131072 | bytes 1572865 | tf_op jit(solution)/shard_map/jit(_where)/select_n | solution.py:193
  27.0 5.0 %collective-permute-done.1.refs_3_ = f32[2,64,8,128]{3,2,1,0:T(8,128)} collective-permute-done((f32[2,64,8,128]{3,2,1,0:T(8,128)S(1)}, f32[2,64,8,128]{3,2,1,0:T(8,128)}, u32[]{:S(2)}, u32[]{:S(2)}) %collective-permute-start.1) | collective-permute-done | bytes 524320 | tf_op jit(solution)/shard_map/ppermute | solution.py:172
  32.0 2.1 %collective-permute-start.5 = (f32[2,64,8,128]{3,2,1,0:T(8,128)}, f32[2,64,8,128]{3,2,1,0:T(8,128)S(1)}, u32[]{:S(2)}, u32[]{:S(2)}) collective-permute-start(f32[2,64,8,128]{3,2,1,0:T(8,128)} %broadcast_select_fusion.3), channel_id=1, source_target_pairs={{0,1},{1,0},{2,3},{3,2},{4,5},{5,4},{6,7},{7,6},{8,9},{9,8},{10,11... | collective-permute-start | bytes 1572872 | tf_op jit(solution)/shard_map/ppermute | solution.py:172
  34.0 0.7 collective-permute-start.8
  34.7 2.9 %collective-permute-done.3.refs_6_ = f32[2,32,8,128]{3,2,1,0:T(8,128)} collective-permute-done((f32[2,32,8,128]{3,2,1,0:T(8,128)S(1)}, f32[2,32,8,128]{3,2,1,0:T(8,128)}, u32[]{:S(2)}, u32[]{:S(2)}) %collective-permute-start.3) | collective-permute-done | bytes 262176 | tf_op jit(solution)/shard_map/ppermute | solution.py:172
  37.6 0.7 collective-permute-start.12
  38.3 1.1 %broadcast_select_fusion.2 = f32[2,64,8,128]{3,2,1,0:T(8,128)S(1)} fusion(f32[2,64,8,128]{3,2,1,0:T(8,128)} %bitcast.108, f32[2,64,8,128]{3,2,1,0:T(8,128)S(1)} %collective-permute-done.4.refs_2_, pred[]{:T(512)S(6)} %or.3), kind=kLoop, calls=%fused_computation.7 | loop fusion | flops 131072 | bytes 1572865 | tf_op jit(solution)/shard_map/jit(_where)/select_n | solution.py:195
  39.4 2.8 %collective-permute-start.7 = (f32[2,64,8,128]{3,2,1,0:T(8,128)S(1)}, f32[2,64,8,128]{3,2,1,0:T(8,128)S(1)}, u32[]{:S(2)}, u32[]{:S(2)}) collective-permute-start(f32[2,64,8,128]{3,2,1,0:T(8,128)S(1)} %broadcast_select_fusion.2), channel_id=1, source_target_pairs={{0,1},{1,0},{2,3},{3,2},{4,5},{5,4},{6,7},{7,6},{8,9},{9,8},{10,11... | collective-permute-start | bytes 1572872 | tf_op jit(solution)/shard_map/ppermute | solution.py:172
  42.2 6.6 %collective-permute-done.5.refs_1_ = f32[2,64,8,128]{3,2,1,0:T(8,128)S(1)} collective-permute-done((f32[2,64,8,128]{3,2,1,0:T(8,128)}, f32[2,64,8,128]{3,2,1,0:T(8,128)S(1)}, u32[]{:S(2)}, u32[]{:S(2)}) %collective-permute-start.5) | collective-permute-done | bytes 524320 | tf_op jit(solution)/shard_map/ppermute | solution.py:172
  48.7 0.7 collective-permute-start.10
  49.4 0.9 copy-done.3
  50.4 1.0 copy-done.5
  51.4 6.5 %shard_map.37 = f32[2,3,16,128]{3,2,1,0:T(8,128)S(1)} custom-call(s32[1]{0:T(128)} %bitcast.side_ref, f32[2,64,8,128]{3,2,1,0:T(8,128)S(1)} %get-tuple-element.78.refs_0_, f32[2,64,8,128]{3,2,1,0:T(8,128)S(1)} %copy-done.5, f32[2,64,8,128]{3,2,1,0:T(8,128)S(1)} %get-tuple-element.77.refs_2_, f32[2,64,8,128]{3,2,1,0:T(8,128)} %collective-permute-done.1.refs_3_, ...), custom_call_target="tpu_custom_call" | custom-call | flops 1610612736 | bytes 15466496 | tf_op jit(solution)/shard_map/pallas_call | solution.py:128
  58.0 3.8 %collective-permute-start.9 = (f32[2,32,8,128]{3,2,1,0:T(8,128)S(1)}, f32[2,32,8,128]{3,2,1,0:T(8,128)S(1)}, u32[]{:S(2)}, u32[]{:S(2)}) collective-permute-start(f32[2,32,8,128]{3,2,1,0:T(8,128)S(1)} %broadcast_select_fusion.4), channel_id=1, source_target_pairs={{0,1},{1,0},{2,3},{3,2},{4,5},{5,4},{6,7},{7,6},{8,9},{9,8},{10,11... | collective-permute-start | bytes 786440 | tf_op jit(solution)/shard_map/ppermute | solution.py:172
  62.0 7.0 %collective-permute-done.9.refs_5_.refs_8_ = f32[2,32,8,128]{3,2,1,0:T(8,128)S(1)} collective-permute-done((f32[2,32,8,128]{3,2,1,0:T(8,128)S(1)}, f32[2,32,8,128]{3,2,1,0:T(8,128)S(1)}, u32[]{:S(2)}, u32[]{:S(2)}) %collective-permute-start.9) | collective-permute-done | bytes 262176 | tf_op jit(solution)/shard_map/ppermute | solution.py:172
  69.0 2.0 %collective-permute-start.14 = (f32[2,64,8,128]{3,2,1,0:T(8,128)S(1)}, f32[2,64,8,128]{3,2,1,0:T(8,128)S(1)}, u32[]{:S(2)}, u32[]{:S(2)}) collective-permute-start(f32[2,64,8,128]{3,2,1,0:T(8,128)S(1)} %broadcast_select_fusion), channel_id=1, source_target_pairs={{0,1},{1,0},{2,3},{3,2},{4,5},{5,4},{6,7},{7,6},{8,9},{9,8},{10,11... | collective-permute-start | bytes 1572872 | tf_op jit(solution)/shard_map/ppermute | solution.py:172
  71.0 0.7 collective-permute-start.11
  71.7 1.4 %collective-permute-start.15 = (f32[2,32,8,128]{3,2,1,0:T(8,128)}, f32[2,32,8,128]{3,2,1,0:T(8,128)}, u32[]{:S(2)}, u32[]{:S(2)}) collective-permute-start(f32[2,32,8,128]{3,2,1,0:T(8,128)} %collective-permute-done.3.refs_6_), channel_id=1, source_target_pairs={{1,2},{2,1},{5,6},{6,5},{9,10},{10,9},{13,14},{14,13},{17,18},{18,... | collective-permute-start | bytes 786440 | tf_op jit(solution)/shard_map/ppermute | solution.py:173
  73.1 0.2 shard_map.41
  73.3 0.2 shard_map.42
  73.5 5.2 %shard_map.38 = f32[3,3,16,128]{3,2,1,0:T(8,128)S(1)} custom-call(s32[1]{0:T(128)} %bitcast.side_ref, f32[2,64,8,128]{3,2,1,0:T(8,128)S(1)} %collective-permute-done.2.refs_0_, f32[2,64,8,128]{3,2,1,0:T(8,128)S(1)} %collective-permute-done.5.refs_1_, f32[2,64,8,128]{3,2,1,0:T(8,128)S(1)} %collective-permute-done.4.refs_2_, ...), custom_call_target="tpu_custom_call" | custom-call | flops 1073741824 | bytes 15990784 | tf_op jit(solution)/shard_map/pallas_call | solution.py:128
  78.7 1.5 %collective-permute-done.13.refs_1_ = f32[2,64,8,128]{3,2,1,0:T(8,128)S(1)} collective-permute-done((f32[2,64,8,128]{3,2,1,0:T(8,128)S(1)}, f32[2,64,8,128]{3,2,1,0:T(8,128)S(1)}, u32[]{:S(2)}, u32[]{:S(2)}) %collective-permute-start.13) | collective-permute-done | bytes 524320 | tf_op jit(solution)/shard_map/ppermute | solution.py:172
  80.2 0.2 shard_map.43
  80.4 5.1 %shard_map.39 = f32[1,3,16,128]{3,2,1,0:T(8,128)S(1)} custom-call(s32[1]{0:T(128)} %bitcast.side_ref, f32[2,64,8,128]{3,2,1,0:T(8,128)S(1)} %collective-permute-done.12.refs_0_, f32[2,64,8,128]{3,2,1,0:T(8,128)S(1)} %collective-permute-done.13.refs_1_, f32[3,8192,128]{2,1,0:T(8,128)} %refs_2_.3), custom_call_target="tpu_custom_call" | custom-call | flops 402653184 | bytes 13631488 | tf_op jit(solution)/shard_map/pallas_call | solution.py:128
  85.6 2.6 %collective-permute-done.14.refs_1_ = f32[2,64,8,128]{3,2,1,0:T(8,128)S(1)} collective-permute-done((f32[2,64,8,128]{3,2,1,0:T(8,128)S(1)}, f32[2,64,8,128]{3,2,1,0:T(8,128)S(1)}, u32[]{:S(2)}, u32[]{:S(2)}) %collective-permute-start.14) | collective-permute-done | bytes 524320 | tf_op jit(solution)/shard_map/ppermute | solution.py:172
  88.2 0.2 shard_map.45
  88.4 2.2 %collective-permute-start.16 = (f32[2,32,8,128]{3,2,1,0:T(8,128)}, f32[2,32,8,128]{3,2,1,0:T(8,128)S(1)}, u32[]{:S(2)}, u32[]{:S(2)}) collective-permute-start(f32[2,32,8,128]{3,2,1,0:T(8,128)} %collective-permute-done.15.refs_0_), channel_id=1, source_target_pairs={{0,1},{1,0},{2,3},{3,2},{4,5},{5,4},{6,7},{7,6},{8,9},{9,8},{10,11... | collective-permute-start | bytes 786440 | tf_op jit(solution)/shard_map/ppermute | solution.py:172
  90.6 1.3 %collective-permute-start.17 = (f32[3,16,128]{2,1,0:T(8,128)S(1)}, f32[3,16,128]{2,1,0:T(8,128)S(1)}, u32[]{:S(2)}, u32[]{:S(2)}) collective-permute-start(f32[3,16,128]{2,1,0:T(8,128)S(1)} %fusion.1), channel_id=1, source_target_pairs={{1,0},{2,3},{5,4},{6,7},{9,8},{10,11},{13,12},{14,15},{17,16},{18,... | collective-permute-start | bytes 73736 | tf_op jit(solution)/shard_map/ppermute | solution.py:174
  91.9 4.2 %shard_map.40 = (f32[1,3,16,128]{3,2,1,0:T(8,128)S(1)}, f32[1,4096,128]{2,1,0:T(8,128)S(1)}) custom-call(s32[1]{0:T(128)} %bitcast.side_ref, f32[2,64,8,128]{3,2,1,0:T(8,128)S(1)} %collective-permute-done.10.refs_0_, f32[2,64,8,128]{3,2,1,0:T(8,128)S(1)} %collective-permute-done.14.refs_1_, f32[3,8192,128]{2,1,0:T(8,128)} %refs_2_.3), custom_call_target="tpu_custom_call" | custom-call | flops 268435456 | bytes 9437184 | tf_op jit(solution)/shard_map/pallas_call | solution.py:128
  96.1 1.7 %shard_map.44 = f32[1,3,16,128]{3,2,1,0:T(8,128)S(1)} custom-call(s32[1]{0:T(128)} %bitcast.side_ref, f32[2,32,8,128]{3,2,1,0:T(8,128)} %collective-permute-done.15.refs_0_, f32[2,32,8,128]{3,2,1,0:T(8,128)S(1)} %collective-permute-done.16.refs_1_, f32[1,4096,128]{2,1,0:T(8,128)S(1)} %get-tuple-element.70.refs_2_), custom_call_target="tpu_custom_call" | custom-call | flops 67108864 | bytes 2621440 | tf_op jit(solution)/shard_map/pallas_call | solution.py:128
  98.1 1.2 %collective-permute-done.18 = f32[4,3,8,128]{3,2,1,0:T(8,128)S(1)} collective-permute-done((f32[4,3,8,128]{3,2,1,0:T(8,128)S(1)}, f32[4,3,8,128]{3,2,1,0:T(8,128)S(1)}, u32[]{:S(2)}, u32[]{:S(2)}) %collective-permute-start.18) | collective-permute-done | bytes 49184 | tf_op jit(solution)/shard_map/ppermute | solution.py:153
  99.4 1.6 %collective-permute-start.19 = (f32[3,8,128]{2,1,0:T(8,128)S(1)}, f32[3,8,128]{2,1,0:T(8,128)S(1)}, u32[]{:S(2)}, u32[]{:S(2)}) collective-permute-start(f32[3,8,128]{2,1,0:T(8,128)S(1)} %get-tuple-element.87), channel_id=1, source_target_pairs={{0,8},{4,12},{8,0},{12,4},{16,24},{20,28},{24,16},{28,20},{1,9},{5... | collective-permute-start | bytes 36872 | tf_op jit(solution)/shard_map/ppermute | solution.py:157
  100.9 1.5 %collective-permute-start.21 = (f32[3,8,128]{2,1,0:T(8,128)S(1)}, f32[3,8,128]{2,1,0:T(8,128)S(1)}, u32[]{:S(2)}, u32[]{:S(2)}) collective-permute-start(f32[3,8,128]{2,1,0:T(8,128)S(1)} %get-tuple-element.88), channel_id=1, source_target_pairs={{0,24},{4,28},{8,16},{12,20},{16,8},{20,12},{24,0},{28,4},{1,25},{... | collective-permute-start | bytes 36872 | tf_op jit(solution)/shard_map/ppermute | solution.py:157
  102.4 0.5 collective-permute-start.20
  103.1 2.4 %collective-permute-done.21 = f32[3,8,128]{2,1,0:T(8,128)S(1)} collective-permute-done((f32[3,8,128]{2,1,0:T(8,128)S(1)}, f32[3,8,128]{2,1,0:T(8,128)S(1)}, u32[]{:S(2)}, u32[]{:S(2)}) %collective-permute-start.21) | collective-permute-done | bytes 12320 | tf_op jit(solution)/shard_map/ppermute | solution.py:157
  105.5 0.6 collective-permute-done.20
  106.1 0.6 fusion.8
  (48 shorter events, 0.7 us)
Async XLA Ops:
  1.3 14.9 %collective-permute-start.2 = (f32[2,64,8,128]{3,2,1,0:T(8,128)S(1)}, f32[2,64,8,128]{3,2,1,0:T(8,128)S(1)}, u32[]{:S(2)}, u32[]{:S(2)}) collective-permute-start(f32[2,64,8,128]{3,2,1,0:T(8,128)S(1)} %get-tuple-element.78.refs_0_), channel_id=1, source_target_pairs={{1,2},{2,1},{5,6},{6,5},{9,10},{10,9},{13,14},{14,13},{17,18},{18,... | collective-permute-start | bytes 1572872 | tf_op jit(solution)/shard_map/ppermute | solution.py:173
  2.0 18.7 %collective-permute-start = (f32[2,64,8,128]{3,2,1,0:T(8,128)S(1)}, f32[2,64,8,128]{3,2,1,0:T(8,128)S(1)}, u32[]{:S(2)}, u32[]{:S(2)}) collective-permute-start(f32[2,64,8,128]{3,2,1,0:T(8,128)S(1)} %get-tuple-element.78.refs_0_), channel_id=1, source_target_pairs={{0,1},{1,0},{2,3},{3,2},{4,5},{5,4},{6,7},{7,6},{8,9},{9,8},{10,11... | collective-permute-start | bytes 1572872 | tf_op jit(solution)/shard_map/ppermute | solution.py:172
  7.9 19.2 %collective-permute-start.4 = (f32[2,64,8,128]{3,2,1,0:T(8,128)S(1)}, f32[2,64,8,128]{3,2,1,0:T(8,128)S(1)}, u32[]{:S(2)}, u32[]{:S(2)}) collective-permute-start(f32[2,64,8,128]{3,2,1,0:T(8,128)S(1)} %get-tuple-element.77.refs_2_), channel_id=1, source_target_pairs={{1,2},{2,1},{5,6},{6,5},{9,10},{10,9},{13,14},{14,13},{17,18},{18,... | collective-permute-start | bytes 1572872 | tf_op jit(solution)/shard_map/ppermute | solution.py:173
  8.5 23.4 %collective-permute-start.1 = (f32[2,64,8,128]{3,2,1,0:T(8,128)S(1)}, f32[2,64,8,128]{3,2,1,0:T(8,128)}, u32[]{:S(2)}, u32[]{:S(2)}) collective-permute-start(f32[2,64,8,128]{3,2,1,0:T(8,128)S(1)} %get-tuple-element.77.refs_2_), channel_id=1, source_target_pairs={{0,1},{1,0},{2,3},{3,2},{4,5},{5,4},{6,7},{7,6},{8,9},{9,8},{10,11... | collective-permute-start | bytes 1572872 | tf_op jit(solution)/shard_map/ppermute | solution.py:172
  16.1 26.0 %copy-start.2 = (f32[2,32,8,128]{3,2,1,0:T(8,128)}, f32[2,32,8,128]{3,2,1,0:T(8,128)S(1)}, u32[]{:S(2)}) copy-start(f32[2,32,8,128]{3,2,1,0:T(8,128)S(1)} %get-tuple-element.57.refs_4_) | copy-start | bytes 786436
  20.6 6.4 %copy-start.4 = (f32[2,64,8,128]{3,2,1,0:T(8,128)}, f32[2,64,8,128]{3,2,1,0:T(8,128)S(1)}, u32[]{:S(2)}) copy-start(f32[2,64,8,128]{3,2,1,0:T(8,128)S(1)} %collective-permute-done.refs_1_) | copy-start | bytes 1572868
  20.6 14.1 %collective-permute-start.6 = (f32[2,32,8,128]{3,2,1,0:T(8,128)S(1)}, f32[2,32,8,128]{3,2,1,0:T(8,128)S(1)}, u32[]{:S(2)}, u32[]{:S(2)}) collective-permute-start(f32[2,32,8,128]{3,2,1,0:T(8,128)S(1)} %get-tuple-element.57.refs_4_), channel_id=1, source_target_pairs={{1,2},{2,1},{5,6},{6,5},{9,10},{10,9},{13,14},{14,13},{17,18},{18,... | collective-permute-start | bytes 786440 | tf_op jit(solution)/shard_map/ppermute | solution.py:173
  21.3 16.3 %collective-permute-start.3 = (f32[2,32,8,128]{3,2,1,0:T(8,128)S(1)}, f32[2,32,8,128]{3,2,1,0:T(8,128)}, u32[]{:S(2)}, u32[]{:S(2)}) collective-permute-start(f32[2,32,8,128]{3,2,1,0:T(8,128)S(1)} %get-tuple-element.57.refs_4_), channel_id=1, source_target_pairs={{0,1},{1,0},{2,3},{3,2},{4,5},{5,4},{6,7},{7,6},{8,9},{9,8},{10,11... | collective-permute-start | bytes 786440 | tf_op jit(solution)/shard_map/ppermute | solution.py:172
  32.0 16.7 %collective-permute-start.5 = (f32[2,64,8,128]{3,2,1,0:T(8,128)}, f32[2,64,8,128]{3,2,1,0:T(8,128)S(1)}, u32[]{:S(2)}, u32[]{:S(2)}) collective-permute-start(f32[2,64,8,128]{3,2,1,0:T(8,128)} %broadcast_select_fusion.3), channel_id=1, source_target_pairs={{0,1},{1,0},{2,3},{3,2},{4,5},{5,4},{6,7},{7,6},{8,9},{9,8},{10,11... | collective-permute-start | bytes 1572872 | tf_op jit(solution)/shard_map/ppermute | solution.py:172
  34.0 8.1 %collective-permute-start.8 = (f32[2,32,8,128]{3,2,1,0:T(8,128)S(1)}, f32[2,32,8,128]{3,2,1,0:T(8,128)S(1)}, u32[]{:S(2)}, u32[]{:S(2)}) collective-permute-start(f32[2,32,8,128]{3,2,1,0:T(8,128)S(1)} %get-tuple-element.60.refs_5_.refs_0_), channel_id=1, source_target_pairs={{1,2},{2,1},{5,6},{6,5},{9,10},{10,9},{13,14},{14,13},{17,18},{18,... | collective-permute-start | bytes 786440 | tf_op jit(solution)/shard_map/ppermute | solution.py:173
  34.7 7.4 %copy-start = (f32[2,32,8,128]{3,2,1,0:T(8,128)}, f32[2,32,8,128]{3,2,1,0:T(8,128)S(1)}, u32[]{:S(2)}) copy-start(f32[2,32,8,128]{3,2,1,0:T(8,128)S(1)} %collective-permute-done.6.refs_4_) | copy-start | bytes 786436
  37.6 24.2 %collective-permute-start.12 = (f32[2,64,8,128]{3,2,1,0:T(8,128)}, f32[2,64,8,128]{3,2,1,0:T(8,128)S(1)}, u32[]{:S(2)}, u32[]{:S(2)}) collective-permute-start(f32[2,64,8,128]{3,2,1,0:T(8,128)} %copy-done.4), channel_id=1, source_target_pairs={{1,2},{2,1},{5,6},{6,5},{9,10},{10,9},{13,14},{14,13},{17,18},{18,... | collective-permute-start | bytes 1572872 | tf_op jit(solution)/shard_map/ppermute | solution.py:173
  39.4 22.4 %collective-permute-start.7 = (f32[2,64,8,128]{3,2,1,0:T(8,128)S(1)}, f32[2,64,8,128]{3,2,1,0:T(8,128)S(1)}, u32[]{:S(2)}, u32[]{:S(2)}) collective-permute-start(f32[2,64,8,128]{3,2,1,0:T(8,128)S(1)} %broadcast_select_fusion.2), channel_id=1, source_target_pairs={{0,1},{1,0},{2,3},{3,2},{4,5},{5,4},{6,7},{7,6},{8,9},{9,8},{10,11... | collective-permute-start | bytes 1572872 | tf_op jit(solution)/shard_map/ppermute | solution.py:172
  48.7 13.2 %collective-permute-start.10 = (f32[2,64,8,128]{3,2,1,0:T(8,128)}, f32[2,64,8,128]{3,2,1,0:T(8,128)S(1)}, u32[]{:S(2)}, u32[]{:S(2)}) collective-permute-start(f32[2,64,8,128]{3,2,1,0:T(8,128)} %collective-permute-done.1.refs_3_), channel_id=1, source_target_pairs={{1,2},{2,1},{5,6},{6,5},{9,10},{10,9},{13,14},{14,13},{17,18},{18,... | collective-permute-start | bytes 1572872 | tf_op jit(solution)/shard_map/ppermute | solution.py:173
  49.4 1.0 copy-start.3
  50.4 1.0 copy-start.5
  51.4 6.5 %copy-start.1 = (f32[2,32,8,128]{3,2,1,0:T(8,128)S(1)}, f32[2,32,8,128]{3,2,1,0:T(8,128)}, u32[]{:S(2)}) copy-start(f32[2,32,8,128]{3,2,1,0:T(8,128)} %copy-done) | copy-start | bytes 786436
  51.4 6.5 %copy-start.6 = (f32[16,8192]{1,0:T(8,128)S(1)}, f32[16,8192]{1,0:T(8,128)}, u32[]{:S(2)}) copy-start(f32[16,8192]{1,0:T(8,128)} %slice_bitcast_fusion) | copy-start | bytes 1572868
  51.4 10.3 %copy-start.8 = (f32[1,1024,128]{2,1,0:T(8,128)S(1)}, f32[1,1024,128]{2,1,0:T(8,128)}, u32[]{:S(2)}) copy-start(f32[1,1024,128]{2,1,0:T(8,128)} %get-tuple-element.74) | copy-start | bytes 1572868
  57.9 4.0 %copy-start.7 = (f32[1,1024,128]{2,1,0:T(8,128)S(1)}, f32[1,1024,128]{2,1,0:T(8,128)}, u32[]{:S(2)}) copy-start(f32[1,1024,128]{2,1,0:T(8,128)} %get-tuple-element.73) | copy-start | bytes 1572868
  58.0 11.0 %collective-permute-start.9 = (f32[2,32,8,128]{3,2,1,0:T(8,128)S(1)}, f32[2,32,8,128]{3,2,1,0:T(8,128)S(1)}, u32[]{:S(2)}, u32[]{:S(2)}) collective-permute-start(f32[2,32,8,128]{3,2,1,0:T(8,128)S(1)} %broadcast_select_fusion.4), channel_id=1, source_target_pairs={{0,1},{1,0},{2,3},{3,2},{4,5},{5,4},{6,7},{7,6},{8,9},{9,8},{10,11... | collective-permute-start | bytes 786440 | tf_op jit(solution)/shard_map/ppermute | solution.py:172
  61.8 18.4 %collective-permute-start.13 = (f32[2,64,8,128]{3,2,1,0:T(8,128)S(1)}, f32[2,64,8,128]{3,2,1,0:T(8,128)S(1)}, u32[]{:S(2)}, u32[]{:S(2)}) collective-permute-start(f32[2,64,8,128]{3,2,1,0:T(8,128)S(1)} %broadcast_select_fusion.1), channel_id=1, source_target_pairs={{0,1},{1,0},{2,3},{3,2},{4,5},{5,4},{6,7},{7,6},{8,9},{9,8},{10,11... | collective-permute-start | bytes 1572872 | tf_op jit(solution)/shard_map/ppermute | solution.py:172
  69.0 19.2 %collective-permute-start.14 = (f32[2,64,8,128]{3,2,1,0:T(8,128)S(1)}, f32[2,64,8,128]{3,2,1,0:T(8,128)S(1)}, u32[]{:S(2)}, u32[]{:S(2)}) collective-permute-start(f32[2,64,8,128]{3,2,1,0:T(8,128)S(1)} %broadcast_select_fusion), channel_id=1, source_target_pairs={{0,1},{1,0},{2,3},{3,2},{4,5},{5,4},{6,7},{7,6},{8,9},{9,8},{10,11... | collective-permute-start | bytes 1572872 | tf_op jit(solution)/shard_map/ppermute | solution.py:172
  71.0 2.0 %collective-permute-start.11 = (f32[2,32,8,128]{3,2,1,0:T(8,128)S(1)}, f32[2,32,8,128]{3,2,1,0:T(8,128)S(1)}, u32[]{:S(2)}, u32[]{:S(2)}) collective-permute-start(f32[2,32,8,128]{3,2,1,0:T(8,128)S(1)} %collective-permute-done.9.refs_5_.refs_8_), channel_id=1, source_target_pairs={{1,2},{2,1},{5,6},{6,5},{9,10},{10,9},{13,14},{14,13},{17,18},{18,... | collective-permute-start | bytes 786440 | tf_op jit(solution)/shard_map/ppermute | solution.py:173
  71.7 16.7 %collective-permute-start.15 = (f32[2,32,8,128]{3,2,1,0:T(8,128)}, f32[2,32,8,128]{3,2,1,0:T(8,128)}, u32[]{:S(2)}, u32[]{:S(2)}) collective-permute-start(f32[2,32,8,128]{3,2,1,0:T(8,128)} %collective-permute-done.3.refs_6_), channel_id=1, source_target_pairs={{1,2},{2,1},{5,6},{6,5},{9,10},{10,9},{13,14},{14,13},{17,18},{18,... | collective-permute-start | bytes 786440 | tf_op jit(solution)/shard_map/ppermute | solution.py:173
  88.4 7.7 %collective-permute-start.16 = (f32[2,32,8,128]{3,2,1,0:T(8,128)}, f32[2,32,8,128]{3,2,1,0:T(8,128)S(1)}, u32[]{:S(2)}, u32[]{:S(2)}) collective-permute-start(f32[2,32,8,128]{3,2,1,0:T(8,128)} %collective-permute-done.15.refs_0_), channel_id=1, source_target_pairs={{0,1},{1,0},{2,3},{3,2},{4,5},{5,4},{6,7},{7,6},{8,9},{9,8},{10,11... | collective-permute-start | bytes 786440 | tf_op jit(solution)/shard_map/ppermute | solution.py:172
  90.6 7.3 %collective-permute-start.17 = (f32[3,16,128]{2,1,0:T(8,128)S(1)}, f32[3,16,128]{2,1,0:T(8,128)S(1)}, u32[]{:S(2)}, u32[]{:S(2)}) collective-permute-start(f32[3,16,128]{2,1,0:T(8,128)S(1)} %fusion.1), channel_id=1, source_target_pairs={{1,0},{2,3},{5,4},{6,7},{9,8},{10,11},{13,12},{14,15},{17,16},{18,... | collective-permute-start | bytes 73736 | tf_op jit(solution)/shard_map/ppermute | solution.py:174
  96.1 10.0 %copy-start.9 = (f32[3,8,128]{2,1,0:T(8,128)S(1)}, f32[3,8,128]{2,1,0:T(8,128)}, u32[]{:S(2)}) copy-start(f32[3,8,128]{2,1,0:T(8,128)} %param.11) | copy-start | bytes 36868
  98.0 1.3 %collective-permute-start.18 = (f32[4,3,8,128]{3,2,1,0:T(8,128)S(1)}, f32[4,3,8,128]{3,2,1,0:T(8,128)S(1)}, u32[]{:S(2)}, u32[]{:S(2)}) collective-permute-start(f32[4,3,8,128]{3,2,1,0:T(8,128)S(1)} %bitcast.110), channel_id=1, source_target_pairs={{0,4},{4,0},{8,12},{12,8},{16,20},{20,16},{24,28},{28,24},{1,5},{5... | collective-permute-start | bytes 147464 | tf_op jit(solution)/shard_map/ppermute | solution.py:153
  99.4 3.8 %collective-permute-start.19 = (f32[3,8,128]{2,1,0:T(8,128)S(1)}, f32[3,8,128]{2,1,0:T(8,128)S(1)}, u32[]{:S(2)}, u32[]{:S(2)}) collective-permute-start(f32[3,8,128]{2,1,0:T(8,128)S(1)} %get-tuple-element.87), channel_id=1, source_target_pairs={{0,8},{4,12},{8,0},{12,4},{16,24},{20,28},{24,16},{28,20},{1,9},{5... | collective-permute-start | bytes 36872 | tf_op jit(solution)/shard_map/ppermute | solution.py:157
  100.9 4.6 %collective-permute-start.21 = (f32[3,8,128]{2,1,0:T(8,128)S(1)}, f32[3,8,128]{2,1,0:T(8,128)S(1)}, u32[]{:S(2)}, u32[]{:S(2)}) collective-permute-start(f32[3,8,128]{2,1,0:T(8,128)S(1)} %get-tuple-element.88), channel_id=1, source_target_pairs={{0,24},{4,28},{8,16},{12,20},{16,8},{20,12},{24,0},{28,4},{1,25},{... | collective-permute-start | bytes 36872 | tf_op jit(solution)/shard_map/ppermute | solution.py:157
  102.4 3.7 %collective-permute-start.20 = (f32[3,8,128]{2,1,0:T(8,128)S(1)}, f32[3,8,128]{2,1,0:T(8,128)S(1)}, u32[]{:S(2)}, u32[]{:S(2)}) collective-permute-start(f32[3,8,128]{2,1,0:T(8,128)S(1)} %get-tuple-element.89), channel_id=1, source_target_pairs={{0,16},{4,20},{8,24},{12,28},{16,0},{20,4},{24,8},{28,12},{1,17},{... | collective-permute-start | bytes 36872 | tf_op jit(solution)/shard_map/ppermute | solution.py:157

commit v4 on v3

v4 whole, which is shorter than its diff:
```python
import functools

import jax
import jax.numpy as jnp
from jax import lax
from jax.experimental import pallas as pl
from jax.experimental.pallas import tpu as pltpu
from jax.sharding import PartitionSpec as P

ORDERS = 3
LANES, SUBLANES = 128, 8
TILE = 1024
VMEM_LIMIT = 48 * 1024 * 1024


def halves(values):
    high = values.astype(jnp.bfloat16)
    return high, (values - high.astype(jnp.float32)).astype(jnp.bfloat16)


def blocked(left):
    height, extent = left.shape
    return left.reshape(height // SUBLANES, SUBLANES, extent // LANES, LANES).transpose(0, 2, 1, 3)


def unblocked(blocks):
    return jnp.concatenate(
        [jnp.concatenate([blocks[a, c] for c in range(blocks.shape[1])], axis=1) for a in range(blocks.shape[0])], axis=0
    )


def products_kernel(layout, steps, orders, keep, only, side_ref, *refs):
    count = sum(len(terms) for sources in layout for terms in sources)
    left_refs, right_ref, out_ref = refs[:count], refs[count], refs[count + 1]
    kept_ref = refs[count + 2] if keep else None
    scratch = refs[count + 2 + bool(keep) :]
    totals, held = scratch[:orders], scratch[orders:]
    sources_of = [len(sources) for sources in layout]
    tile = right_ref.shape[1] // steps if not held else held[0].shape[1] // steps
    columns = tile // LANES

    def arrival(step):
        rows = pl.ds(step * tile, tile)
        return pltpu.make_async_copy(right_ref.at[:orders, rows], held[0].at[:, rows], held[1].at[step])

    def add_up():
        if held:
            for step in range(steps):
                arrival(step).start()
        panels = held[0] if held else right_ref

        @pl.loop(0, steps)
        def _(step):
            if held:
                arrival(step).wait()
            if keep:

                @pl.when(step < keep // tile)
                def _():
                    rows = pl.ds(step * tile, tile)
                    kept_ref[0, rows] = panels[0, rows]
            rows, place = [], 0
            for sources in layout:
                for terms in sources:
                    piece = None
                    for first, tiles, skip, side in terms:
                        at = skip + (jnp.clip(step - first, 0, tiles - 1) if tiles < steps else step)
                        term = unblocked(left_refs[place][:, pl.ds(at * columns, columns)])
                        counts = None
                        if tiles < steps:
                            counts = (step >= first) & (step < first + tiles)
                        if side is not None:
                            here = side_ref[0] == side
                            counts = here if counts is None else counts & here
                        if counts is not None:
                            term = jnp.where(counts, term, 0.0)
                        piece = term if piece is None else piece + term
                        place += 1
                    rows.extend(halves(piece))
            stacked = jnp.concatenate(rows, axis=0)
            height = rows[0].shape[0]
            for order, parts in enumerate(totals):
                panel = jnp.concatenate(halves(panels[order, pl.ds(step * tile, tile), :]), axis=1)
                used = 2 * height * sum(sources_of[: ORDERS - order])
                parts[step] = jnp.dot(stacked[:used], panel, preferred_element_type=jnp.float32)

        height, width = out_ref.shape[2:]
        sums = [jnp.sum(parts[...], axis=0) for parts in totals]
        for source in range(max(sources_of)):
            for out_order in range(ORDERS):
                value = jnp.zeros((height, width), jnp.float32)
                first_row = 0
                for left_order in range(ORDERS):
                    right_order = out_order - left_order
                    if 0 <= right_order < len(totals) and source < sources_of[left_order]:
                        top = (first_row + source) * 2 * height
                        block = sums[right_order][top : top + 2 * height]
                        block = block[:height] + block[height:]
                        value = value + (block[:, :width] + block[:, width:])
                    first_row += sources_of[left_order]
                out_ref[source, out_order] = value

    if only is None:
        add_up()
    else:
        here = side_ref[0] == only
        pl.when(here)(add_up)

        @pl.when(jnp.logical_not(here))
        def _():
            out_ref[...] = jnp.zeros_like(out_ref)


def products(lefts, right, extent, side, resident=False, keep=0, only=None):
    flat = [term for sources in lefts for terms in sources for term in terms]
    height = flat[0][1].shape[0] * SUBLANES
    width = right.shape[2]
    tile = min(TILE, extent)
    steps = extent // tile
    tiles_of = lambda array, part: (extent if part is not None else array.shape[1] * LANES) // tile
    layout = [
        [
            [(first // tile, tiles_of(array, part), (part or 0) * steps, on) for first, array, on, part in terms]
            for terms in sources
        ]
        for sources in lefts
    ]
    sources_of = [len(sources) for sources in lefts]
    orders = min(ORDERS - min(a for a in range(ORDERS) if sources_of[a]), right.shape[0])
    rows_of = [2 * height * sum(sources_of[: ORDERS - order]) for order in range(orders)]
    in_vmem = pl.BlockSpec(memory_space=pltpu.VMEM)
    held = [] if resident else [
        pltpu.VMEM((orders, extent, width), jnp.float32),
        pltpu.SemaphoreType.DMA((steps,)),
    ]
    out = jax.ShapeDtypeStruct((max(sources_of), ORDERS, height, width), jnp.float32)
    kept = jax.ShapeDtypeStruct((1, keep, width), jnp.float32)
    return pl.pallas_call(
        functools.partial(products_kernel, layout, steps, orders, keep, only),
        in_specs=[pl.BlockSpec(memory_space=pltpu.SMEM)]
        + [in_vmem] * len(flat)
        + [in_vmem if resident else pl.BlockSpec(memory_space=pltpu.HBM)],
        out_specs=(in_vmem, in_vmem) if keep else in_vmem,
        out_shape=(out, kept) if keep else out,
        scratch_shapes=[pltpu.VMEM((steps, rows, 2 * width), jnp.float32) for rows in rows_of] + held,
        compiler_params=pltpu.CompilerParams(vmem_limit_bytes=VMEM_LIMIT),
        cost_estimate=pl.CostEstimate(
            flops=int(3 * 4 * sum(rows_of) * extent * width),
            bytes_accessed=int(3 * 4 * (sum(term[1].size for term in flat) + orders * extent * width)),
            transcendentals=0,
        ),
    )(side, *[term[1] for term in flat], right)


def sum_over_row(blocks, row_size):
    if row_size != 8:
        return lax.psum_scatter(blocks, "row", scatter_dimension=0, tiled=True)[0]
    me = lax.axis_index("row")
    pairs = blocks.reshape((4, 2) + blocks.shape[1:])
    core, chip = me % 2, me // 2
    keep = lax.dynamic_index_in_dim(pairs, core, 1, False)
    give = lax.dynamic_index_in_dim(pairs, 1 - core, 1, False)
    mine = keep + lax.ppermute(give, "row", [(i, i ^ 1) for i in range(8)])
    total = lax.dynamic_index_in_dim(mine, chip, 0, False)
    for offset in (3, 1, 2):
        block = lax.dynamic_index_in_dim(mine, chip ^ offset, 0, False)
        total = total + lax.ppermute(block, "row", [(i, i ^ (2 * offset)) for i in range(8)])
    return total


def after(array, *earlier):
    return lax.optimization_barrier((array, *earlier))[0]


END, INNER = 1, 0


def line_of_four(left, right):
    place = lax.axis_index("col")
    at_end = (place == 0) | (place == 3)
    side = at_end.astype(jnp.int32).reshape(1)
    pairs = lambda array, *earlier: lax.ppermute(after(array, *earlier), "col", [(0, 1), (1, 0), (2, 3), (3, 2)])
    middle = lambda array, *earlier: lax.ppermute(after(array, *earlier), "col", [(1, 2), (2, 1)])
    outward = lambda array: lax.ppermute(array, "col", [(1, 0), (2, 3)])
    extent = left.shape[2]
    half = extent // 2
    own0, own1 = blocked(left[0]), blocked(left[1])
    left2 = after(left, own0, own1)[2]
    own2, own3 = blocked(left2[:, :half]), blocked(left2[:, half:])
    width = right.shape[2]
    depth = own0.size // width
    chunk = lambda i: right[0, half + i * depth : half + (i + 1) * depth].reshape(own0.shape)
    full = lambda array: (0, array, None, None)
    at_ends = lambda array: (0, array, END, None)
    upper = lambda array, on: (half, array, on, None)
    for_end = lambda panel, i, side: products(
        [[], [], [[(0, piece, None, i)] for piece in (own3, across3, far3)]],
        panel.reshape(1, depth, width),
        depth,
        side,
        resident=True,
        only=INNER,
    )[:, 2]

    near0 = pairs(own0)
    across0 = middle(own0)
    near1 = pairs(own1)
    across1 = middle(own1)
    near2 = pairs(own2, near0, across0)
    across3 = middle(own3, near1, across1)
    across2 = middle(own2, near0, across0)
    far0 = middle(near0, near2, across2)
    out0 = pairs(jnp.where(at_end, chunk(0), across0), near1, across1)
    out1 = pairs(jnp.where(at_end, chunk(1), across1), near2)
    first = products([[[full(own0)], [full(near0)]], [[full(own1)], [full(near1)]], [[full(own2), upper(own3, None)], [full(near2)]]], right, extent, side)
    out2 = pairs(jnp.where(at_end, own3, across2), out0, across3, first)
    far2 = middle(near2, out1, far0)
    far1 = middle(near1, out0, across3, first)
    far_out0 = pairs(jnp.where(at_end, chunk(2), far0))
    second = products([[[full(across0), at_ends(out0)]], [[full(across1), at_ends(out1)]], []], right, extent, side)
    far3 = middle(out2, far1, second)
    third = products([[[full(far0), at_ends(far_out0)]], [[full(far1)]], [[full(far2), upper(far3, None)], [full(across2), at_ends(out2), upper(across3, None)], [upper(out2, INNER)]]], right, extent, side)
    far_out1 = pairs(jnp.where(at_end, chunk(3), far1), out2, far1, second)
    end0 = for_end(out0, 0, side)
    end1 = for_end(out1, 1, side)
    end2 = for_end(far_out0, 2, side)
    far_out2 = pairs(far2, far_out0, far2)
    end3 = for_end(far_out1, 3, side)
    back = outward(after(end0 + end1 + end2 + end3, third))
    fourth, panel = products([[], [[full(far_out1)]], []], right, extent, side, keep=half, only=END)
    fifth = products([[], [], [[full(far_out2)]]], panel, half, side, resident=True, only=END)

    shards = jnp.stack([first[0], first[1], second[0], third[0] + fourth[0] + fifth[0]])
    shards = shards.at[1, 2].add(third[2, 2]).at[2, 2].add(third[1, 2])
    shards = shards.at[1:, 2].add(back)
    slots = lambda *at: functools.reduce(lambda rest, i: jnp.where(place == i, at[i], rest), range(3), at[3])
    where_is = (slots(0, 1, 3, 3), slots(1, 0, 2, 2), slots(2, 2, 0, 1), slots(3, 3, 1, 0))
    return jnp.stack([lax.dynamic_index_in_dim(shards, slot, 0, False) for slot in where_is])


def on_device(cols, rows, left_panels, right_panels, window_tiles):
    height, width = window_tiles.shape[1:]
    chunks = right_panels.shape[1] // 2 * width // left_panels[0].size
    if (cols, chunks) == (4, 4):
        shards = line_of_four(left_panels, right_panels)
    else:
        gathered = lax.all_gather(left_panels, "col", axis=1, tiled=True)
        lefts = [[[(0, blocked(gathered[a]), None, None)]] for a in range(ORDERS)]
        shards = products(lefts, right_panels, right_panels.shape[1], jnp.zeros((1,), jnp.int32))
    blocks = shards.reshape(-1, ORDERS, shards.shape[2] // height, height, width)
    blocks = jnp.swapaxes(blocks, 1, 2).reshape(rows, ORDERS, height, width)
    return 2.0 * window_tiles - sum_over_row(blocks, rows)


def solution(mesh):
    return jax.shard_map(
        functools.partial(on_device, mesh.shape["col"], mesh.shape["row"]),
        mesh=mesh,
        in_specs=(P(None, "col", "row"), P(None, "row", "col"), P(None, "row", "col")),
        out_specs=P(None, "row", "col"),
        check_vma=False,
    )
```

time: 107 us -> 101 us (0.944)
  waiting for transfers between devices: 34.4 us -> 14 us
  starting transfers between devices: 35.4 us -> 50.3 us
  Pallas kernels: 23.6 us -> 22.5 us
    ppermute x9, waiting for transfers between devices: 30 us -> 9.61 us  [line_of_four(): lax.ppermute(after(array, *earlier), 'col', [(0, 1), (1, 0), (2, 3), (3,...]
    ppermute x9, starting transfers between devices: 24.3 us -> 39.3 us  [line_of_four(): lax.ppermute(after(array, *earlier), 'col', [(0, 1), (1, 0), (2, 3), (3,...]
    pallas_call x9, Pallas kernels: 23.6 us -> 22.5 us  [products(): pl.pallas_call(functools.partial(products_kernel, layout, steps, orders,...]
    unnamed x22 -> x31, local copies, waits for them, and re-layouts: 2.03 us -> 2.68 us
  transfers between devices with their start and end apart: 22 -> 22, of which waited for: 11 -> 10; matrix products, arithmetic and copies ran while one was open for 8% -> 9% of each run, Pallas kernels for 22% -> 22%
where the time goes in v4:
time: 101 us
  starting transfers between devices  50.3 us (50%)
  Pallas kernels  22.5 us (22%)
  waiting for transfers between devices  14 us (14%)
  local copies, waits for them, and re-layouts  9.92 us (10%)
  other arithmetic  3.58 us (4%)
    ppermute x9, starting transfers between devices, line_of_four(): lax.ppermute(after(array, *earlier), 'col', [(0, 1), (1, 0), (2, 3), (3,...  39.3 us
    pallas_call x9, Pallas kernels, products(): pl.pallas_call(functools.partial(products_kernel, layout, steps, orders,...  22.5 us
    ppermute x9, waiting for transfers between devices, line_of_four(): lax.ppermute(after(array, *earlier), 'col', [(0, 1), (1, 0), (2, 3), (3,...  9.61 us
    ppermute x8, starting transfers between devices, line_of_four(): lax.ppermute(after(array, *earlier), 'col', [(1, 2), (2, 1)])  6.1 us
    ppermute x3, starting transfers between devices, sum_over_row(): lax.ppermute(block, 'row', [(i, i ^ 2 * offset) for i in range(8)])  3.55 us
    ppermute x3, waiting for transfers between devices, sum_over_row(): lax.ppermute(block, 'row', [(i, i ^ 2 * offset) for i in range(8)])  3.19 us
    slice x1, local copies, waits for them, and re-layouts, line_of_four(): right[0, half + i * depth:half + (i + 1) * depth].reshape(own0.shape)  2.9 us
    unnamed x31, local copies, waits for them, and re-layouts  2.68 us
  transfers between devices with their start and end apart: 22, of which 10 were waited for; matrix products, arithmetic and copies ran while one was open for 9% of the time, Pallas kernels for 22%

profile of v4, /device:TPU:0, one launch (start us, length us, event | category | flops | bytes accessed | tf_op | source)
XLA Modules:
  0.0 100.7 jit_solution(11632713302138873787)
XLA Ops:
  0.0 1.3 %slice_bitcast_fusion.1 = (f32[2,64,8,128]{3,2,1,0:T(8,128)S(1)}, f32[2,64,8,128]{3,2,1,0:T(8,128)S(1)}) fusion(f32[3,16,8192]{2,1,0:T(8,128)} %param.9), kind=kLoop, calls=%fused_computation.1 | loop fusion | bytes 2097152 | tf_op jit(solution)/shard_map/transpose | solution.py:23
  1.3 3.1 %collective-permute-start = (f32[2,64,8,128]{3,2,1,0:T(8,128)S(1)}, f32[2,64,8,128]{3,2,1,0:T(8,128)}, u32[]{:S(2)}, u32[]{:S(2)}) collective-permute-start(f32[2,64,8,128]{3,2,1,0:T(8,128)S(1)} %get-tuple-element.76.refs_0_), channel_id=1, source_target_pairs={{0,1},{1,0},{2,3},{3,2},{4,5},{5,4},{6,7},{7,6},{8,9},{9,8},{10,11... | collective-permute-start | bytes 1572872 | tf_op jit(solution)/shard_map/ppermute | solution.py:182
  4.4 0.7 collective-permute-start.2
  5.1 4.4 %collective-permute-start.1 = (f32[2,64,8,128]{3,2,1,0:T(8,128)S(1)}, f32[2,64,8,128]{3,2,1,0:T(8,128)S(1)}, u32[]{:S(2)}, u32[]{:S(2)}) collective-permute-start(f32[2,64,8,128]{3,2,1,0:T(8,128)S(1)} %get-tuple-element.75.refs_2_), channel_id=1, source_target_pairs={{0,1},{1,0},{2,3},{3,2},{4,5},{5,4},{6,7},{7,6},{8,9},{9,8},{10,11... | collective-permute-start | bytes 1572872 | tf_op jit(solution)/shard_map/ppermute | solution.py:182
  9.5 0.7 collective-permute-start.4
  10.2 1.9 %slice_bitcast_fusion = f32[16,8192]{1,0:T(8,128)} fusion(f32[3,16,8192]{2,1,0:T(8,128)} %param.9), kind=kLoop, calls=%fused_computation | loop fusion | bytes 1048576 | tf_op jit(solution)/shard_map/squeeze | solution.py:188
  12.1 2.9 %fusion.12 = (f32[1,1024,128]{2,1,0:T(8,128)}, f32[1,1024,128]{2,1,0:T(8,128)}, f32[1,1024,128]{2,1,0:T(8,128)}, f32[1,1024,128]{2,1,0:T(8,128)}) fusion(f32[3,8192,128]{2,1,0:T(8,128)} %refs_1_.1), kind=kLoop, calls=%fused_computation.43 | loop fusion | bytes 4194304 | tf_op jit(solution)/shard_map/slice | solution.py:192
  15.0 1.2 %slice_bitcast_fusion.3 = (f32[2,32,8,128]{3,2,1,0:T(8,128)S(1)}, f32[2,32,8,128]{3,2,1,0:T(8,128)S(1)}) fusion(f32[16,8192]{1,0:T(8,128)} %slice_bitcast_fusion), kind=kLoop, calls=%fused_computation.3 | loop fusion | bytes 1048576 | tf_op jit(solution)/shard_map/transpose | solution.py:23
  16.1 1.1 %collective-permute-done.refs_1_ = f32[2,64,8,128]{3,2,1,0:T(8,128)} collective-permute-done((f32[2,64,8,128]{3,2,1,0:T(8,128)S(1)}, f32[2,64,8,128]{3,2,1,0:T(8,128)}, u32[]{:S(2)}, u32[]{:S(2)}) %collective-permute-start) | collective-permute-done | bytes 524320 | tf_op jit(solution)/shard_map/ppermute | solution.py:182
  17.2 5.0 %collective-permute-start.3 = (f32[2,32,8,128]{3,2,1,0:T(8,128)S(1)}, f32[2,32,8,128]{3,2,1,0:T(8,128)}, u32[]{:S(2)}, u32[]{:S(2)}) collective-permute-start(f32[2,32,8,128]{3,2,1,0:T(8,128)S(1)} %get-tuple-element.57.refs_4_), channel_id=1, source_target_pairs={{0,1},{1,0},{2,3},{3,2},{4,5},{5,4},{6,7},{7,6},{8,9},{9,8},{10,11... | collective-permute-start | bytes 786440 | tf_op jit(solution)/shard_map/ppermute | solution.py:182
  22.2 0.7 collective-permute-start.7
  22.9 1.1 %broadcast_select_fusion.3 = f32[2,64,8,128]{3,2,1,0:T(8,128)S(1)} fusion(f32[2,64,8,128]{3,2,1,0:T(8,128)} %bitcast.87, f32[2,64,8,128]{3,2,1,0:T(8,128)S(1)} %collective-permute-done.2.refs_0_, pred[]{:T(512)S(6)} %or.3), kind=kLoop, calls=%fused_computation.8 | loop fusion | flops 131072 | bytes 1572865 | tf_op jit(solution)/shard_map/jit(_where)/select_n | solution.py:213
  24.0 4.4 %collective-permute-done.1.refs_3_ = f32[2,64,8,128]{3,2,1,0:T(8,128)S(1)} collective-permute-done((f32[2,64,8,128]{3,2,1,0:T(8,128)S(1)}, f32[2,64,8,128]{3,2,1,0:T(8,128)S(1)}, u32[]{:S(2)}, u32[]{:S(2)}) %collective-permute-start.1) | collective-permute-done | bytes 524320 | tf_op jit(solution)/shard_map/ppermute | solution.py:182
  28.4 0.8 copy-done.8
  29.2 4.3 %collective-permute-start.5 = (f32[2,64,8,128]{3,2,1,0:T(8,128)S(1)}, f32[2,64,8,128]{3,2,1,0:T(8,128)S(1)}, u32[]{:S(2)}, u32[]{:S(2)}) collective-permute-start(f32[2,64,8,128]{3,2,1,0:T(8,128)S(1)} %broadcast_select_fusion.3), channel_id=1, source_target_pairs={{0,1},{1,0},{2,3},{3,2},{4,5},{5,4},{6,7},{7,6},{8,9},{9,8},{10,11... | collective-permute-start | bytes 1572872 | tf_op jit(solution)/shard_map/ppermute | solution.py:182
  33.4 0.7 collective-permute-start.10
  34.2 3.4 %collective-permute-start.6 = (f32[2,64,8,128]{3,2,1,0:T(8,128)S(1)}, f32[2,64,8,128]{3,2,1,0:T(8,128)S(1)}, u32[]{:S(2)}, u32[]{:S(2)}) collective-permute-start(f32[2,64,8,128]{3,2,1,0:T(8,128)S(1)} %broadcast_select_fusion.2), channel_id=1, source_target_pairs={{0,1},{1,0},{2,3},{3,2},{4,5},{5,4},{6,7},{7,6},{8,9},{9,8},{10,11... | collective-permute-start | bytes 1572872 | tf_op jit(solution)/shard_map/ppermute | solution.py:182
  37.6 0.7 collective-permute-start.8
  38.3 1.0 %copy-done.9 = f32[2,64,8,128]{3,2,1,0:T(8,128)S(1)} copy-done((f32[2,64,8,128]{3,2,1,0:T(8,128)S(1)}, f32[2,64,8,128]{3,2,1,0:T(8,128)}, u32[]{:S(2)}) %copy-start.9) | copy-done | bytes 524312
  39.3 6.5 %shard_map.37 = f32[2,3,16,128]{3,2,1,0:T(8,128)S(1)} custom-call(s32[1]{0:T(128)} %bitcast.side_ref, f32[2,64,8,128]{3,2,1,0:T(8,128)S(1)} %copy-done.7, f32[2,64,8,128]{3,2,1,0:T(8,128)} %collective-permute-done.refs_1_, f32[2,64,8,128]{3,2,1,0:T(8,128)S(1)} %get-tuple-element.75.refs_2_, f32[2,64,8,128]{3,2,1,0:T(8,128)S(1)} %copy-done.9, ...), custom_call_target="tpu_custom_call" | custom-call | flops 4831838208 | bytes 46399488 | tf_op jit(solution)/shard_map/pallas_call | solution.py:138
  45.8 0.5 collective-permute-done.5.refs_1_
  46.3 0.7 collective-permute-start.11
  47.0 5.7 %collective-permute-start.13 = (f32[2,32,8,128]{3,2,1,0:T(8,128)S(1)}, f32[2,32,8,128]{3,2,1,0:T(8,128)}, u32[]{:S(2)}, u32[]{:S(2)}) collective-permute-start(f32[2,32,8,128]{3,2,1,0:T(8,128)S(1)} %broadcast_select_fusion.4), channel_id=1, source_target_pairs={{0,1},{1,0},{2,3},{3,2},{4,5},{5,4},{6,7},{7,6},{8,9},{9,8},{10,11... | collective-permute-start | bytes 786440 | tf_op jit(solution)/shard_map/ppermute | solution.py:182
  52.8 0.8 broadcast_select_fusion.1
  53.6 3.3 %collective-permute-start.9 = (f32[2,64,8,128]{3,2,1,0:T(8,128)}, f32[2,64,8,128]{3,2,1,0:T(8,128)S(1)}, u32[]{:S(2)}, u32[]{:S(2)}) collective-permute-start(f32[2,64,8,128]{3,2,1,0:T(8,128)} %broadcast_select_fusion.1), channel_id=1, source_target_pairs={{0,1},{1,0},{2,3},{3,2},{4,5},{5,4},{6,7},{7,6},{8,9},{9,8},{10,11... | collective-permute-start | bytes 1572872 | tf_op jit(solution)/shard_map/ppermute | solution.py:182
  56.9 0.6 collective-permute-done.6.refs_3_
  57.5 1.4 %collective-permute-start.12 = (f32[2,32,8,128]{3,2,1,0:T(8,128)}, f32[2,32,8,128]{3,2,1,0:T(8,128)}, u32[]{:S(2)}, u32[]{:S(2)}) collective-permute-start(f32[2,32,8,128]{3,2,1,0:T(8,128)} %collective-permute-done.3.refs_6_), channel_id=1, source_target_pairs={{1,2},{2,1},{5,6},{6,5},{9,10},{10,9},{13,14},{14,13},{17,18},{18,... | collective-permute-start | bytes 786440 | tf_op jit(solution)/shard_map/ppermute | solution.py:183
  58.9 5.1 %shard_map.38 = f32[1,3,16,128]{3,2,1,0:T(8,128)S(1)} custom-call(s32[1]{0:T(128)} %bitcast.side_ref, f32[2,64,8,128]{3,2,1,0:T(8,128)S(1)} %collective-permute-done.2.refs_0_, f32[2,64,8,128]{3,2,1,0:T(8,128)S(1)} %collective-permute-done.5.refs_1_, f32[2,64,8,128]{3,2,1,0:T(8,128)S(1)} %copy-done.3, f32[2,64,8,128]{3,2,1,0:T(8,128)S(1)} %collective-permute-done.6.refs_3_, ...), custom_call_target="tpu_custom_call" | custom-call | flops 2013265920 | bytes 44040192 | tf_op jit(solution)/shard_map/pallas_call | solution.py:138
  64.0 0.7 collective-permute-start.14
  64.7 0.9 broadcast_select_fusion
  65.6 0.8 copy-done
  66.4 6.5 %collective-permute-start.15 = (f32[2,64,8,128]{3,2,1,0:T(8,128)}, f32[2,64,8,128]{3,2,1,0:T(8,128)S(1)}, u32[]{:S(2)}, u32[]{:S(2)}) collective-permute-start(f32[2,64,8,128]{3,2,1,0:T(8,128)} %broadcast_select_fusion), channel_id=1, source_target_pairs={{0,1},{1,0},{2,3},{3,2},{4,5},{5,4},{6,7},{7,6},{8,9},{9,8},{10,11... | collective-permute-start | bytes 1572872 | tf_op jit(solution)/shard_map/ppermute | solution.py:182
  72.9 1.2 %collective-permute-done.9.refs_1_ = f32[2,64,8,128]{3,2,1,0:T(8,128)S(1)} collective-permute-done((f32[2,64,8,128]{3,2,1,0:T(8,128)}, f32[2,64,8,128]{3,2,1,0:T(8,128)S(1)}, u32[]{:S(2)}, u32[]{:S(2)}) %collective-permute-start.9) | collective-permute-done | bytes 524320 | tf_op jit(solution)/shard_map/ppermute | solution.py:182
  74.1 3.6 %collective-permute-start.16 = (f32[2,32,8,128]{3,2,1,0:T(8,128)}, f32[2,32,8,128]{3,2,1,0:T(8,128)S(1)}, u32[]{:S(2)}, u32[]{:S(2)}) collective-permute-start(f32[2,32,8,128]{3,2,1,0:T(8,128)} %collective-permute-done.12.refs_3_), channel_id=1, source_target_pairs={{0,1},{1,0},{2,3},{3,2},{4,5},{5,4},{6,7},{7,6},{8,9},{9,8},{10,11... | collective-permute-start | bytes 786440 | tf_op jit(solution)/shard_map/ppermute | solution.py:182
  77.8 6.3 %shard_map.39 = f32[3,3,16,128]{3,2,1,0:T(8,128)S(1)} custom-call(s32[1]{0:T(128)} %bitcast.side_ref, f32[2,64,8,128]{3,2,1,0:T(8,128)S(1)} %collective-permute-done.8.refs_0_, f32[2,64,8,128]{3,2,1,0:T(8,128)S(1)} %collective-permute-done.9.refs_1_, f32[2,64,8,128]{3,2,1,0:T(8,128)S(1)} %copy-done.1, f32[2,32,8,128]{3,2,1,0:T(8,128)} %collective-permute-done.12.refs_3_, ...), custom_call_target="tpu_custom_call" | custom-call | flops 3221225472 | bytes 47185920 | tf_op jit(solution)/shard_map/pallas_call | solution.py:138
  84.1 1.8 %collective-permute-done.15.refs_0_ = f32[2,64,8,128]{3,2,1,0:T(8,128)S(1)} collective-permute-done((f32[2,64,8,128]{3,2,1,0:T(8,128)}, f32[2,64,8,128]{3,2,1,0:T(8,128)S(1)}, u32[]{:S(2)}, u32[]{:S(2)}) %collective-permute-start.15) | collective-permute-done | bytes 524320 | tf_op jit(solution)/shard_map/ppermute | solution.py:182
  85.9 1.3 %collective-permute-start.17 = (f32[3,16,128]{2,1,0:T(8,128)S(1)}, f32[3,16,128]{2,1,0:T(8,128)S(1)}, u32[]{:S(2)}, u32[]{:S(2)}) collective-permute-start(f32[3,16,128]{2,1,0:T(8,128)S(1)} %fusion.1), channel_id=1, source_target_pairs={{1,0},{2,3},{5,4},{6,7},{9,8},{10,11},{13,12},{14,15},{17,16},{18,... | collective-permute-start | bytes 73736 | tf_op jit(solution)/shard_map/ppermute | solution.py:184
  87.2 3.8 %shard_map.40 = (f32[1,3,16,128]{3,2,1,0:T(8,128)S(1)}, f32[1,4096,128]{2,1,0:T(8,128)S(1)}) custom-call(s32[1]{0:T(128)} %bitcast.side_ref, f32[2,64,8,128]{3,2,1,0:T(8,128)S(1)} %collective-permute-done.15.refs_0_, f32[3,8192,128]{2,1,0:T(8,128)} %refs_1_.1), custom_call_target="tpu_custom_call" | custom-call | flops 805306368 | bytes 26738688 | tf_op jit(solution)/shard_map/pallas_call | solution.py:138
  91.1 0.8 shard_map.41
  92.0 0.1 collective-permute-start.18
  92.1 1.2 %collective-permute-done.18 = f32[4,3,8,128]{3,2,1,0:T(8,128)S(1)} collective-permute-done((f32[4,3,8,128]{3,2,1,0:T(8,128)S(1)}, f32[4,3,8,128]{3,2,1,0:T(8,128)S(1)}, u32[]{:S(2)}, u32[]{:S(2)}) %collective-permute-start.18) | collective-permute-done | bytes 49184 | tf_op jit(solution)/shard_map/ppermute | solution.py:163
  93.4 2.5 %collective-permute-start.19 = (f32[3,8,128]{2,1,0:T(8,128)S(1)}, f32[3,8,128]{2,1,0:T(8,128)S(1)}, u32[]{:S(2)}, u32[]{:S(2)}) collective-permute-start(f32[3,8,128]{2,1,0:T(8,128)S(1)} %get-tuple-element.85), channel_id=1, source_target_pairs={{0,24},{4,28},{8,16},{12,20},{16,8},{20,12},{24,0},{28,4},{1,25},{... | collective-permute-start | bytes 36872 | tf_op jit(solution)/shard_map/ppermute | solution.py:167
  95.9 0.5 collective-permute-start.20
  96.4 0.5 collective-permute-start.21
  96.9 1.1 %collective-permute-done.19 = f32[3,8,128]{2,1,0:T(8,128)S(1)} collective-permute-done((f32[3,8,128]{2,1,0:T(8,128)S(1)}, f32[3,8,128]{2,1,0:T(8,128)S(1)}, u32[]{:S(2)}, u32[]{:S(2)}) %collective-permute-start.19) | collective-permute-done | bytes 12320 | tf_op jit(solution)/shard_map/ppermute | solution.py:167
  98.0 1.6 %collective-permute-done.20 = f32[3,8,128]{2,1,0:T(8,128)S(1)} collective-permute-done((f32[3,8,128]{2,1,0:T(8,128)S(1)}, f32[3,8,128]{2,1,0:T(8,128)S(1)}, u32[]{:S(2)}, u32[]{:S(2)}) %collective-permute-start.20) | collective-permute-done | bytes 12320 | tf_op jit(solution)/shard_map/ppermute | solution.py:167
  99.6 0.5 collective-permute-done.21
  100.1 0.6 fusion.7
  (57 shorter events, 0.3 us)
Async XLA Ops:
  1.3 13.7 %copy-start.6 = (f32[2,64,8,128]{3,2,1,0:T(8,128)}, f32[2,64,8,128]{3,2,1,0:T(8,128)S(1)}, u32[]{:S(2)}) copy-start(f32[2,64,8,128]{3,2,1,0:T(8,128)S(1)} %get-tuple-element.76.refs_0_) | copy-start | bytes 1572868
  1.3 15.9 %collective-permute-start = (f32[2,64,8,128]{3,2,1,0:T(8,128)S(1)}, f32[2,64,8,128]{3,2,1,0:T(8,128)}, u32[]{:S(2)}, u32[]{:S(2)}) collective-permute-start(f32[2,64,8,128]{3,2,1,0:T(8,128)S(1)} %get-tuple-element.76.refs_0_), channel_id=1, source_target_pairs={{0,1},{1,0},{2,3},{3,2},{4,5},{5,4},{6,7},{7,6},{8,9},{9,8},{10,11... | collective-permute-start | bytes 1572872 | tf_op jit(solution)/shard_map/ppermute | solution.py:182
  4.4 12.9 %collective-permute-start.2 = (f32[2,64,8,128]{3,2,1,0:T(8,128)S(1)}, f32[2,64,8,128]{3,2,1,0:T(8,128)S(1)}, u32[]{:S(2)}, u32[]{:S(2)}) collective-permute-start(f32[2,64,8,128]{3,2,1,0:T(8,128)S(1)} %get-tuple-element.76.refs_0_), channel_id=1, source_target_pairs={{1,2},{2,1},{5,6},{6,5},{9,10},{10,9},{13,14},{14,13},{17,18},{18,... | collective-permute-start | bytes 1572872 | tf_op jit(solution)/shard_map/ppermute | solution.py:183
  5.1 23.3 %collective-permute-start.1 = (f32[2,64,8,128]{3,2,1,0:T(8,128)S(1)}, f32[2,64,8,128]{3,2,1,0:T(8,128)S(1)}, u32[]{:S(2)}, u32[]{:S(2)}) collective-permute-start(f32[2,64,8,128]{3,2,1,0:T(8,128)S(1)} %get-tuple-element.75.refs_2_), channel_id=1, source_target_pairs={{0,1},{1,0},{2,3},{3,2},{4,5},{5,4},{6,7},{7,6},{8,9},{9,8},{10,11... | collective-permute-start | bytes 1572872 | tf_op jit(solution)/shard_map/ppermute | solution.py:182
  9.5 19.7 %collective-permute-start.4 = (f32[2,64,8,128]{3,2,1,0:T(8,128)S(1)}, f32[2,64,8,128]{3,2,1,0:T(8,128)S(1)}, u32[]{:S(2)}, u32[]{:S(2)}) collective-permute-start(f32[2,64,8,128]{3,2,1,0:T(8,128)S(1)} %get-tuple-element.75.refs_2_), channel_id=1, source_target_pairs={{1,2},{2,1},{5,6},{6,5},{9,10},{10,9},{13,14},{14,13},{17,18},{18,... | collective-permute-start | bytes 1572872 | tf_op jit(solution)/shard_map/ppermute | solution.py:183
  15.0 19.2 %copy-start.13 = (f32[1,1024,128]{2,1,0:T(8,128)S(1)}, f32[1,1024,128]{2,1,0:T(8,128)}, u32[]{:S(2)}) copy-start(f32[1,1024,128]{2,1,0:T(8,128)} %get-tuple-element.73) | copy-start | bytes 1572868
  15.0 23.3 %copy-start.7 = (f32[2,64,8,128]{3,2,1,0:T(8,128)S(1)}, f32[2,64,8,128]{3,2,1,0:T(8,128)}, u32[]{:S(2)}) copy-start(f32[2,64,8,128]{3,2,1,0:T(8,128)} %copy-done.6) | copy-start | bytes 1572868
  17.2 17.0 %collective-permute-start.3 = (f32[2,32,8,128]{3,2,1,0:T(8,128)S(1)}, f32[2,32,8,128]{3,2,1,0:T(8,128)}, u32[]{:S(2)}, u32[]{:S(2)}) collective-permute-start(f32[2,32,8,128]{3,2,1,0:T(8,128)S(1)} %get-tuple-element.57.refs_4_), channel_id=1, source_target_pairs={{0,1},{1,0},{2,3},{3,2},{4,5},{5,4},{6,7},{7,6},{8,9},{9,8},{10,11... | collective-permute-start | bytes 786440 | tf_op jit(solution)/shard_map/ppermute | solution.py:182
  22.2 15.4 %collective-permute-start.7 = (f32[2,32,8,128]{3,2,1,0:T(8,128)S(1)}, f32[2,32,8,128]{3,2,1,0:T(8,128)S(1)}, u32[]{:S(2)}, u32[]{:S(2)}) collective-permute-start(f32[2,32,8,128]{3,2,1,0:T(8,128)S(1)} %get-tuple-element.57.refs_4_), channel_id=1, source_target_pairs={{1,2},{2,1},{5,6},{6,5},{9,10},{10,9},{13,14},{14,13},{17,18},{18,... | collective-permute-start | bytes 786440 | tf_op jit(solution)/shard_map/ppermute | solution.py:183
  28.4 0.8 copy-start.8
  29.2 5.0 %copy-start.2 = (f32[2,64,8,128]{3,2,1,0:T(8,128)}, f32[2,64,8,128]{3,2,1,0:T(8,128)S(1)}, u32[]{:S(2)}) copy-start(f32[2,64,8,128]{3,2,1,0:T(8,128)S(1)} %collective-permute-done.4.refs_2_) | copy-start | bytes 1572868
  29.2 17.1 %collective-permute-start.5 = (f32[2,64,8,128]{3,2,1,0:T(8,128)S(1)}, f32[2,64,8,128]{3,2,1,0:T(8,128)S(1)}, u32[]{:S(2)}, u32[]{:S(2)}) collective-permute-start(f32[2,64,8,128]{3,2,1,0:T(8,128)S(1)} %broadcast_select_fusion.3), channel_id=1, source_target_pairs={{0,1},{1,0},{2,3},{3,2},{4,5},{5,4},{6,7},{7,6},{8,9},{9,8},{10,11... | collective-permute-start | bytes 1572872 | tf_op jit(solution)/shard_map/ppermute | solution.py:182
  33.4 12.4 %collective-permute-start.10 = (f32[2,32,8,128]{3,2,1,0:T(8,128)S(1)}, f32[2,32,8,128]{3,2,1,0:T(8,128)S(1)}, u32[]{:S(2)}, u32[]{:S(2)}) collective-permute-start(f32[2,32,8,128]{3,2,1,0:T(8,128)S(1)} %get-tuple-element.61.refs_5_.refs_0_), channel_id=1, source_target_pairs={{1,2},{2,1},{5,6},{6,5},{9,10},{10,9},{13,14},{14,13},{17,18},{18,... | collective-permute-start | bytes 786440 | tf_op jit(solution)/shard_map/ppermute | solution.py:183
  34.2 23.3 %collective-permute-start.6 = (f32[2,64,8,128]{3,2,1,0:T(8,128)S(1)}, f32[2,64,8,128]{3,2,1,0:T(8,128)S(1)}, u32[]{:S(2)}, u32[]{:S(2)}) collective-permute-start(f32[2,64,8,128]{3,2,1,0:T(8,128)S(1)} %broadcast_select_fusion.2), channel_id=1, source_target_pairs={{0,1},{1,0},{2,3},{3,2},{4,5},{5,4},{6,7},{7,6},{8,9},{9,8},{10,11... | collective-permute-start | bytes 1572872 | tf_op jit(solution)/shard_map/ppermute | solution.py:182
  37.6 9.4 %copy-start.4 = (f32[2,32,8,128]{3,2,1,0:T(8,128)}, f32[2,32,8,128]{3,2,1,0:T(8,128)S(1)}, u32[]{:S(2)}) copy-start(f32[2,32,8,128]{3,2,1,0:T(8,128)S(1)} %collective-permute-done.7.refs_5_) | copy-start | bytes 786436
  37.6 15.2 %collective-permute-start.8 = (f32[2,64,8,128]{3,2,1,0:T(8,128)}, f32[2,64,8,128]{3,2,1,0:T(8,128)S(1)}, u32[]{:S(2)}, u32[]{:S(2)}) collective-permute-start(f32[2,64,8,128]{3,2,1,0:T(8,128)} %collective-permute-done.refs_1_), channel_id=1, source_target_pairs={{1,2},{2,1},{5,6},{6,5},{9,10},{10,9},{13,14},{14,13},{17,18},{18,... | collective-permute-start | bytes 1572872 | tf_op jit(solution)/shard_map/ppermute | solution.py:183
  38.3 1.0 %copy-start.9 = (f32[2,64,8,128]{3,2,1,0:T(8,128)S(1)}, f32[2,64,8,128]{3,2,1,0:T(8,128)}, u32[]{:S(2)}) copy-start(f32[2,64,8,128]{3,2,1,0:T(8,128)} %copy-done.8) | copy-start | bytes 1572868
  39.3 7.7 %copy-start.10 = (f32[16,8192]{1,0:T(8,128)S(1)}, f32[16,8192]{1,0:T(8,128)}, u32[]{:S(2)}) copy-start(f32[16,8192]{1,0:T(8,128)} %slice_bitcast_fusion) | copy-start | bytes 1572868
  39.3 13.4 %copy-start.12 = (f32[1,1024,128]{2,1,0:T(8,128)S(1)}, f32[1,1024,128]{2,1,0:T(8,128)}, u32[]{:S(2)}) copy-start(f32[1,1024,128]{2,1,0:T(8,128)} %get-tuple-element.72) | copy-start | bytes 1572868
  45.8 13.1 %copy-start.3 = (f32[2,64,8,128]{3,2,1,0:T(8,128)S(1)}, f32[2,64,8,128]{3,2,1,0:T(8,128)}, u32[]{:S(2)}) copy-start(f32[2,64,8,128]{3,2,1,0:T(8,128)} %copy-done.2) | copy-start | bytes 1572868
  46.3 17.8 %collective-permute-start.11 = (f32[2,64,8,128]{3,2,1,0:T(8,128)S(1)}, f32[2,64,8,128]{3,2,1,0:T(8,128)S(1)}, u32[]{:S(2)}, u32[]{:S(2)}) collective-permute-start(f32[2,64,8,128]{3,2,1,0:T(8,128)S(1)} %copy-done.9), channel_id=1, source_target_pairs={{1,2},{2,1},{5,6},{6,5},{9,10},{10,9},{13,14},{14,13},{17,18},{18,... | collective-permute-start | bytes 1572872 | tf_op jit(solution)/shard_map/ppermute | solution.py:183
  47.0 17.0 %collective-permute-start.13 = (f32[2,32,8,128]{3,2,1,0:T(8,128)S(1)}, f32[2,32,8,128]{3,2,1,0:T(8,128)}, u32[]{:S(2)}, u32[]{:S(2)}) collective-permute-start(f32[2,32,8,128]{3,2,1,0:T(8,128)S(1)} %broadcast_select_fusion.4), channel_id=1, source_target_pairs={{0,1},{1,0},{2,3},{3,2},{4,5},{5,4},{6,7},{7,6},{8,9},{9,8},{10,11... | collective-permute-start | bytes 786440 | tf_op jit(solution)/shard_map/ppermute | solution.py:182
  53.6 11.1 %copy-start.11 = (f32[1,1024,128]{2,1,0:T(8,128)S(1)}, f32[1,1024,128]{2,1,0:T(8,128)}, u32[]{:S(2)}) copy-start(f32[1,1024,128]{2,1,0:T(8,128)} %get-tuple-element.71) | copy-start | bytes 1572868
  53.6 20.5 %collective-permute-start.9 = (f32[2,64,8,128]{3,2,1,0:T(8,128)}, f32[2,64,8,128]{3,2,1,0:T(8,128)S(1)}, u32[]{:S(2)}, u32[]{:S(2)}) collective-permute-start(f32[2,64,8,128]{3,2,1,0:T(8,128)} %broadcast_select_fusion.1), channel_id=1, source_target_pairs={{0,1},{1,0},{2,3},{3,2},{4,5},{5,4},{6,7},{7,6},{8,9},{9,8},{10,11... | collective-permute-start | bytes 1572872 | tf_op jit(solution)/shard_map/ppermute | solution.py:182
  57.5 15.4 %collective-permute-start.12 = (f32[2,32,8,128]{3,2,1,0:T(8,128)}, f32[2,32,8,128]{3,2,1,0:T(8,128)}, u32[]{:S(2)}, u32[]{:S(2)}) collective-permute-start(f32[2,32,8,128]{3,2,1,0:T(8,128)} %collective-permute-done.3.refs_6_), channel_id=1, source_target_pairs={{1,2},{2,1},{5,6},{6,5},{9,10},{10,9},{13,14},{14,13},{17,18},{18,... | collective-permute-start | bytes 786440 | tf_op jit(solution)/shard_map/ppermute | solution.py:183
  64.0 8.9 %collective-permute-start.14 = (f32[2,32,8,128]{3,2,1,0:T(8,128)}, f32[2,32,8,128]{3,2,1,0:T(8,128)S(1)}, u32[]{:S(2)}, u32[]{:S(2)}) collective-permute-start(f32[2,32,8,128]{3,2,1,0:T(8,128)} %collective-permute-done.13.refs_6_.refs_8_), channel_id=1, source_target_pairs={{1,2},{2,1},{5,6},{6,5},{9,10},{10,9},{13,14},{14,13},{17,18},{18,... | collective-permute-start | bytes 786440 | tf_op jit(solution)/shard_map/ppermute | solution.py:183
  65.6 0.8 copy-start
  66.4 19.5 %collective-permute-start.15 = (f32[2,64,8,128]{3,2,1,0:T(8,128)}, f32[2,64,8,128]{3,2,1,0:T(8,128)S(1)}, u32[]{:S(2)}, u32[]{:S(2)}) collective-permute-start(f32[2,64,8,128]{3,2,1,0:T(8,128)} %broadcast_select_fusion), channel_id=1, source_target_pairs={{0,1},{1,0},{2,3},{3,2},{4,5},{5,4},{6,7},{7,6},{8,9},{9,8},{10,11... | collective-permute-start | bytes 1572872 | tf_op jit(solution)/shard_map/ppermute | solution.py:182
  72.9 4.9 %copy-start.1 = (f32[2,64,8,128]{3,2,1,0:T(8,128)S(1)}, f32[2,64,8,128]{3,2,1,0:T(8,128)}, u32[]{:S(2)}) copy-start(f32[2,64,8,128]{3,2,1,0:T(8,128)} %copy-done) | copy-start | bytes 1572868
  72.9 4.9 %copy-start.5 = (f32[2,32,8,128]{3,2,1,0:T(8,128)S(1)}, f32[2,32,8,128]{3,2,1,0:T(8,128)}, u32[]{:S(2)}) copy-start(f32[2,32,8,128]{3,2,1,0:T(8,128)} %copy-done.4) | copy-start | bytes 786436
  74.1 16.9 %collective-permute-start.16 = (f32[2,32,8,128]{3,2,1,0:T(8,128)}, f32[2,32,8,128]{3,2,1,0:T(8,128)S(1)}, u32[]{:S(2)}, u32[]{:S(2)}) collective-permute-start(f32[2,32,8,128]{3,2,1,0:T(8,128)} %collective-permute-done.12.refs_3_), channel_id=1, source_target_pairs={{0,1},{1,0},{2,3},{3,2},{4,5},{5,4},{6,7},{7,6},{8,9},{9,8},{10,11... | collective-permute-start | bytes 786440 | tf_op jit(solution)/shard_map/ppermute | solution.py:182
  85.9 6.0 %collective-permute-start.17 = (f32[3,16,128]{2,1,0:T(8,128)S(1)}, f32[3,16,128]{2,1,0:T(8,128)S(1)}, u32[]{:S(2)}, u32[]{:S(2)}) collective-permute-start(f32[3,16,128]{2,1,0:T(8,128)S(1)} %fusion.1), channel_id=1, source_target_pairs={{1,0},{2,3},{5,4},{6,7},{9,8},{10,11},{13,12},{14,15},{17,16},{18,... | collective-permute-start | bytes 73736 | tf_op jit(solution)/shard_map/ppermute | solution.py:184
  91.0 9.1 %copy-start.14 = (f32[3,8,128]{2,1,0:T(8,128)S(1)}, f32[3,8,128]{2,1,0:T(8,128)}, u32[]{:S(2)}) copy-start(f32[3,8,128]{2,1,0:T(8,128)} %param.11) | copy-start | bytes 36868
  92.0 1.3 %collective-permute-start.18 = (f32[4,3,8,128]{3,2,1,0:T(8,128)S(1)}, f32[4,3,8,128]{3,2,1,0:T(8,128)S(1)}, u32[]{:S(2)}, u32[]{:S(2)}) collective-permute-start(f32[4,3,8,128]{3,2,1,0:T(8,128)S(1)} %bitcast.88), channel_id=1, source_target_pairs={{0,4},{4,0},{8,12},{12,8},{16,20},{20,16},{24,28},{28,24},{1,5},{5... | collective-permute-start | bytes 147464 | tf_op jit(solution)/shard_map/ppermute | solution.py:163
  93.4 4.7 %collective-permute-start.19 = (f32[3,8,128]{2,1,0:T(8,128)S(1)}, f32[3,8,128]{2,1,0:T(8,128)S(1)}, u32[]{:S(2)}, u32[]{:S(2)}) collective-permute-start(f32[3,8,128]{2,1,0:T(8,128)S(1)} %get-tuple-element.85), channel_id=1, source_target_pairs={{0,24},{4,28},{8,16},{12,20},{16,8},{20,12},{24,0},{28,4},{1,25},{... | collective-permute-start | bytes 36872 | tf_op jit(solution)/shard_map/ppermute | solution.py:167
  95.9 3.7 %collective-permute-start.20 = (f32[3,8,128]{2,1,0:T(8,128)S(1)}, f32[3,8,128]{2,1,0:T(8,128)S(1)}, u32[]{:S(2)}, u32[]{:S(2)}) collective-permute-start(f32[3,8,128]{2,1,0:T(8,128)S(1)} %get-tuple-element.87), channel_id=1, source_target_pairs={{0,8},{4,12},{8,0},{12,4},{16,24},{20,28},{24,16},{28,20},{1,9},{5... | collective-permute-start | bytes 36872 | tf_op jit(solution)/shard_map/ppermute | solution.py:167
  96.4 3.7 %collective-permute-start.21 = (f32[3,8,128]{2,1,0:T(8,128)S(1)}, f32[3,8,128]{2,1,0:T(8,128)S(1)}, u32[]{:S(2)}, u32[]{:S(2)}) collective-permute-start(f32[3,8,128]{2,1,0:T(8,128)S(1)} %get-tuple-element.86), channel_id=1, source_target_pairs={{0,16},{4,20},{8,24},{12,28},{16,0},{20,4},{24,8},{28,12},{1,17},{... | collective-permute-start | bytes 36872 | tf_op jit(solution)/shard_map/ppermute | solution.py:167

commit v5 on v4

--- a/solution.py
+++ b/solution.py
@@ -152,24 +152,24 @@
     )(side, *[term[1] for term in flat], right)
 
 
+def after(array, *earlier):
+    return lax.optimization_barrier((array, *earlier))[0]
+
+
 def sum_over_row(blocks, row_size):
     if row_size != 8:
         return lax.psum_scatter(blocks, "row", scatter_dimension=0, tiled=True)[0]
     me = lax.axis_index("row")
     pairs = blocks.reshape((4, 2) + blocks.shape[1:])
     core, chip = me % 2, me // 2
-    keep = lax.dynamic_index_in_dim(pairs, core, 1, False)
-    give = lax.dynamic_index_in_dim(pairs, 1 - core, 1, False)
-    mine = keep + lax.ppermute(give, "row", [(i, i ^ 1) for i in range(8)])
-    total = lax.dynamic_index_in_dim(mine, chip, 0, False)
-    for offset in (3, 1, 2):
-        block = lax.dynamic_index_in_dim(mine, chip ^ offset, 0, False)
-        total = total + lax.ppermute(block, "row", [(i, i ^ (2 * offset)) for i in range(8)])
-    return total
-
-
-def after(array, *earlier):
-    return lax.optimization_barrier((array, *earlier))[0]
+    to = lambda array, offset: lax.ppermute(array, "row", [(i, i ^ offset) for i in range(8)])
+    pick = lambda array, index, axis=0: lax.dynamic_index_in_dim(array, index, axis, False)
+    mine = pick(pairs, core, 1) + to(pick(pairs, 1 - core, 1), 1)
+    early = to(pick(pairs, chip ^ 1), 2)
+    one = to(pick(mine, chip ^ 2), 4)
+    two = to(pick(mine, chip ^ 3), 6)
+    early = after(early, two)
+    return pick(mine, chip) + one + two + pick(early, core) + to(pick(early, 1 - core), 1)
 
 
 END, INNER = 1, 0
@@ -184,9 +184,9 @@
     outward = lambda array: lax.ppermute(array, "col", [(1, 0), (2, 3)])
     extent = left.shape[2]
     half = extent // 2
-    own0, own1 = blocked(left[0]), blocked(left[1])
-    left2 = after(left, own0, own1)[2]
-    own2, own3 = blocked(left2[:, :half]), blocked(left2[:, half:])
+    own0 = blocked(left[0])
+    left1 = after(left, own0)
+    own1, own2, own3 = blocked(left1[1]), blocked(left1[2, :, :half]), blocked(left1[2, :, half:])
     width = right.shape[2]
     depth = own0.size // width
     chunk = lambda i: right[0, half + i * depth : half + (i + 1) * depth].reshape(own0.shape)

time: 101 us -> 101 us (level)
  local copies, waits for them, and re-layouts: 9.92 us -> 7.88 us
  other arithmetic: 3.58 us -> 4.61 us
    squeeze x2 -> x3, local copies, waits for them, and re-layouts: 1.88 us -> 0.03 us  [sum_over_row(): lax.dynamic_index_in_dim(array, index, axis, False)]
    ppermute x9, waiting for transfers between devices: 9.61 us -> 11.2 us  [line_of_four(): lax.ppermute(after(array, *earlier), 'col', [(0, 1), (1, 0), (2, 3), (3,...]
    ppermute x4 -> x5, waiting for transfers between devices: 4.38 us -> 3.19 us  [sum_over_row(): lax.ppermute(array, 'row', [(i, i ^ offset) for i in range(8)])]
    unnamed x31 -> x29, local copies, waits for them, and re-layouts: 2.68 us -> 1.64 us
    transpose x2 -> x3, local copies, waits for them, and re-layouts: 2.42 us -> 3.28 us  [blocked(): left.reshape(height // SUBLANES, SUBLANES, extent // LANES, LANES)]
    ppermute x4 -> x5, starting transfers between devices: 3.62 us -> 4.28 us  [sum_over_row(): lax.ppermute(array, 'row', [(i, i ^ offset) for i in range(8)])]
  transfers between devices with their start and end apart: 22 -> 23, of which waited for: 10 -> 8; matrix products, arithmetic and copies ran while one was open for 9% -> 9% of each run, Pallas kernels for 22% -> 22%
where the time goes in v5:
time: 101 us; the launch traced here: 100 us
  starting transfers between devices  50.2 us (50%)
  Pallas kernels  22.5 us (22%)
  waiting for transfers between devices  14.4 us (14%)
  local copies, waits for them, and re-layouts  7.88 us (8%)
  other arithmetic  4.61 us (5%)
    ppermute x9, starting transfers between devices, line_of_four(): lax.ppermute(after(array, *earlier), 'col', [(0, 1), (1, 0), (2, 3), (3,...  38.5 us
    pallas_call x9, Pallas kernels, products(): pl.pallas_call(functools.partial(products_kernel, layout, steps, orders,...  22.5 us
    ppermute x9, waiting for transfers between devices, line_of_four(): lax.ppermute(after(array, *earlier), 'col', [(0, 1), (1, 0), (2, 3), (3,...  11.2 us
    ppermute x8, starting transfers between devices, line_of_four(): lax.ppermute(after(array, *earlier), 'col', [(1, 2), (2, 1)])  6.1 us
    ppermute x5, starting transfers between devices, sum_over_row(): lax.ppermute(array, 'row', [(i, i ^ offset) for i in range(8)])  4.28 us
    transpose x3, local copies, waits for them, and re-layouts, blocked(): left.reshape(height // SUBLANES, SUBLANES, extent // LANES, LANES)  3.28 us
    ppermute x5, waiting for transfers between devices, sum_over_row(): lax.ppermute(array, 'row', [(i, i ^ offset) for i in range(8)])  3.19 us
    slice x1, local copies, waits for them, and re-layouts, line_of_four(): right[0, half + i * depth:half + (i + 1) * depth].reshape(own0.shape)  2.89 us
  transfers between devices with their start and end apart: 23, of which 8 were waited for; matrix products, arithmetic and copies ran while one was open for 9% of the time, Pallas kernels for 22%

profile of v5, /device:TPU:0, one launch (start us, length us, event | category | flops | bytes accessed | tf_op | source)
XLA Modules:
  0.0 100.0 jit_solution(2282370766539438525)
XLA Ops:
  0.0 1.1 %slice_bitcast_fusion.1.refs_0_ = f32[2,64,8,128]{3,2,1,0:T(8,128)S(1)} fusion(f32[3,16,8192]{2,1,0:T(8,128)} %param.9), kind=kLoop, calls=%fused_computation.1 | loop fusion | bytes 1048576 | tf_op jit(solution)/shard_map/transpose | solution.py:23
  1.1 3.1 %collective-permute-start = (f32[2,64,8,128]{3,2,1,0:T(8,128)S(1)}, f32[2,64,8,128]{3,2,1,0:T(8,128)}, u32[]{:S(2)}, u32[]{:S(2)}) collective-permute-start(f32[2,64,8,128]{3,2,1,0:T(8,128)S(1)} %slice_bitcast_fusion.1.refs_0_), channel_id=1, source_target_pairs={{0,1},{1,0},{2,3},{3,2},{4,5},{5,4},{6,7},{7,6},{8,9},{9,8},{10,11... | collective-permute-start | bytes 1572872 | tf_op jit(solution)/shard_map/ppermute | solution.py:182
  4.2 0.7 collective-permute-start.2
  4.9 1.1 %slice_bitcast_fusion.refs_2_ = f32[2,64,8,128]{3,2,1,0:T(8,128)S(1)} fusion(f32[3,16,8192]{2,1,0:T(8,128)} %param.9), kind=kLoop, calls=%fused_computation | loop fusion | bytes 1048576 | tf_op jit(solution)/shard_map/transpose | solution.py:23
  6.0 4.4 %collective-permute-start.1 = (f32[2,64,8,128]{3,2,1,0:T(8,128)S(1)}, f32[2,64,8,128]{3,2,1,0:T(8,128)S(1)}, u32[]{:S(2)}, u32[]{:S(2)}) collective-permute-start(f32[2,64,8,128]{3,2,1,0:T(8,128)S(1)} %slice_bitcast_fusion.refs_2_), channel_id=1, source_target_pairs={{0,1},{1,0},{2,3},{3,2},{4,5},{5,4},{6,7},{7,6},{8,9},{9,8},{10,11... | collective-permute-start | bytes 1572872 | tf_op jit(solution)/shard_map/ppermute | solution.py:182
  10.4 0.7 collective-permute-start.4
  11.1 2.9 %fusion.12 = (f32[1,1024,128]{2,1,0:T(8,128)}, f32[1,1024,128]{2,1,0:T(8,128)}, f32[1,1024,128]{2,1,0:T(8,128)}, f32[1,1024,128]{2,1,0:T(8,128)}) fusion(f32[3,8192,128]{2,1,0:T(8,128)} %refs_1_.1), kind=kLoop, calls=%fused_computation.44 | loop fusion | bytes 4194304 | tf_op jit(solution)/shard_map/slice | solution.py:192
  14.0 1.1 %slice_bitcast_fusion.2 = (f32[2,32,8,128]{3,2,1,0:T(8,128)S(1)}, f32[2,32,8,128]{3,2,1,0:T(8,128)S(1)}) fusion(f32[3,16,8192]{2,1,0:T(8,128)} %param.9), kind=kLoop, calls=%fused_computation.2 | loop fusion | bytes 1048576 | tf_op jit(solution)/shard_map/transpose | solution.py:23
  15.1 1.9 %collective-permute-done.refs_1_ = f32[2,64,8,128]{3,2,1,0:T(8,128)} collective-permute-done((f32[2,64,8,128]{3,2,1,0:T(8,128)S(1)}, f32[2,64,8,128]{3,2,1,0:T(8,128)}, u32[]{:S(2)}, u32[]{:S(2)}) %collective-permute-start) | collective-permute-done | bytes 524320 | tf_op jit(solution)/shard_map/ppermute | solution.py:182
  17.0 5.0 %collective-permute-start.3 = (f32[2,32,8,128]{3,2,1,0:T(8,128)S(1)}, f32[2,32,8,128]{3,2,1,0:T(8,128)}, u32[]{:S(2)}, u32[]{:S(2)}) collective-permute-start(f32[2,32,8,128]{3,2,1,0:T(8,128)S(1)} %get-tuple-element.58.refs_4_), channel_id=1, source_target_pairs={{0,1},{1,0},{2,3},{3,2},{4,5},{5,4},{6,7},{7,6},{8,9},{9,8},{10,11... | collective-permute-start | bytes 786440 | tf_op jit(solution)/shard_map/ppermute | solution.py:182
  22.0 0.7 collective-permute-start.7
  22.7 1.2 %broadcast_select_fusion.3 = f32[2,64,8,128]{3,2,1,0:T(8,128)S(1)} fusion(f32[2,64,8,128]{3,2,1,0:T(8,128)} %bitcast.93, f32[2,64,8,128]{3,2,1,0:T(8,128)S(1)} %collective-permute-done.2.refs_0_, pred[]{:T(512)S(6)} %or.3), kind=kLoop, calls=%fused_computation.7 | loop fusion | flops 131072 | bytes 1572865 | tf_op jit(solution)/shard_map/jit(_where)/select_n | solution.py:213
  23.9 4.3 %collective-permute-done.1.refs_3_ = f32[2,64,8,128]{3,2,1,0:T(8,128)S(1)} collective-permute-done((f32[2,64,8,128]{3,2,1,0:T(8,128)S(1)}, f32[2,64,8,128]{3,2,1,0:T(8,128)S(1)}, u32[]{:S(2)}, u32[]{:S(2)}) %collective-permute-start.1) | collective-permute-done | bytes 524320 | tf_op jit(solution)/shard_map/ppermute | solution.py:182
  28.2 0.8 copy-done.8
  29.0 4.3 %collective-permute-start.5 = (f32[2,64,8,128]{3,2,1,0:T(8,128)S(1)}, f32[2,64,8,128]{3,2,1,0:T(8,128)S(1)}, u32[]{:S(2)}, u32[]{:S(2)}) collective-permute-start(f32[2,64,8,128]{3,2,1,0:T(8,128)S(1)} %broadcast_select_fusion.3), channel_id=1, source_target_pairs={{0,1},{1,0},{2,3},{3,2},{4,5},{5,4},{6,7},{7,6},{8,9},{9,8},{10,11... | collective-permute-start | bytes 1572872 | tf_op jit(solution)/shard_map/ppermute | solution.py:182
  33.2 0.7 collective-permute-start.10
  33.9 0.1 broadcast_select_fusion.2
  34.0 3.5 %collective-permute-start.6 = (f32[2,64,8,128]{3,2,1,0:T(8,128)S(1)}, f32[2,64,8,128]{3,2,1,0:T(8,128)S(1)}, u32[]{:S(2)}, u32[]{:S(2)}) collective-permute-start(f32[2,64,8,128]{3,2,1,0:T(8,128)S(1)} %broadcast_select_fusion.2), channel_id=1, source_target_pairs={{0,1},{1,0},{2,3},{3,2},{4,5},{5,4},{6,7},{7,6},{8,9},{9,8},{10,11... | collective-permute-start | bytes 1572872 | tf_op jit(solution)/shard_map/ppermute | solution.py:182
  37.5 0.7 collective-permute-start.8
  38.2 6.4 %shard_map.37 = f32[2,3,16,128]{3,2,1,0:T(8,128)S(1)} custom-call(s32[1]{0:T(128)} %bitcast.side_ref, f32[2,64,8,128]{3,2,1,0:T(8,128)S(1)} %slice_bitcast_fusion.1.refs_0_, f32[2,64,8,128]{3,2,1,0:T(8,128)} %collective-permute-done.refs_1_, f32[2,64,8,128]{3,2,1,0:T(8,128)S(1)} %copy-done.7, f32[2,64,8,128]{3,2,1,0:T(8,128)S(1)} %copy-done.9, ...), custom_call_target="tpu_custom_call" | custom-call | flops 4831838208 | bytes 46399488 | tf_op jit(solution)/shard_map/pallas_call | solution.py:138
  44.7 1.4 %collective-permute-done.5.refs_1_ = f32[2,64,8,128]{3,2,1,0:T(8,128)S(1)} collective-permute-done((f32[2,64,8,128]{3,2,1,0:T(8,128)S(1)}, f32[2,64,8,128]{3,2,1,0:T(8,128)S(1)}, u32[]{:S(2)}, u32[]{:S(2)}) %collective-permute-start.5) | collective-permute-done | bytes 524320 | tf_op jit(solution)/shard_map/ppermute | solution.py:182
  46.1 0.7 collective-permute-start.11
  46.8 1.0 broadcast_select_fusion.4
  47.8 5.4 %collective-permute-start.13 = (f32[2,32,8,128]{3,2,1,0:T(8,128)S(1)}, f32[2,32,8,128]{3,2,1,0:T(8,128)}, u32[]{:S(2)}, u32[]{:S(2)}) collective-permute-start(f32[2,32,8,128]{3,2,1,0:T(8,128)S(1)} %broadcast_select_fusion.4), channel_id=1, source_target_pairs={{0,1},{1,0},{2,3},{3,2},{4,5},{5,4},{6,7},{7,6},{8,9},{9,8},{10,11... | collective-permute-start | bytes 786440 | tf_op jit(solution)/shard_map/ppermute | solution.py:182
  53.1 0.8 broadcast_select_fusion.1
  54.0 2.7 %collective-permute-start.9 = (f32[2,64,8,128]{3,2,1,0:T(8,128)}, f32[2,64,8,128]{3,2,1,0:T(8,128)S(1)}, u32[]{:S(2)}, u32[]{:S(2)}) collective-permute-start(f32[2,64,8,128]{3,2,1,0:T(8,128)} %broadcast_select_fusion.1), channel_id=1, source_target_pairs={{0,1},{1,0},{2,3},{3,2},{4,5},{5,4},{6,7},{7,6},{8,9},{9,8},{10,11... | collective-permute-start | bytes 1572872 | tf_op jit(solution)/shard_map/ppermute | solution.py:182
  56.7 0.6 collective-permute-done.6.refs_3_
  57.3 1.4 %collective-permute-start.12 = (f32[2,32,8,128]{3,2,1,0:T(8,128)}, f32[2,32,8,128]{3,2,1,0:T(8,128)}, u32[]{:S(2)}, u32[]{:S(2)}) collective-permute-start(f32[2,32,8,128]{3,2,1,0:T(8,128)} %collective-permute-done.3.refs_6_), channel_id=1, source_target_pairs={{1,2},{2,1},{5,6},{6,5},{9,10},{10,9},{13,14},{14,13},{17,18},{18,... | collective-permute-start | bytes 786440 | tf_op jit(solution)/shard_map/ppermute | solution.py:183
  58.7 5.1 %shard_map.38 = f32[1,3,16,128]{3,2,1,0:T(8,128)S(1)} custom-call(s32[1]{0:T(128)} %bitcast.side_ref, f32[2,64,8,128]{3,2,1,0:T(8,128)S(1)} %collective-permute-done.2.refs_0_, f32[2,64,8,128]{3,2,1,0:T(8,128)S(1)} %collective-permute-done.5.refs_1_, f32[2,64,8,128]{3,2,1,0:T(8,128)S(1)} %copy-done.3, f32[2,64,8,128]{3,2,1,0:T(8,128)S(1)} %collective-permute-done.6.refs_3_, ...), custom_call_target="tpu_custom_call" | custom-call | flops 2013265920 | bytes 44040192 | tf_op jit(solution)/shard_map/pallas_call | solution.py:138
  63.8 0.7 collective-permute-start.14
  64.5 0.9 broadcast_select_fusion
  65.4 0.8 copy-done
  66.2 6.5 %collective-permute-start.15 = (f32[2,64,8,128]{3,2,1,0:T(8,128)}, f32[2,64,8,128]{3,2,1,0:T(8,128)S(1)}, u32[]{:S(2)}, u32[]{:S(2)}) collective-permute-start(f32[2,64,8,128]{3,2,1,0:T(8,128)} %broadcast_select_fusion), channel_id=1, source_target_pairs={{0,1},{1,0},{2,3},{3,2},{4,5},{5,4},{6,7},{7,6},{8,9},{9,8},{10,11... | collective-permute-start | bytes 1572872 | tf_op jit(solution)/shard_map/ppermute | solution.py:182
  72.8 1.1 %collective-permute-done.9.refs_1_ = f32[2,64,8,128]{3,2,1,0:T(8,128)S(1)} collective-permute-done((f32[2,64,8,128]{3,2,1,0:T(8,128)}, f32[2,64,8,128]{3,2,1,0:T(8,128)S(1)}, u32[]{:S(2)}, u32[]{:S(2)}) %collective-permute-start.9) | collective-permute-done | bytes 524320 | tf_op jit(solution)/shard_map/ppermute | solution.py:182
  73.9 3.7 %collective-permute-start.16 = (f32[2,32,8,128]{3,2,1,0:T(8,128)}, f32[2,32,8,128]{3,2,1,0:T(8,128)S(1)}, u32[]{:S(2)}, u32[]{:S(2)}) collective-permute-start(f32[2,32,8,128]{3,2,1,0:T(8,128)} %collective-permute-done.12.refs_3_), channel_id=1, source_target_pairs={{0,1},{1,0},{2,3},{3,2},{4,5},{5,4},{6,7},{7,6},{8,9},{9,8},{10,11... | collective-permute-start | bytes 786440 | tf_op jit(solution)/shard_map/ppermute | solution.py:182
  77.6 6.3 %shard_map.39 = f32[3,3,16,128]{3,2,1,0:T(8,128)S(1)} custom-call(s32[1]{0:T(128)} %bitcast.side_ref, f32[2,64,8,128]{3,2,1,0:T(8,128)S(1)} %collective-permute-done.8.refs_0_, f32[2,64,8,128]{3,2,1,0:T(8,128)S(1)} %collective-permute-done.9.refs_1_, f32[2,64,8,128]{3,2,1,0:T(8,128)S(1)} %copy-done.1, f32[2,32,8,128]{3,2,1,0:T(8,128)} %collective-permute-done.12.refs_3_, ...), custom_call_target="tpu_custom_call" | custom-call | flops 3221225472 | bytes 47185920 | tf_op jit(solution)/shard_map/pallas_call | solution.py:138
  83.9 1.8 %collective-permute-done.15.refs_0_ = f32[2,64,8,128]{3,2,1,0:T(8,128)S(1)} collective-permute-done((f32[2,64,8,128]{3,2,1,0:T(8,128)}, f32[2,64,8,128]{3,2,1,0:T(8,128)S(1)}, u32[]{:S(2)}, u32[]{:S(2)}) %collective-permute-start.15) | collective-permute-done | bytes 524320 | tf_op jit(solution)/shard_map/ppermute | solution.py:182
  85.8 1.3 %collective-permute-start.17 = (f32[3,16,128]{2,1,0:T(8,128)S(1)}, f32[3,16,128]{2,1,0:T(8,128)S(1)}, u32[]{:S(2)}, u32[]{:S(2)}) collective-permute-start(f32[3,16,128]{2,1,0:T(8,128)S(1)} %fusion.1), channel_id=1, source_target_pairs={{1,0},{2,3},{5,4},{6,7},{9,8},{10,11},{13,12},{14,15},{17,16},{18,... | collective-permute-start | bytes 73736 | tf_op jit(solution)/shard_map/ppermute | solution.py:184
  87.1 3.8 %shard_map.40 = (f32[1,3,16,128]{3,2,1,0:T(8,128)S(1)}, f32[1,4096,128]{2,1,0:T(8,128)S(1)}) custom-call(s32[1]{0:T(128)} %bitcast.side_ref, f32[2,64,8,128]{3,2,1,0:T(8,128)S(1)} %collective-permute-done.15.refs_0_, f32[3,8192,128]{2,1,0:T(8,128)} %refs_1_.1), custom_call_target="tpu_custom_call" | custom-call | flops 805306368 | bytes 26738688 | tf_op jit(solution)/shard_map/pallas_call | solution.py:138
  90.9 0.0 copy-start.13
  90.9 0.8 shard_map.41
  91.9 0.1 collective-permute-start.18
  92.0 1.6 %collective-permute-start.21 = (f32[2,3,8,128]{3,2,0,1:T(8,128)S(1)}, f32[2,3,8,128]{3,2,0,1:T(8,128)S(1)}, u32[]{:S(2)}, u32[]{:S(2)}) collective-permute-start(f32[2,3,8,128]{3,2,0,1:T(8,128)S(1)} %dynamic-slice_bitcast_fusion), channel_id=1, source_target_pairs={{0,8},{4,12},{8,0},{12,4},{16,24},{20,28},{24,16},{28,20},{1,9},{5... | collective-permute-start | bytes 73736 | tf_op jit(solution)/shard_map/ppermute | solution.py:165
  93.5 2.1 %collective-permute-start.20 = (f32[3,8,128]{2,1,0:T(8,128)S(1)}, f32[3,8,128]{2,1,0:T(8,128)S(1)}, u32[]{:S(2)}, u32[]{:S(2)}) collective-permute-start(f32[3,8,128]{2,1,0:T(8,128)S(1)} %get-tuple-element.86), channel_id=1, source_target_pairs={{0,24},{4,28},{8,16},{12,20},{16,8},{20,12},{24,0},{28,4},{1,25},{... | collective-permute-start | bytes 36872 | tf_op jit(solution)/shard_map/ppermute | solution.py:165
  95.7 0.5 collective-permute-start.19
  96.2 2.0 %collective-permute-done.20 = f32[3,8,128]{2,1,0:T(8,128)S(1)} collective-permute-done((f32[3,8,128]{2,1,0:T(8,128)S(1)}, f32[3,8,128]{2,1,0:T(8,128)S(1)}, u32[]{:S(2)}, u32[]{:S(2)}) %collective-permute-start.20) | collective-permute-done | bytes 12320 | tf_op jit(solution)/shard_map/ppermute | solution.py:165
  98.2 1.2 %collective-permute-done.19 = f32[3,8,128]{2,1,0:T(8,128)S(1)} collective-permute-done((f32[3,8,128]{2,1,0:T(8,128)S(1)}, f32[3,8,128]{2,1,0:T(8,128)S(1)}, u32[]{:S(2)}, u32[]{:S(2)}) %collective-permute-start.19) | collective-permute-done | bytes 12320 | tf_op jit(solution)/shard_map/ppermute | solution.py:165
  99.4 0.6 fusion.6
  (59 shorter events, 0.3 us)
Async XLA Ops:
  1.1 15.9 %collective-permute-start = (f32[2,64,8,128]{3,2,1,0:T(8,128)S(1)}, f32[2,64,8,128]{3,2,1,0:T(8,128)}, u32[]{:S(2)}, u32[]{:S(2)}) collective-permute-start(f32[2,64,8,128]{3,2,1,0:T(8,128)S(1)} %slice_bitcast_fusion.1.refs_0_), channel_id=1, source_target_pairs={{0,1},{1,0},{2,3},{3,2},{4,5},{5,4},{6,7},{7,6},{8,9},{9,8},{10,11... | collective-permute-start | bytes 1572872 | tf_op jit(solution)/shard_map/ppermute | solution.py:182
  4.2 12.9 %collective-permute-start.2 = (f32[2,64,8,128]{3,2,1,0:T(8,128)S(1)}, f32[2,64,8,128]{3,2,1,0:T(8,128)S(1)}, u32[]{:S(2)}, u32[]{:S(2)}) collective-permute-start(f32[2,64,8,128]{3,2,1,0:T(8,128)S(1)} %slice_bitcast_fusion.1.refs_0_), channel_id=1, source_target_pairs={{1,2},{2,1},{5,6},{6,5},{9,10},{10,9},{13,14},{14,13},{17,18},{18,... | collective-permute-start | bytes 1572872 | tf_op jit(solution)/shard_map/ppermute | solution.py:183
  5.9 8.0 %copy-start.6 = (f32[2,64,8,128]{3,2,1,0:T(8,128)}, f32[2,64,8,128]{3,2,1,0:T(8,128)S(1)}, u32[]{:S(2)}) copy-start(f32[2,64,8,128]{3,2,1,0:T(8,128)S(1)} %slice_bitcast_fusion.refs_2_) | copy-start | bytes 1572868
  6.0 22.2 %collective-permute-start.1 = (f32[2,64,8,128]{3,2,1,0:T(8,128)S(1)}, f32[2,64,8,128]{3,2,1,0:T(8,128)S(1)}, u32[]{:S(2)}, u32[]{:S(2)}) collective-permute-start(f32[2,64,8,128]{3,2,1,0:T(8,128)S(1)} %slice_bitcast_fusion.refs_2_), channel_id=1, source_target_pairs={{0,1},{1,0},{2,3},{3,2},{4,5},{5,4},{6,7},{7,6},{8,9},{9,8},{10,11... | collective-permute-start | bytes 1572872 | tf_op jit(solution)/shard_map/ppermute | solution.py:182
  10.4 18.6 %collective-permute-start.4 = (f32[2,64,8,128]{3,2,1,0:T(8,128)S(1)}, f32[2,64,8,128]{3,2,1,0:T(8,128)S(1)}, u32[]{:S(2)}, u32[]{:S(2)}) collective-permute-start(f32[2,64,8,128]{3,2,1,0:T(8,128)S(1)} %slice_bitcast_fusion.refs_2_), channel_id=1, source_target_pairs={{1,2},{2,1},{5,6},{6,5},{9,10},{10,9},{13,14},{14,13},{17,18},{18,... | collective-permute-start | bytes 1572872 | tf_op jit(solution)/shard_map/ppermute | solution.py:183
  14.0 19.9 %copy-start.12 = (f32[1,1024,128]{2,1,0:T(8,128)S(1)}, f32[1,1024,128]{2,1,0:T(8,128)}, u32[]{:S(2)}) copy-start(f32[1,1024,128]{2,1,0:T(8,128)} %get-tuple-element.75) | copy-start | bytes 1572868
  17.0 17.0 %collective-permute-start.3 = (f32[2,32,8,128]{3,2,1,0:T(8,128)S(1)}, f32[2,32,8,128]{3,2,1,0:T(8,128)}, u32[]{:S(2)}, u32[]{:S(2)}) collective-permute-start(f32[2,32,8,128]{3,2,1,0:T(8,128)S(1)} %get-tuple-element.58.refs_4_), channel_id=1, source_target_pairs={{0,1},{1,0},{2,3},{3,2},{4,5},{5,4},{6,7},{7,6},{8,9},{9,8},{10,11... | collective-permute-start | bytes 786440 | tf_op jit(solution)/shard_map/ppermute | solution.py:182
  22.0 15.5 %collective-permute-start.7 = (f32[2,32,8,128]{3,2,1,0:T(8,128)S(1)}, f32[2,32,8,128]{3,2,1,0:T(8,128)S(1)}, u32[]{:S(2)}, u32[]{:S(2)}) collective-permute-start(f32[2,32,8,128]{3,2,1,0:T(8,128)S(1)} %get-tuple-element.58.refs_4_), channel_id=1, source_target_pairs={{1,2},{2,1},{5,6},{6,5},{9,10},{10,9},{13,14},{14,13},{17,18},{18,... | collective-permute-start | bytes 786440 | tf_op jit(solution)/shard_map/ppermute | solution.py:183
  22.7 15.5 %copy-start.7 = (f32[2,64,8,128]{3,2,1,0:T(8,128)S(1)}, f32[2,64,8,128]{3,2,1,0:T(8,128)}, u32[]{:S(2)}) copy-start(f32[2,64,8,128]{3,2,1,0:T(8,128)} %copy-done.6) | copy-start | bytes 1572868
  28.2 0.8 copy-start.8
  28.9 5.0 %copy-start.2 = (f32[2,64,8,128]{3,2,1,0:T(8,128)}, f32[2,64,8,128]{3,2,1,0:T(8,128)S(1)}, u32[]{:S(2)}) copy-start(f32[2,64,8,128]{3,2,1,0:T(8,128)S(1)} %collective-permute-done.4.refs_2_) | copy-start | bytes 1572868
  28.9 9.3 %copy-start.9 = (f32[2,64,8,128]{3,2,1,0:T(8,128)S(1)}, f32[2,64,8,128]{3,2,1,0:T(8,128)}, u32[]{:S(2)}) copy-start(f32[2,64,8,128]{3,2,1,0:T(8,128)} %copy-done.8) | copy-start | bytes 1572868
  29.0 17.1 %collective-permute-start.5 = (f32[2,64,8,128]{3,2,1,0:T(8,128)S(1)}, f32[2,64,8,128]{3,2,1,0:T(8,128)S(1)}, u32[]{:S(2)}, u32[]{:S(2)}) collective-permute-start(f32[2,64,8,128]{3,2,1,0:T(8,128)S(1)} %broadcast_select_fusion.3), channel_id=1, source_target_pairs={{0,1},{1,0},{2,3},{3,2},{4,5},{5,4},{6,7},{7,6},{8,9},{9,8},{10,11... | collective-permute-start | bytes 1572872 | tf_op jit(solution)/shard_map/ppermute | solution.py:182
  33.2 11.4 %collective-permute-start.10 = (f32[2,32,8,128]{3,2,1,0:T(8,128)S(1)}, f32[2,32,8,128]{3,2,1,0:T(8,128)S(1)}, u32[]{:S(2)}, u32[]{:S(2)}) collective-permute-start(f32[2,32,8,128]{3,2,1,0:T(8,128)S(1)} %get-tuple-element.62.refs_5_.refs_0_), channel_id=1, source_target_pairs={{1,2},{2,1},{5,6},{6,5},{9,10},{10,9},{13,14},{14,13},{17,18},{18,... | collective-permute-start | bytes 786440 | tf_op jit(solution)/shard_map/ppermute | solution.py:183
  34.0 23.3 %collective-permute-start.6 = (f32[2,64,8,128]{3,2,1,0:T(8,128)S(1)}, f32[2,64,8,128]{3,2,1,0:T(8,128)S(1)}, u32[]{:S(2)}, u32[]{:S(2)}) collective-permute-start(f32[2,64,8,128]{3,2,1,0:T(8,128)S(1)} %broadcast_select_fusion.2), channel_id=1, source_target_pairs={{0,1},{1,0},{2,3},{3,2},{4,5},{5,4},{6,7},{7,6},{8,9},{9,8},{10,11... | collective-permute-start | bytes 1572872 | tf_op jit(solution)/shard_map/ppermute | solution.py:182
  37.5 9.3 %copy-start.4 = (f32[2,32,8,128]{3,2,1,0:T(8,128)}, f32[2,32,8,128]{3,2,1,0:T(8,128)S(1)}, u32[]{:S(2)}) copy-start(f32[2,32,8,128]{3,2,1,0:T(8,128)S(1)} %collective-permute-done.7.refs_5_) | copy-start | bytes 786436
  37.5 15.6 %collective-permute-start.8 = (f32[2,64,8,128]{3,2,1,0:T(8,128)}, f32[2,64,8,128]{3,2,1,0:T(8,128)S(1)}, u32[]{:S(2)}, u32[]{:S(2)}) collective-permute-start(f32[2,64,8,128]{3,2,1,0:T(8,128)} %collective-permute-done.refs_1_), channel_id=1, source_target_pairs={{1,2},{2,1},{5,6},{6,5},{9,10},{10,9},{13,14},{14,13},{17,18},{18,... | collective-permute-start | bytes 1572872 | tf_op jit(solution)/shard_map/ppermute | solution.py:183
  38.2 14.9 %copy-start.11 = (f32[1,1024,128]{2,1,0:T(8,128)S(1)}, f32[1,1024,128]{2,1,0:T(8,128)}, u32[]{:S(2)}) copy-start(f32[1,1024,128]{2,1,0:T(8,128)} %get-tuple-element.74) | copy-start | bytes 1572868
  44.7 14.0 %copy-start.3 = (f32[2,64,8,128]{3,2,1,0:T(8,128)S(1)}, f32[2,64,8,128]{3,2,1,0:T(8,128)}, u32[]{:S(2)}) copy-start(f32[2,64,8,128]{3,2,1,0:T(8,128)} %copy-done.2) | copy-start | bytes 1572868
  46.1 17.8 %collective-permute-start.11 = (f32[2,64,8,128]{3,2,1,0:T(8,128)S(1)}, f32[2,64,8,128]{3,2,1,0:T(8,128)S(1)}, u32[]{:S(2)}, u32[]{:S(2)}) collective-permute-start(f32[2,64,8,128]{3,2,1,0:T(8,128)S(1)} %copy-done.9), channel_id=1, source_target_pairs={{1,2},{2,1},{5,6},{6,5},{9,10},{10,9},{13,14},{14,13},{17,18},{18,... | collective-permute-start | bytes 1572872 | tf_op jit(solution)/shard_map/ppermute | solution.py:183
  47.8 16.1 %collective-permute-start.13 = (f32[2,32,8,128]{3,2,1,0:T(8,128)S(1)}, f32[2,32,8,128]{3,2,1,0:T(8,128)}, u32[]{:S(2)}, u32[]{:S(2)}) collective-permute-start(f32[2,32,8,128]{3,2,1,0:T(8,128)S(1)} %broadcast_select_fusion.4), channel_id=1, source_target_pairs={{0,1},{1,0},{2,3},{3,2},{4,5},{5,4},{6,7},{7,6},{8,9},{9,8},{10,11... | collective-permute-start | bytes 786440 | tf_op jit(solution)/shard_map/ppermute | solution.py:182
  54.0 10.6 %copy-start.10 = (f32[1,1024,128]{2,1,0:T(8,128)S(1)}, f32[1,1024,128]{2,1,0:T(8,128)}, u32[]{:S(2)}) copy-start(f32[1,1024,128]{2,1,0:T(8,128)} %get-tuple-element.73) | copy-start | bytes 1572868
  54.0 19.9 %collective-permute-start.9 = (f32[2,64,8,128]{3,2,1,0:T(8,128)}, f32[2,64,8,128]{3,2,1,0:T(8,128)S(1)}, u32[]{:S(2)}, u32[]{:S(2)}) collective-permute-start(f32[2,64,8,128]{3,2,1,0:T(8,128)} %broadcast_select_fusion.1), channel_id=1, source_target_pairs={{0,1},{1,0},{2,3},{3,2},{4,5},{5,4},{6,7},{7,6},{8,9},{9,8},{10,11... | collective-permute-start | bytes 1572872 | tf_op jit(solution)/shard_map/ppermute | solution.py:182
  57.3 15.4 %collective-permute-start.12 = (f32[2,32,8,128]{3,2,1,0:T(8,128)}, f32[2,32,8,128]{3,2,1,0:T(8,128)}, u32[]{:S(2)}, u32[]{:S(2)}) collective-permute-start(f32[2,32,8,128]{3,2,1,0:T(8,128)} %collective-permute-done.3.refs_6_), channel_id=1, source_target_pairs={{1,2},{2,1},{5,6},{6,5},{9,10},{10,9},{13,14},{14,13},{17,18},{18,... | collective-permute-start | bytes 786440 | tf_op jit(solution)/shard_map/ppermute | solution.py:183
  63.8 8.9 %collective-permute-start.14 = (f32[2,32,8,128]{3,2,1,0:T(8,128)}, f32[2,32,8,128]{3,2,1,0:T(8,128)S(1)}, u32[]{:S(2)}, u32[]{:S(2)}) collective-permute-start(f32[2,32,8,128]{3,2,1,0:T(8,128)} %collective-permute-done.13.refs_6_.refs_8_), channel_id=1, source_target_pairs={{1,2},{2,1},{5,6},{6,5},{9,10},{10,9},{13,14},{14,13},{17,18},{18,... | collective-permute-start | bytes 786440 | tf_op jit(solution)/shard_map/ppermute | solution.py:183
  65.4 0.8 copy-start
  66.2 19.5 %collective-permute-start.15 = (f32[2,64,8,128]{3,2,1,0:T(8,128)}, f32[2,64,8,128]{3,2,1,0:T(8,128)S(1)}, u32[]{:S(2)}, u32[]{:S(2)}) collective-permute-start(f32[2,64,8,128]{3,2,1,0:T(8,128)} %broadcast_select_fusion), channel_id=1, source_target_pairs={{0,1},{1,0},{2,3},{3,2},{4,5},{5,4},{6,7},{7,6},{8,9},{9,8},{10,11... | collective-permute-start | bytes 1572872 | tf_op jit(solution)/shard_map/ppermute | solution.py:182
  72.7 4.9 %copy-start.1 = (f32[2,64,8,128]{3,2,1,0:T(8,128)S(1)}, f32[2,64,8,128]{3,2,1,0:T(8,128)}, u32[]{:S(2)}) copy-start(f32[2,64,8,128]{3,2,1,0:T(8,128)} %copy-done) | copy-start | bytes 1572868
  72.7 4.9 %copy-start.5 = (f32[2,32,8,128]{3,2,1,0:T(8,128)S(1)}, f32[2,32,8,128]{3,2,1,0:T(8,128)}, u32[]{:S(2)}) copy-start(f32[2,32,8,128]{3,2,1,0:T(8,128)} %copy-done.4) | copy-start | bytes 786436
  73.9 17.0 %collective-permute-start.16 = (f32[2,32,8,128]{3,2,1,0:T(8,128)}, f32[2,32,8,128]{3,2,1,0:T(8,128)S(1)}, u32[]{:S(2)}, u32[]{:S(2)}) collective-permute-start(f32[2,32,8,128]{3,2,1,0:T(8,128)} %collective-permute-done.12.refs_3_), channel_id=1, source_target_pairs={{0,1},{1,0},{2,3},{3,2},{4,5},{5,4},{6,7},{7,6},{8,9},{9,8},{10,11... | collective-permute-start | bytes 786440 | tf_op jit(solution)/shard_map/ppermute | solution.py:182
  85.8 6.0 %collective-permute-start.17 = (f32[3,16,128]{2,1,0:T(8,128)S(1)}, f32[3,16,128]{2,1,0:T(8,128)S(1)}, u32[]{:S(2)}, u32[]{:S(2)}) collective-permute-start(f32[3,16,128]{2,1,0:T(8,128)S(1)} %fusion.1), channel_id=1, source_target_pairs={{1,0},{2,3},{5,4},{6,7},{9,8},{10,11},{13,12},{14,15},{17,16},{18,... | collective-permute-start | bytes 73736 | tf_op jit(solution)/shard_map/ppermute | solution.py:184
  90.9 8.5 %copy-start.13 = (f32[3,8,128]{2,1,0:T(8,128)S(1)}, f32[3,8,128]{2,1,0:T(8,128)}, u32[]{:S(2)}) copy-start(f32[3,8,128]{2,1,0:T(8,128)} %param.11) | copy-start | bytes 36868
  91.9 1.7 %collective-permute-start.18 = (f32[4,3,8,128]{3,2,1,0:T(8,128)S(1)}, f32[4,3,8,128]{3,2,1,0:T(8,128)S(1)}, u32[]{:S(2)}, u32[]{:S(2)}) collective-permute-start(f32[4,3,8,128]{3,2,1,0:T(8,128)S(1)} %bitcast.94), channel_id=1, source_target_pairs={{0,4},{4,0},{8,12},{12,8},{16,20},{20,16},{24,28},{28,24},{1,5},{5... | collective-permute-start | bytes 147464 | tf_op jit(solution)/shard_map/ppermute | solution.py:165
  92.0 4.2 %collective-permute-start.21 = (f32[2,3,8,128]{3,2,0,1:T(8,128)S(1)}, f32[2,3,8,128]{3,2,0,1:T(8,128)S(1)}, u32[]{:S(2)}, u32[]{:S(2)}) collective-permute-start(f32[2,3,8,128]{3,2,0,1:T(8,128)S(1)} %dynamic-slice_bitcast_fusion), channel_id=1, source_target_pairs={{0,8},{4,12},{8,0},{12,4},{16,24},{20,28},{24,16},{28,20},{1,9},{5... | collective-permute-start | bytes 73736 | tf_op jit(solution)/shard_map/ppermute | solution.py:165
  93.5 4.7 %collective-permute-start.20 = (f32[3,8,128]{2,1,0:T(8,128)S(1)}, f32[3,8,128]{2,1,0:T(8,128)S(1)}, u32[]{:S(2)}, u32[]{:S(2)}) collective-permute-start(f32[3,8,128]{2,1,0:T(8,128)S(1)} %get-tuple-element.86), channel_id=1, source_target_pairs={{0,24},{4,28},{8,16},{12,20},{16,8},{20,12},{24,0},{28,4},{1,25},{... | collective-permute-start | bytes 36872 | tf_op jit(solution)/shard_map/ppermute | solution.py:165
  95.7 3.7 %collective-permute-start.19 = (f32[3,8,128]{2,1,0:T(8,128)S(1)}, f32[3,8,128]{2,1,0:T(8,128)S(1)}, u32[]{:S(2)}, u32[]{:S(2)}) collective-permute-start(f32[3,8,128]{2,1,0:T(8,128)S(1)} %get-tuple-element.85), channel_id=1, source_target_pairs={{0,16},{4,20},{8,24},{12,28},{16,0},{20,4},{24,8},{28,12},{1,17},{... | collective-permute-start | bytes 36872 | tf_op jit(solution)/shard_map/ppermute | solution.py:165
  98.2 1.2 %collective-permute-start.22 = (f32[3,8,128]{2,1,0:T(8,128)S(1)}, f32[3,8,128]{2,1,0:T(8,128)S(1)}, u32[]{:S(2)}, u32[]{:S(2)}) collective-permute-start(f32[3,8,128]{2,1,0:T(8,128)S(1)} %dynamic-slice_bitcast_fusion.1), channel_id=1, source_target_pairs={{0,4},{4,0},{8,12},{12,8},{16,20},{20,16},{24,28},{28,24},{1,5},{5... | collective-permute-start | bytes 36872 | tf_op jit(solution)/shard_map/ppermute | solution.py:165

commit v6 on v5

--- a/solution.py
+++ b/solution.py
@@ -11,6 +11,7 @@
 LANES, SUBLANES = 128, 8
 TILE = 1024
 VMEM_LIMIT = 48 * 1024 * 1024
+COST_WEIGHT = 3
 
 
 def halves(values):
@@ -145,8 +146,8 @@
         scratch_shapes=[pltpu.VMEM((steps, rows, 2 * width), jnp.float32) for rows in rows_of] + held,
         compiler_params=pltpu.CompilerParams(vmem_limit_bytes=VMEM_LIMIT),
         cost_estimate=pl.CostEstimate(
-            flops=int(3 * 4 * sum(rows_of) * extent * width),
-            bytes_accessed=int(3 * 4 * (sum(term[1].size for term in flat) + orders * extent * width)),
+            flops=COST_WEIGHT * 4 * sum(rows_of) * extent * width,
+            bytes_accessed=COST_WEIGHT * 4 * (sum(term[1].size for term in flat) + orders * extent * width),
             transcendentals=0,
         ),
     )(side, *[term[1] for term in flat], right)
@@ -212,14 +213,38 @@
     far0 = middle(near0, near2, across2)
     out0 = pairs(jnp.where(at_end, chunk(0), across0), near1, across1)
     out1 = pairs(jnp.where(at_end, chunk(1), across1), near2)
-    first = products([[[full(own0)], [full(near0)]], [[full(own1)], [full(near1)]], [[full(own2), upper(own3, None)], [full(near2)]]], right, extent, side)
+    first = products(
+        [
+            [[full(own0)], [full(near0)]],
+            [[full(own1)], [full(near1)]],
+            [[full(own2), upper(own3, None)], [full(near2)]],
+        ],
+        right,
+        extent,
+        side,
+    )
     out2 = pairs(jnp.where(at_end, own3, across2), out0, across3, first)
     far2 = middle(near2, out1, far0)
     far1 = middle(near1, out0, across3, first)
     far_out0 = pairs(jnp.where(at_end, chunk(2), far0))
-    second = products([[[full(across0), at_ends(out0)]], [[full(across1), at_ends(out1)]], []], right, extent, side)
+    second = products(
+        [[[full(across0), at_ends(out0)]], [[full(across1), at_ends(out1)]], []], right, extent, side
+    )
     far3 = middle(out2, far1, second)
-    third = products([[[full(far0), at_ends(far_out0)]], [[full(far1)]], [[full(far2), upper(far3, None)], [full(across2), at_ends(out2), upper(across3, None)], [upper(out2, INNER)]]], right, extent, side)
+    third = products(
+        [
+            [[full(far0), at_ends(far_out0)]],
+            [[full(far1)]],
+            [
+                [full(far2), upper(far3, None)],
+                [full(across2), at_ends(out2), upper(across3, None)],
+                [upper(out2, INNER)],
+            ],
+        ],
+        right,
+        extent,
+        side,
+    )
     far_out1 = pairs(jnp.where(at_end, chunk(3), far1), out2, far1, second)
     end0 = for_end(out0, 0, side)
     end1 = for_end(out1, 1, side)

time: 101 us -> 101 us (level)
  no operation moved by 1% of the time
where the time goes in v6:
time: 101 us; the launch traced here: 100 us
  starting transfers between devices  50.2 us (50%)
  Pallas kernels  22.5 us (22%)
  waiting for transfers between devices  14.4 us (14%)
  local copies, waits for them, and re-layouts  7.88 us (8%)
  other arithmetic  4.61 us (5%)
    ppermute x9, starting transfers between devices, line_of_four(): lax.ppermute(after(array, *earlier), 'col', [(0, 1), (1, 0), (2, 3), (3,...  38.5 us
    pallas_call x9, Pallas kernels, products(): pl.pallas_call(functools.partial(products_kernel, layout, steps, orders,...  22.5 us
    ppermute x9, waiting for transfers between devices, line_of_four(): lax.ppermute(after(array, *earlier), 'col', [(0, 1), (1, 0), (2, 3), (3,...  11.2 us
    ppermute x8, starting transfers between devices, line_of_four(): lax.ppermute(after(array, *earlier), 'col', [(1, 2), (2, 1)])  6.1 us
    ppermute x5, starting transfers between devices, sum_over_row(): lax.ppermute(array, 'row', [(i, i ^ offset) for i in range(8)])  4.28 us
    transpose x3, local copies, waits for them, and re-layouts, blocked(): left.reshape(height // SUBLANES, SUBLANES, extent // LANES, LANES)  3.28 us
    ppermute x5, waiting for transfers between devices, sum_over_row(): lax.ppermute(array, 'row', [(i, i ^ offset) for i in range(8)])  3.19 us
    slice x1, local copies, waits for them, and re-layouts, line_of_four(): right[0, half + i * depth:half + (i + 1) * depth].reshape(own0.shape)  2.89 us
  transfers between devices with their start and end apart: 23, of which 8 were waited for; matrix products, arithmetic and copies ran while one was open for 9% of the time, Pallas kernels for 22%

profile of v6, /device:TPU:0, one launch (start us, length us, event | category | flops | bytes accessed | tf_op | source)
XLA Modules:
  0.0 100.0 jit_solution(2282370766539438525)
XLA Ops:
  0.0 1.1 %slice_bitcast_fusion.1.refs_0_ = f32[2,64,8,128]{3,2,1,0:T(8,128)S(1)} fusion(f32[3,16,8192]{2,1,0:T(8,128)} %param.9), kind=kLoop, calls=%fused_computation.1 | loop fusion | bytes 1048576 | tf_op jit(solution)/shard_map/transpose | solution.py:24
  1.1 3.1 %collective-permute-start = (f32[2,64,8,128]{3,2,1,0:T(8,128)S(1)}, f32[2,64,8,128]{3,2,1,0:T(8,128)}, u32[]{:S(2)}, u32[]{:S(2)}) collective-permute-start(f32[2,64,8,128]{3,2,1,0:T(8,128)S(1)} %slice_bitcast_fusion.1.refs_0_), channel_id=1, source_target_pairs={{0,1},{1,0},{2,3},{3,2},{4,5},{5,4},{6,7},{7,6},{8,9},{9,8},{10,11... | collective-permute-start | bytes 1572872 | tf_op jit(solution)/shard_map/ppermute | solution.py:183
  4.2 0.7 collective-permute-start.2
  4.9 1.1 %slice_bitcast_fusion.refs_2_ = f32[2,64,8,128]{3,2,1,0:T(8,128)S(1)} fusion(f32[3,16,8192]{2,1,0:T(8,128)} %param.9), kind=kLoop, calls=%fused_computation | loop fusion | bytes 1048576 | tf_op jit(solution)/shard_map/transpose | solution.py:24
  6.0 4.4 %collective-permute-start.1 = (f32[2,64,8,128]{3,2,1,0:T(8,128)S(1)}, f32[2,64,8,128]{3,2,1,0:T(8,128)S(1)}, u32[]{:S(2)}, u32[]{:S(2)}) collective-permute-start(f32[2,64,8,128]{3,2,1,0:T(8,128)S(1)} %slice_bitcast_fusion.refs_2_), channel_id=1, source_target_pairs={{0,1},{1,0},{2,3},{3,2},{4,5},{5,4},{6,7},{7,6},{8,9},{9,8},{10,11... | collective-permute-start | bytes 1572872 | tf_op jit(solution)/shard_map/ppermute | solution.py:183
  10.4 0.7 collective-permute-start.4
  11.1 2.9 %fusion.12 = (f32[1,1024,128]{2,1,0:T(8,128)}, f32[1,1024,128]{2,1,0:T(8,128)}, f32[1,1024,128]{2,1,0:T(8,128)}, f32[1,1024,128]{2,1,0:T(8,128)}) fusion(f32[3,8192,128]{2,1,0:T(8,128)} %refs_1_.1), kind=kLoop, calls=%fused_computation.44 | loop fusion | bytes 4194304 | tf_op jit(solution)/shard_map/slice | solution.py:193
  14.0 1.1 %slice_bitcast_fusion.2 = (f32[2,32,8,128]{3,2,1,0:T(8,128)S(1)}, f32[2,32,8,128]{3,2,1,0:T(8,128)S(1)}) fusion(f32[3,16,8192]{2,1,0:T(8,128)} %param.9), kind=kLoop, calls=%fused_computation.2 | loop fusion | bytes 1048576 | tf_op jit(solution)/shard_map/transpose | solution.py:24
  15.1 1.9 %collective-permute-done.refs_1_ = f32[2,64,8,128]{3,2,1,0:T(8,128)} collective-permute-done((f32[2,64,8,128]{3,2,1,0:T(8,128)S(1)}, f32[2,64,8,128]{3,2,1,0:T(8,128)}, u32[]{:S(2)}, u32[]{:S(2)}) %collective-permute-start) | collective-permute-done | bytes 524320 | tf_op jit(solution)/shard_map/ppermute | solution.py:183
  17.0 5.0 %collective-permute-start.3 = (f32[2,32,8,128]{3,2,1,0:T(8,128)S(1)}, f32[2,32,8,128]{3,2,1,0:T(8,128)}, u32[]{:S(2)}, u32[]{:S(2)}) collective-permute-start(f32[2,32,8,128]{3,2,1,0:T(8,128)S(1)} %get-tuple-element.58.refs_4_), channel_id=1, source_target_pairs={{0,1},{1,0},{2,3},{3,2},{4,5},{5,4},{6,7},{7,6},{8,9},{9,8},{10,11... | collective-permute-start | bytes 786440 | tf_op jit(solution)/shard_map/ppermute | solution.py:183
  22.0 0.7 collective-permute-start.7
  22.7 1.2 %broadcast_select_fusion.3 = f32[2,64,8,128]{3,2,1,0:T(8,128)S(1)} fusion(f32[2,64,8,128]{3,2,1,0:T(8,128)} %bitcast.93, f32[2,64,8,128]{3,2,1,0:T(8,128)S(1)} %collective-permute-done.2.refs_0_, pred[]{:T(512)S(6)} %or.3), kind=kLoop, calls=%fused_computation.7 | loop fusion | flops 131072 | bytes 1572865 | tf_op jit(solution)/shard_map/jit(_where)/select_n | solution.py:214
  23.9 4.3 %collective-permute-done.1.refs_3_ = f32[2,64,8,128]{3,2,1,0:T(8,128)S(1)} collective-permute-done((f32[2,64,8,128]{3,2,1,0:T(8,128)S(1)}, f32[2,64,8,128]{3,2,1,0:T(8,128)S(1)}, u32[]{:S(2)}, u32[]{:S(2)}) %collective-permute-start.1) | collective-permute-done | bytes 524320 | tf_op jit(solution)/shard_map/ppermute | solution.py:183
  28.2 0.8 copy-done.8
  29.0 4.3 %collective-permute-start.5 = (f32[2,64,8,128]{3,2,1,0:T(8,128)S(1)}, f32[2,64,8,128]{3,2,1,0:T(8,128)S(1)}, u32[]{:S(2)}, u32[]{:S(2)}) collective-permute-start(f32[2,64,8,128]{3,2,1,0:T(8,128)S(1)} %broadcast_select_fusion.3), channel_id=1, source_target_pairs={{0,1},{1,0},{2,3},{3,2},{4,5},{5,4},{6,7},{7,6},{8,9},{9,8},{10,11... | collective-permute-start | bytes 1572872 | tf_op jit(solution)/shard_map/ppermute | solution.py:183
  33.2 0.7 collective-permute-start.10
  33.9 0.1 broadcast_select_fusion.2
  34.0 3.5 %collective-permute-start.6 = (f32[2,64,8,128]{3,2,1,0:T(8,128)S(1)}, f32[2,64,8,128]{3,2,1,0:T(8,128)S(1)}, u32[]{:S(2)}, u32[]{:S(2)}) collective-permute-start(f32[2,64,8,128]{3,2,1,0:T(8,128)S(1)} %broadcast_select_fusion.2), channel_id=1, source_target_pairs={{0,1},{1,0},{2,3},{3,2},{4,5},{5,4},{6,7},{7,6},{8,9},{9,8},{10,11... | collective-permute-start | bytes 1572872 | tf_op jit(solution)/shard_map/ppermute | solution.py:183
  37.5 0.7 collective-permute-start.8
  38.2 6.4 %shard_map.37 = f32[2,3,16,128]{3,2,1,0:T(8,128)S(1)} custom-call(s32[1]{0:T(128)} %bitcast.side_ref, f32[2,64,8,128]{3,2,1,0:T(8,128)S(1)} %slice_bitcast_fusion.1.refs_0_, f32[2,64,8,128]{3,2,1,0:T(8,128)} %collective-permute-done.refs_1_, f32[2,64,8,128]{3,2,1,0:T(8,128)S(1)} %copy-done.7, f32[2,64,8,128]{3,2,1,0:T(8,128)S(1)} %copy-done.9, ...), custom_call_target="tpu_custom_call" | custom-call | flops 4831838208 | bytes 46399488 | tf_op jit(solution)/shard_map/pallas_call | solution.py:139
  44.7 1.4 %collective-permute-done.5.refs_1_ = f32[2,64,8,128]{3,2,1,0:T(8,128)S(1)} collective-permute-done((f32[2,64,8,128]{3,2,1,0:T(8,128)S(1)}, f32[2,64,8,128]{3,2,1,0:T(8,128)S(1)}, u32[]{:S(2)}, u32[]{:S(2)}) %collective-permute-start.5) | collective-permute-done | bytes 524320 | tf_op jit(solution)/shard_map/ppermute | solution.py:183
  46.1 0.7 collective-permute-start.11
  46.8 1.0 broadcast_select_fusion.4
  47.8 5.4 %collective-permute-start.13 = (f32[2,32,8,128]{3,2,1,0:T(8,128)S(1)}, f32[2,32,8,128]{3,2,1,0:T(8,128)}, u32[]{:S(2)}, u32[]{:S(2)}) collective-permute-start(f32[2,32,8,128]{3,2,1,0:T(8,128)S(1)} %broadcast_select_fusion.4), channel_id=1, source_target_pairs={{0,1},{1,0},{2,3},{3,2},{4,5},{5,4},{6,7},{7,6},{8,9},{9,8},{10,11... | collective-permute-start | bytes 786440 | tf_op jit(solution)/shard_map/ppermute | solution.py:183
  53.1 0.8 broadcast_select_fusion.1
  54.0 2.7 %collective-permute-start.9 = (f32[2,64,8,128]{3,2,1,0:T(8,128)}, f32[2,64,8,128]{3,2,1,0:T(8,128)S(1)}, u32[]{:S(2)}, u32[]{:S(2)}) collective-permute-start(f32[2,64,8,128]{3,2,1,0:T(8,128)} %broadcast_select_fusion.1), channel_id=1, source_target_pairs={{0,1},{1,0},{2,3},{3,2},{4,5},{5,4},{6,7},{7,6},{8,9},{9,8},{10,11... | collective-permute-start | bytes 1572872 | tf_op jit(solution)/shard_map/ppermute | solution.py:183
  56.7 0.6 collective-permute-done.6.refs_3_
  57.3 1.4 %collective-permute-start.12 = (f32[2,32,8,128]{3,2,1,0:T(8,128)}, f32[2,32,8,128]{3,2,1,0:T(8,128)}, u32[]{:S(2)}, u32[]{:S(2)}) collective-permute-start(f32[2,32,8,128]{3,2,1,0:T(8,128)} %collective-permute-done.3.refs_6_), channel_id=1, source_target_pairs={{1,2},{2,1},{5,6},{6,5},{9,10},{10,9},{13,14},{14,13},{17,18},{18,... | collective-permute-start | bytes 786440 | tf_op jit(solution)/shard_map/ppermute | solution.py:184
  58.7 5.1 %shard_map.38 = f32[1,3,16,128]{3,2,1,0:T(8,128)S(1)} custom-call(s32[1]{0:T(128)} %bitcast.side_ref, f32[2,64,8,128]{3,2,1,0:T(8,128)S(1)} %collective-permute-done.2.refs_0_, f32[2,64,8,128]{3,2,1,0:T(8,128)S(1)} %collective-permute-done.5.refs_1_, f32[2,64,8,128]{3,2,1,0:T(8,128)S(1)} %copy-done.3, f32[2,64,8,128]{3,2,1,0:T(8,128)S(1)} %collective-permute-done.6.refs_3_, ...), custom_call_target="tpu_custom_call" | custom-call | flops 2013265920 | bytes 44040192 | tf_op jit(solution)/shard_map/pallas_call | solution.py:139
  63.8 0.7 collective-permute-start.14
  64.5 0.9 broadcast_select_fusion
  65.4 0.8 copy-done
  66.2 6.5 %collective-permute-start.15 = (f32[2,64,8,128]{3,2,1,0:T(8,128)}, f32[2,64,8,128]{3,2,1,0:T(8,128)S(1)}, u32[]{:S(2)}, u32[]{:S(2)}) collective-permute-start(f32[2,64,8,128]{3,2,1,0:T(8,128)} %broadcast_select_fusion), channel_id=1, source_target_pairs={{0,1},{1,0},{2,3},{3,2},{4,5},{5,4},{6,7},{7,6},{8,9},{9,8},{10,11... | collective-permute-start | bytes 1572872 | tf_op jit(solution)/shard_map/ppermute | solution.py:183
  72.8 1.1 %collective-permute-done.9.refs_1_ = f32[2,64,8,128]{3,2,1,0:T(8,128)S(1)} collective-permute-done((f32[2,64,8,128]{3,2,1,0:T(8,128)}, f32[2,64,8,128]{3,2,1,0:T(8,128)S(1)}, u32[]{:S(2)}, u32[]{:S(2)}) %collective-permute-start.9) | collective-permute-done | bytes 524320 | tf_op jit(solution)/shard_map/ppermute | solution.py:183
  73.9 3.7 %collective-permute-start.16 = (f32[2,32,8,128]{3,2,1,0:T(8,128)}, f32[2,32,8,128]{3,2,1,0:T(8,128)S(1)}, u32[]{:S(2)}, u32[]{:S(2)}) collective-permute-start(f32[2,32,8,128]{3,2,1,0:T(8,128)} %collective-permute-done.12.refs_3_), channel_id=1, source_target_pairs={{0,1},{1,0},{2,3},{3,2},{4,5},{5,4},{6,7},{7,6},{8,9},{9,8},{10,11... | collective-permute-start | bytes 786440 | tf_op jit(solution)/shard_map/ppermute | solution.py:183
  77.6 6.3 %shard_map.39 = f32[3,3,16,128]{3,2,1,0:T(8,128)S(1)} custom-call(s32[1]{0:T(128)} %bitcast.side_ref, f32[2,64,8,128]{3,2,1,0:T(8,128)S(1)} %collective-permute-done.8.refs_0_, f32[2,64,8,128]{3,2,1,0:T(8,128)S(1)} %collective-permute-done.9.refs_1_, f32[2,64,8,128]{3,2,1,0:T(8,128)S(1)} %copy-done.1, f32[2,32,8,128]{3,2,1,0:T(8,128)} %collective-permute-done.12.refs_3_, ...), custom_call_target="tpu_custom_call" | custom-call | flops 3221225472 | bytes 47185920 | tf_op jit(solution)/shard_map/pallas_call | solution.py:139
  83.9 1.8 %collective-permute-done.15.refs_0_ = f32[2,64,8,128]{3,2,1,0:T(8,128)S(1)} collective-permute-done((f32[2,64,8,128]{3,2,1,0:T(8,128)}, f32[2,64,8,128]{3,2,1,0:T(8,128)S(1)}, u32[]{:S(2)}, u32[]{:S(2)}) %collective-permute-start.15) | collective-permute-done | bytes 524320 | tf_op jit(solution)/shard_map/ppermute | solution.py:183
  85.8 1.3 %collective-permute-start.17 = (f32[3,16,128]{2,1,0:T(8,128)S(1)}, f32[3,16,128]{2,1,0:T(8,128)S(1)}, u32[]{:S(2)}, u32[]{:S(2)}) collective-permute-start(f32[3,16,128]{2,1,0:T(8,128)S(1)} %fusion.1), channel_id=1, source_target_pairs={{1,0},{2,3},{5,4},{6,7},{9,8},{10,11},{13,12},{14,15},{17,16},{18,... | collective-permute-start | bytes 73736 | tf_op jit(solution)/shard_map/ppermute | solution.py:185
  87.1 3.8 %shard_map.40 = (f32[1,3,16,128]{3,2,1,0:T(8,128)S(1)}, f32[1,4096,128]{2,1,0:T(8,128)S(1)}) custom-call(s32[1]{0:T(128)} %bitcast.side_ref, f32[2,64,8,128]{3,2,1,0:T(8,128)S(1)} %collective-permute-done.15.refs_0_, f32[3,8192,128]{2,1,0:T(8,128)} %refs_1_.1), custom_call_target="tpu_custom_call" | custom-call | flops 805306368 | bytes 26738688 | tf_op jit(solution)/shard_map/pallas_call | solution.py:139
  90.9 0.0 copy-start.13
  90.9 0.8 shard_map.41
  91.9 0.1 collective-permute-start.18
  92.0 1.6 %collective-permute-start.21 = (f32[2,3,8,128]{3,2,0,1:T(8,128)S(1)}, f32[2,3,8,128]{3,2,0,1:T(8,128)S(1)}, u32[]{:S(2)}, u32[]{:S(2)}) collective-permute-start(f32[2,3,8,128]{3,2,0,1:T(8,128)S(1)} %dynamic-slice_bitcast_fusion), channel_id=1, source_target_pairs={{0,8},{4,12},{8,0},{12,4},{16,24},{20,28},{24,16},{28,20},{1,9},{5... | collective-permute-start | bytes 73736 | tf_op jit(solution)/shard_map/ppermute | solution.py:166
  93.5 2.1 %collective-permute-start.20 = (f32[3,8,128]{2,1,0:T(8,128)S(1)}, f32[3,8,128]{2,1,0:T(8,128)S(1)}, u32[]{:S(2)}, u32[]{:S(2)}) collective-permute-start(f32[3,8,128]{2,1,0:T(8,128)S(1)} %get-tuple-element.86), channel_id=1, source_target_pairs={{0,24},{4,28},{8,16},{12,20},{16,8},{20,12},{24,0},{28,4},{1,25},{... | collective-permute-start | bytes 36872 | tf_op jit(solution)/shard_map/ppermute | solution.py:166
  95.7 0.5 collective-permute-start.19
  96.2 2.0 %collective-permute-done.20 = f32[3,8,128]{2,1,0:T(8,128)S(1)} collective-permute-done((f32[3,8,128]{2,1,0:T(8,128)S(1)}, f32[3,8,128]{2,1,0:T(8,128)S(1)}, u32[]{:S(2)}, u32[]{:S(2)}) %collective-permute-start.20) | collective-permute-done | bytes 12320 | tf_op jit(solution)/shard_map/ppermute | solution.py:166
  98.2 1.2 %collective-permute-done.19 = f32[3,8,128]{2,1,0:T(8,128)S(1)} collective-permute-done((f32[3,8,128]{2,1,0:T(8,128)S(1)}, f32[3,8,128]{2,1,0:T(8,128)S(1)}, u32[]{:S(2)}, u32[]{:S(2)}) %collective-permute-start.19) | collective-permute-done | bytes 12320 | tf_op jit(solution)/shard_map/ppermute | solution.py:166
  99.4 0.6 fusion.6
  (59 shorter events, 0.3 us)
Async XLA Ops:
  1.1 15.9 %collective-permute-start = (f32[2,64,8,128]{3,2,1,0:T(8,128)S(1)}, f32[2,64,8,128]{3,2,1,0:T(8,128)}, u32[]{:S(2)}, u32[]{:S(2)}) collective-permute-start(f32[2,64,8,128]{3,2,1,0:T(8,128)S(1)} %slice_bitcast_fusion.1.refs_0_), channel_id=1, source_target_pairs={{0,1},{1,0},{2,3},{3,2},{4,5},{5,4},{6,7},{7,6},{8,9},{9,8},{10,11... | collective-permute-start | bytes 1572872 | tf_op jit(solution)/shard_map/ppermute | solution.py:183
  4.2 12.9 %collective-permute-start.2 = (f32[2,64,8,128]{3,2,1,0:T(8,128)S(1)}, f32[2,64,8,128]{3,2,1,0:T(8,128)S(1)}, u32[]{:S(2)}, u32[]{:S(2)}) collective-permute-start(f32[2,64,8,128]{3,2,1,0:T(8,128)S(1)} %slice_bitcast_fusion.1.refs_0_), channel_id=1, source_target_pairs={{1,2},{2,1},{5,6},{6,5},{9,10},{10,9},{13,14},{14,13},{17,18},{18,... | collective-permute-start | bytes 1572872 | tf_op jit(solution)/shard_map/ppermute | solution.py:184
  5.9 8.0 %copy-start.6 = (f32[2,64,8,128]{3,2,1,0:T(8,128)}, f32[2,64,8,128]{3,2,1,0:T(8,128)S(1)}, u32[]{:S(2)}) copy-start(f32[2,64,8,128]{3,2,1,0:T(8,128)S(1)} %slice_bitcast_fusion.refs_2_) | copy-start | bytes 1572868
  6.0 22.2 %collective-permute-start.1 = (f32[2,64,8,128]{3,2,1,0:T(8,128)S(1)}, f32[2,64,8,128]{3,2,1,0:T(8,128)S(1)}, u32[]{:S(2)}, u32[]{:S(2)}) collective-permute-start(f32[2,64,8,128]{3,2,1,0:T(8,128)S(1)} %slice_bitcast_fusion.refs_2_), channel_id=1, source_target_pairs={{0,1},{1,0},{2,3},{3,2},{4,5},{5,4},{6,7},{7,6},{8,9},{9,8},{10,11... | collective-permute-start | bytes 1572872 | tf_op jit(solution)/shard_map/ppermute | solution.py:183
  10.4 18.6 %collective-permute-start.4 = (f32[2,64,8,128]{3,2,1,0:T(8,128)S(1)}, f32[2,64,8,128]{3,2,1,0:T(8,128)S(1)}, u32[]{:S(2)}, u32[]{:S(2)}) collective-permute-start(f32[2,64,8,128]{3,2,1,0:T(8,128)S(1)} %slice_bitcast_fusion.refs_2_), channel_id=1, source_target_pairs={{1,2},{2,1},{5,6},{6,5},{9,10},{10,9},{13,14},{14,13},{17,18},{18,... | collective-permute-start | bytes 1572872 | tf_op jit(solution)/shard_map/ppermute | solution.py:184
  14.0 19.9 %copy-start.12 = (f32[1,1024,128]{2,1,0:T(8,128)S(1)}, f32[1,1024,128]{2,1,0:T(8,128)}, u32[]{:S(2)}) copy-start(f32[1,1024,128]{2,1,0:T(8,128)} %get-tuple-element.75) | copy-start | bytes 1572868
  17.0 17.0 %collective-permute-start.3 = (f32[2,32,8,128]{3,2,1,0:T(8,128)S(1)}, f32[2,32,8,128]{3,2,1,0:T(8,128)}, u32[]{:S(2)}, u32[]{:S(2)}) collective-permute-start(f32[2,32,8,128]{3,2,1,0:T(8,128)S(1)} %get-tuple-element.58.refs_4_), channel_id=1, source_target_pairs={{0,1},{1,0},{2,3},{3,2},{4,5},{5,4},{6,7},{7,6},{8,9},{9,8},{10,11... | collective-permute-start | bytes 786440 | tf_op jit(solution)/shard_map/ppermute | solution.py:183
  22.0 15.5 %collective-permute-start.7 = (f32[2,32,8,128]{3,2,1,0:T(8,128)S(1)}, f32[2,32,8,128]{3,2,1,0:T(8,128)S(1)}, u32[]{:S(2)}, u32[]{:S(2)}) collective-permute-start(f32[2,32,8,128]{3,2,1,0:T(8,128)S(1)} %get-tuple-element.58.refs_4_), channel_id=1, source_target_pairs={{1,2},{2,1},{5,6},{6,5},{9,10},{10,9},{13,14},{14,13},{17,18},{18,... | collective-permute-start | bytes 786440 | tf_op jit(solution)/shard_map/ppermute | solution.py:184
  22.7 15.5 %copy-start.7 = (f32[2,64,8,128]{3,2,1,0:T(8,128)S(1)}, f32[2,64,8,128]{3,2,1,0:T(8,128)}, u32[]{:S(2)}) copy-start(f32[2,64,8,128]{3,2,1,0:T(8,128)} %copy-done.6) | copy-start | bytes 1572868
  28.2 0.8 copy-start.8
  28.9 5.0 %copy-start.2 = (f32[2,64,8,128]{3,2,1,0:T(8,128)}, f32[2,64,8,128]{3,2,1,0:T(8,128)S(1)}, u32[]{:S(2)}) copy-start(f32[2,64,8,128]{3,2,1,0:T(8,128)S(1)} %collective-permute-done.4.refs_2_) | copy-start | bytes 1572868
  28.9 9.3 %copy-start.9 = (f32[2,64,8,128]{3,2,1,0:T(8,128)S(1)}, f32[2,64,8,128]{3,2,1,0:T(8,128)}, u32[]{:S(2)}) copy-start(f32[2,64,8,128]{3,2,1,0:T(8,128)} %copy-done.8) | copy-start | bytes 1572868
  29.0 17.1 %collective-permute-start.5 = (f32[2,64,8,128]{3,2,1,0:T(8,128)S(1)}, f32[2,64,8,128]{3,2,1,0:T(8,128)S(1)}, u32[]{:S(2)}, u32[]{:S(2)}) collective-permute-start(f32[2,64,8,128]{3,2,1,0:T(8,128)S(1)} %broadcast_select_fusion.3), channel_id=1, source_target_pairs={{0,1},{1,0},{2,3},{3,2},{4,5},{5,4},{6,7},{7,6},{8,9},{9,8},{10,11... | collective-permute-start | bytes 1572872 | tf_op jit(solution)/shard_map/ppermute | solution.py:183
  33.2 11.4 %collective-permute-start.10 = (f32[2,32,8,128]{3,2,1,0:T(8,128)S(1)}, f32[2,32,8,128]{3,2,1,0:T(8,128)S(1)}, u32[]{:S(2)}, u32[]{:S(2)}) collective-permute-start(f32[2,32,8,128]{3,2,1,0:T(8,128)S(1)} %get-tuple-element.62.refs_5_.refs_0_), channel_id=1, source_target_pairs={{1,2},{2,1},{5,6},{6,5},{9,10},{10,9},{13,14},{14,13},{17,18},{18,... | collective-permute-start | bytes 786440 | tf_op jit(solution)/shard_map/ppermute | solution.py:184
  34.0 23.3 %collective-permute-start.6 = (f32[2,64,8,128]{3,2,1,0:T(8,128)S(1)}, f32[2,64,8,128]{3,2,1,0:T(8,128)S(1)}, u32[]{:S(2)}, u32[]{:S(2)}) collective-permute-start(f32[2,64,8,128]{3,2,1,0:T(8,128)S(1)} %broadcast_select_fusion.2), channel_id=1, source_target_pairs={{0,1},{1,0},{2,3},{3,2},{4,5},{5,4},{6,7},{7,6},{8,9},{9,8},{10,11... | collective-permute-start | bytes 1572872 | tf_op jit(solution)/shard_map/ppermute | solution.py:183
  37.5 9.3 %copy-start.4 = (f32[2,32,8,128]{3,2,1,0:T(8,128)}, f32[2,32,8,128]{3,2,1,0:T(8,128)S(1)}, u32[]{:S(2)}) copy-start(f32[2,32,8,128]{3,2,1,0:T(8,128)S(1)} %collective-permute-done.7.refs_5_) | copy-start | bytes 786436
  37.5 15.6 %collective-permute-start.8 = (f32[2,64,8,128]{3,2,1,0:T(8,128)}, f32[2,64,8,128]{3,2,1,0:T(8,128)S(1)}, u32[]{:S(2)}, u32[]{:S(2)}) collective-permute-start(f32[2,64,8,128]{3,2,1,0:T(8,128)} %collective-permute-done.refs_1_), channel_id=1, source_target_pairs={{1,2},{2,1},{5,6},{6,5},{9,10},{10,9},{13,14},{14,13},{17,18},{18,... | collective-permute-start | bytes 1572872 | tf_op jit(solution)/shard_map/ppermute | solution.py:184
  38.2 14.9 %copy-start.11 = (f32[1,1024,128]{2,1,0:T(8,128)S(1)}, f32[1,1024,128]{2,1,0:T(8,128)}, u32[]{:S(2)}) copy-start(f32[1,1024,128]{2,1,0:T(8,128)} %get-tuple-element.74) | copy-start | bytes 1572868
  44.7 14.0 %copy-start.3 = (f32[2,64,8,128]{3,2,1,0:T(8,128)S(1)}, f32[2,64,8,128]{3,2,1,0:T(8,128)}, u32[]{:S(2)}) copy-start(f32[2,64,8,128]{3,2,1,0:T(8,128)} %copy-done.2) | copy-start | bytes 1572868
  46.1 17.8 %collective-permute-start.11 = (f32[2,64,8,128]{3,2,1,0:T(8,128)S(1)}, f32[2,64,8,128]{3,2,1,0:T(8,128)S(1)}, u32[]{:S(2)}, u32[]{:S(2)}) collective-permute-start(f32[2,64,8,128]{3,2,1,0:T(8,128)S(1)} %copy-done.9), channel_id=1, source_target_pairs={{1,2},{2,1},{5,6},{6,5},{9,10},{10,9},{13,14},{14,13},{17,18},{18,... | collective-permute-start | bytes 1572872 | tf_op jit(solution)/shard_map/ppermute | solution.py:184
  47.8 16.1 %collective-permute-start.13 = (f32[2,32,8,128]{3,2,1,0:T(8,128)S(1)}, f32[2,32,8,128]{3,2,1,0:T(8,128)}, u32[]{:S(2)}, u32[]{:S(2)}) collective-permute-start(f32[2,32,8,128]{3,2,1,0:T(8,128)S(1)} %broadcast_select_fusion.4), channel_id=1, source_target_pairs={{0,1},{1,0},{2,3},{3,2},{4,5},{5,4},{6,7},{7,6},{8,9},{9,8},{10,11... | collective-permute-start | bytes 786440 | tf_op jit(solution)/shard_map/ppermute | solution.py:183
  54.0 10.6 %copy-start.10 = (f32[1,1024,128]{2,1,0:T(8,128)S(1)}, f32[1,1024,128]{2,1,0:T(8,128)}, u32[]{:S(2)}) copy-start(f32[1,1024,128]{2,1,0:T(8,128)} %get-tuple-element.73) | copy-start | bytes 1572868
  54.0 19.9 %collective-permute-start.9 = (f32[2,64,8,128]{3,2,1,0:T(8,128)}, f32[2,64,8,128]{3,2,1,0:T(8,128)S(1)}, u32[]{:S(2)}, u32[]{:S(2)}) collective-permute-start(f32[2,64,8,128]{3,2,1,0:T(8,128)} %broadcast_select_fusion.1), channel_id=1, source_target_pairs={{0,1},{1,0},{2,3},{3,2},{4,5},{5,4},{6,7},{7,6},{8,9},{9,8},{10,11... | collective-permute-start | bytes 1572872 | tf_op jit(solution)/shard_map/ppermute | solution.py:183
  57.3 15.4 %collective-permute-start.12 = (f32[2,32,8,128]{3,2,1,0:T(8,128)}, f32[2,32,8,128]{3,2,1,0:T(8,128)}, u32[]{:S(2)}, u32[]{:S(2)}) collective-permute-start(f32[2,32,8,128]{3,2,1,0:T(8,128)} %collective-permute-done.3.refs_6_), channel_id=1, source_target_pairs={{1,2},{2,1},{5,6},{6,5},{9,10},{10,9},{13,14},{14,13},{17,18},{18,... | collective-permute-start | bytes 786440 | tf_op jit(solution)/shard_map/ppermute | solution.py:184
  63.8 8.9 %collective-permute-start.14 = (f32[2,32,8,128]{3,2,1,0:T(8,128)}, f32[2,32,8,128]{3,2,1,0:T(8,128)S(1)}, u32[]{:S(2)}, u32[]{:S(2)}) collective-permute-start(f32[2,32,8,128]{3,2,1,0:T(8,128)} %collective-permute-done.13.refs_6_.refs_8_), channel_id=1, source_target_pairs={{1,2},{2,1},{5,6},{6,5},{9,10},{10,9},{13,14},{14,13},{17,18},{18,... | collective-permute-start | bytes 786440 | tf_op jit(solution)/shard_map/ppermute | solution.py:184
  65.4 0.8 copy-start
  66.2 19.5 %collective-permute-start.15 = (f32[2,64,8,128]{3,2,1,0:T(8,128)}, f32[2,64,8,128]{3,2,1,0:T(8,128)S(1)}, u32[]{:S(2)}, u32[]{:S(2)}) collective-permute-start(f32[2,64,8,128]{3,2,1,0:T(8,128)} %broadcast_select_fusion), channel_id=1, source_target_pairs={{0,1},{1,0},{2,3},{3,2},{4,5},{5,4},{6,7},{7,6},{8,9},{9,8},{10,11... | collective-permute-start | bytes 1572872 | tf_op jit(solution)/shard_map/ppermute | solution.py:183
  72.7 4.9 %copy-start.1 = (f32[2,64,8,128]{3,2,1,0:T(8,128)S(1)}, f32[2,64,8,128]{3,2,1,0:T(8,128)}, u32[]{:S(2)}) copy-start(f32[2,64,8,128]{3,2,1,0:T(8,128)} %copy-done) | copy-start | bytes 1572868
  72.7 4.9 %copy-start.5 = (f32[2,32,8,128]{3,2,1,0:T(8,128)S(1)}, f32[2,32,8,128]{3,2,1,0:T(8,128)}, u32[]{:S(2)}) copy-start(f32[2,32,8,128]{3,2,1,0:T(8,128)} %copy-done.4) | copy-start | bytes 786436
  73.9 17.0 %collective-permute-start.16 = (f32[2,32,8,128]{3,2,1,0:T(8,128)}, f32[2,32,8,128]{3,2,1,0:T(8,128)S(1)}, u32[]{:S(2)}, u32[]{:S(2)}) collective-permute-start(f32[2,32,8,128]{3,2,1,0:T(8,128)} %collective-permute-done.12.refs_3_), channel_id=1, source_target_pairs={{0,1},{1,0},{2,3},{3,2},{4,5},{5,4},{6,7},{7,6},{8,9},{9,8},{10,11... | collective-permute-start | bytes 786440 | tf_op jit(solution)/shard_map/ppermute | solution.py:183
  85.8 6.0 %collective-permute-start.17 = (f32[3,16,128]{2,1,0:T(8,128)S(1)}, f32[3,16,128]{2,1,0:T(8,128)S(1)}, u32[]{:S(2)}, u32[]{:S(2)}) collective-permute-start(f32[3,16,128]{2,1,0:T(8,128)S(1)} %fusion.1), channel_id=1, source_target_pairs={{1,0},{2,3},{5,4},{6,7},{9,8},{10,11},{13,12},{14,15},{17,16},{18,... | collective-permute-start | bytes 73736 | tf_op jit(solution)/shard_map/ppermute | solution.py:185
  90.9 8.5 %copy-start.13 = (f32[3,8,128]{2,1,0:T(8,128)S(1)}, f32[3,8,128]{2,1,0:T(8,128)}, u32[]{:S(2)}) copy-start(f32[3,8,128]{2,1,0:T(8,128)} %param.11) | copy-start | bytes 36868
  91.9 1.7 %collective-permute-start.18 = (f32[4,3,8,128]{3,2,1,0:T(8,128)S(1)}, f32[4,3,8,128]{3,2,1,0:T(8,128)S(1)}, u32[]{:S(2)}, u32[]{:S(2)}) collective-permute-start(f32[4,3,8,128]{3,2,1,0:T(8,128)S(1)} %bitcast.94), channel_id=1, source_target_pairs={{0,4},{4,0},{8,12},{12,8},{16,20},{20,16},{24,28},{28,24},{1,5},{5... | collective-permute-start | bytes 147464 | tf_op jit(solution)/shard_map/ppermute | solution.py:166
  92.0 4.2 %collective-permute-start.21 = (f32[2,3,8,128]{3,2,0,1:T(8,128)S(1)}, f32[2,3,8,128]{3,2,0,1:T(8,128)S(1)}, u32[]{:S(2)}, u32[]{:S(2)}) collective-permute-start(f32[2,3,8,128]{3,2,0,1:T(8,128)S(1)} %dynamic-slice_bitcast_fusion), channel_id=1, source_target_pairs={{0,8},{4,12},{8,0},{12,4},{16,24},{20,28},{24,16},{28,20},{1,9},{5... | collective-permute-start | bytes 73736 | tf_op jit(solution)/shard_map/ppermute | solution.py:166
  93.5 4.7 %collective-permute-start.20 = (f32[3,8,128]{2,1,0:T(8,128)S(1)}, f32[3,8,128]{2,1,0:T(8,128)S(1)}, u32[]{:S(2)}, u32[]{:S(2)}) collective-permute-start(f32[3,8,128]{2,1,0:T(8,128)S(1)} %get-tuple-element.86), channel_id=1, source_target_pairs={{0,24},{4,28},{8,16},{12,20},{16,8},{20,12},{24,0},{28,4},{1,25},{... | collective-permute-start | bytes 36872 | tf_op jit(solution)/shard_map/ppermute | solution.py:166
  95.7 3.7 %collective-permute-start.19 = (f32[3,8,128]{2,1,0:T(8,128)S(1)}, f32[3,8,128]{2,1,0:T(8,128)S(1)}, u32[]{:S(2)}, u32[]{:S(2)}) collective-permute-start(f32[3,8,128]{2,1,0:T(8,128)S(1)} %get-tuple-element.85), channel_id=1, source_target_pairs={{0,16},{4,20},{8,24},{12,28},{16,0},{20,4},{24,8},{28,12},{1,17},{... | collective-permute-start | bytes 36872 | tf_op jit(solution)/shard_map/ppermute | solution.py:166
  98.2 1.2 %collective-permute-start.22 = (f32[3,8,128]{2,1,0:T(8,128)S(1)}, f32[3,8,128]{2,1,0:T(8,128)S(1)}, u32[]{:S(2)}, u32[]{:S(2)}) collective-permute-start(f32[3,8,128]{2,1,0:T(8,128)S(1)} %dynamic-slice_bitcast_fusion.1), channel_id=1, source_target_pairs={{0,4},{4,0},{8,12},{12,8},{16,20},{20,16},{24,28},{28,24},{1,5},{5... | collective-permute-start | bytes 36872 | tf_op jit(solution)/shard_map/ppermute | solution.py:166
